TPU v7x, 32 devices: a whole 2x2x4 slice. The times are simulated.
32 devices in a mesh: row: 16 (over z, x, core), col: 2 (over y).
Axes of the slice: x: 2, y: 2, z: 4, core: 2. Of those that a mesh axis runs over, the one named last changes fastest.
Arguments:
- x_tiles: bfloat16 [32, 16, 1, 128, 128], P('row', 'col'), may hold values from -0.5390625 to 0.5390625
- x_cols: int32 [32, 16, 1], P('row', 'col'), may hold values from 0 to 1, as said below
- keep_cols: int32 [32, 16, 2], P('row', 'col'), may hold values from 0 to 1, as said below
Outputs:
- square: bfloat16 [32, 16, 2, 128, 128], P('row', 'col')
- purified: bfloat16 [32, 16, 2, 128, 128], P('row', 'col')
Inputs may be any that keep to these rules, and one draw needn't show every extreme that they name: `x_cols`: within each block row and column panel the 1 entries are distinct. `keep_cols`: within each block row and column panel the 2 entries are distinct.
All inputs are finite; a program needn't handle non-finite values.
Results may differ from a plain program's by a relative error of at most 0.0049.
Values may be sent and summed in bfloat16 or wider, within the bound.
No kernel may reach another device: no remote copies, remote signals or barrier semaphores. Data moves between devices by JAX's collectives and lax.ppermute only.
A program may use at most 64 MiB of HBM per device.

v0:
```python
import jax
import jax.numpy as jnp
from jax import lax
from jax.sharding import PartitionSpec as P


def shifted(value, axis, steps):
    count = lax.axis_size(axis)
    pairs = [(source, (source + steps) % count) for source in range(count)]
    return lax.ppermute(value, axis, pairs)


def collect(local):
    groups = lax.axis_size("col")
    collected = [local] * groups
    current = local
    for step in range(1, groups):
        current = shifted((current[0], current[1]), "col", 1)
        collected[step] = current
    stack_tiles = jnp.stack([entry[0] for entry in collected], axis=0)
    stack_cols = jnp.stack([entry[1] for entry in collected], axis=0)
    return (stack_tiles, stack_cols)


def add_slabs(a_stack, kept_cols, carry, piece, start):
    stack_tiles, stack_cols = a_stack
    piece_tiles, piece_cols = piece
    groups = stack_tiles.shape[0]
    slab_rows = stack_tiles.shape[1]
    group_panels = stack_tiles.shape[2]
    my_group = lax.axis_index("col")
    count = piece_tiles.shape[0] // slab_rows

    def one_slab(step, total):
        slab_idx = start // slab_rows + step
        owner = slab_idx // group_panels
        panel_in = slab_idx % group_panels
        slot = (my_group - owner) % groups
        a_tiles = lax.dynamic_index_in_dim(
            lax.dynamic_index_in_dim(stack_tiles, slot, 0, False), panel_in, 1, False
        )
        a_cols = lax.dynamic_index_in_dim(
            lax.dynamic_index_in_dim(stack_cols, slot, 0, False), panel_in, 1, False
        )
        b_tiles = lax.dynamic_slice_in_dim(piece_tiles, step * slab_rows, slab_rows, 0)
        b_cols = lax.dynamic_slice_in_dim(piece_cols, step * slab_rows, slab_rows, 0)
        b_rows = jnp.take(b_tiles, a_cols, axis=0)
        b_ids = jnp.take(b_cols, a_cols, axis=0)
        matched = (b_ids[:, :, :, None, :] == kept_cols[:, None, :, :, None]).astype(jnp.bfloat16)
        selected = jnp.einsum(
            "iaqtb,iaqbnk->iaqtnk", matched, b_rows, preferred_element_type=jnp.float32
        ).astype(jnp.bfloat16)
        return total + jnp.einsum(
            "iamn,iaqtnk->iqtmk", a_tiles, selected, preferred_element_type=jnp.float32
        )

    return lax.fori_loop(0, count, one_slab, carry)


def shards(x_tiles, x_cols, keep_cols):
    tile_size = x_tiles.shape[-1]
    initial = jnp.zeros(
        (x_tiles.shape[0], x_tiles.shape[1], keep_cols.shape[2], tile_size, tile_size), jnp.float32
    )
    whole = (
        lax.all_gather(x_tiles, "row", axis=0, tiled=True),
        lax.all_gather(x_cols, "row", axis=0, tiled=True),
    )

    def through(a_stack):
        return add_slabs(a_stack, keep_cols, initial, whole, 0)

    square = through(collect((x_tiles, x_cols))).astype(jnp.bfloat16)
    cube = through(collect((square, keep_cols)))
    purified = (3.0 * square.astype(jnp.float32) - 2.0 * cube).astype(jnp.bfloat16)
    return (square, purified)


def solution(mesh):
    in_specs = (P("row", "col", None, None, None), P("row", "col", None), P("row", "col", None))
    out_specs = (P("row", "col", None, None, None), P("row", "col", None, None, None))
    return jax.shard_map(shards, mesh=mesh, in_specs=in_specs, out_specs=out_specs, check_vma=False)
```

profile of v0, /device:TPU:0, one launch (start us, length us, event | category | flops | bytes accessed | tf_op | source)
XLA Modules:
  0.0 388.6 jit_solution(9590911995290894155)
XLA Ops:
  9.0 3.0 collective-permute-start.1
  12.1 22.4 %all_gather.6 = s32[32,8,1]{1,2,0:T(1,128)S(1)} all-gather(s32[2,8,1]{1,2,0:T(1,128)} %param.8), channel_id=1, replica_groups=mesh['row'=16,'col'=2] {'row'}, dimensions={0}, use_global_device_ids=true | all-gather | bytes 1088 | tf_op jit(solution)/shard_map/all_gather | solution.py:67
  36.1 51.7 %all-gather.2.cloned.1.call-done = bf16[32,8,1,128,128]{4,3,2,1,0:T(8,128)(2,1)} async-done(((bf16[2,8,1,128,128]{4,3,2,1,0:T(8,128)(2,1)}), bf16[32,8,1,128,128]{4,3,2,1,0:T(8,128)(2,1)}) %all-gather.2.cloned.1.call-update) | async-done | bytes 8388624 | tf_op jit(solution)/shard_map/all_gather | solution.py:66
  87.8 101.2 %while.34 = (s32[]{:T(128)}, f32[2,8,2,128,128]{3,4,2,1,0:T(8,128)}, s32[]{:T(128)}, s32[2,2,8,1]{1,3,2,0:T(1,128)S(1)}, s32[32,8,1]{1,0,2:T(8,128)S(1)}, /*inde...) while((s32[]{:T(128)}, ...), condition=%wide.region_1.2_spmd.clone, body=%wide.region_0.1_spmd.clone.sunk | while | flops 136840320 | bytes 11089211 | solution.py:57
  90.8 1.9 bitcast_add_fusion.4
  95.6 3.4 bitcast_add_fusion.4
  102.1 3.4 bitcast_add_fusion.4
  108.5 3.4 bitcast_add_fusion.4
  114.9 3.4 bitcast_add_fusion.4
  121.3 3.4 bitcast_add_fusion.4
  127.7 3.4 bitcast_add_fusion.4
  134.2 3.4 bitcast_add_fusion.4
  140.6 3.4 bitcast_add_fusion.4
  147.0 3.4 bitcast_add_fusion.4
  153.4 3.4 bitcast_add_fusion.4
  159.9 3.4 bitcast_add_fusion.4
  166.3 3.4 bitcast_add_fusion.4
  172.7 3.4 bitcast_add_fusion.4
  179.1 3.4 bitcast_add_fusion.4
  185.6 3.4 bitcast_add_fusion.4
  189.0 1.8 copy.39
  190.9 1.5 collective-permute-start.3
  193.0 23.3 %collective-permute-done.2 = s32[2,8,2]{1,2,0:T(2,128)S(1)} collective-permute-done((s32[2,8,2]{1,2,0:T(2,128)S(1)}, s32[2,8,2]{1,2,0:T(2,128)S(1)}, u32[]{:S(2)}, u32[]{:S(2)}) %collective-permute-start.2) | collective-permute-done | bytes 160 | tf_op jit(solution)/shard_map/ppermute | solution.py:10
  216.4 1.5 pad_maximum_fusion
  218.0 160.6 %while.35 = (s32[]{:T(128)}, f32[2,8,2,128,128]{3,4,2,1,0:T(8,128)}, s32[]{:T(128)}, s32[2,2,8,2]{3,1,2,0:T(2,128)S(1)}, s32[32,8,1]{1,0,2:T(8,128)S(1)}, /*inde...) while((s32[]{:T(128)}, ...), condition=%wide.region_3.4_spmd.clone, body=%wide.region_2.3_spmd.clone.sunk | while | flops 272631008 | bytes 16914768 | solution.py:57
  222.3 1.9 copy.56
  224.2 3.1 bitcast_add_fusion.5
  230.1 1.5 select_convert_fusion.5
  231.6 1.9 copy.56
  233.5 3.8 bitcast_add_fusion.5
  241.7 1.9 copy.56
  243.6 3.8 bitcast_add_fusion.5
  251.8 1.9 copy.56
  253.7 3.8 bitcast_add_fusion.5
  260.3 1.5 select_convert_fusion.5
  261.9 1.9 copy.56
  263.8 3.8 bitcast_add_fusion.5
  271.9 1.9 copy.56
  273.9 3.8 bitcast_add_fusion.5
  282.0 1.9 copy.56
  283.9 3.8 bitcast_add_fusion.5
  290.6 1.5 select_convert_fusion.5
  292.1 1.9 copy.56
  294.0 3.8 bitcast_add_fusion.5
  302.2 1.9 copy.56
  304.1 3.8 bitcast_add_fusion.5
  312.3 1.9 copy.56
  314.2 3.8 bitcast_add_fusion.5
  320.8 1.5 select_convert_fusion.5
  322.3 1.9 copy.56
  324.3 3.8 bitcast_add_fusion.5
  330.9 1.5 select_convert_fusion.5
  332.4 1.9 copy.56
  334.4 3.8 bitcast_add_fusion.5
  342.5 1.9 copy.56
  344.4 3.8 bitcast_add_fusion.5
  351.1 1.5 select_convert_fusion.5
  352.6 1.9 copy.56
  354.5 3.8 bitcast_add_fusion.5
  362.7 1.9 copy.56
  364.6 3.8 bitcast_add_fusion.5
  372.8 1.9 copy.56
  374.7 3.8 bitcast_add_fusion.5
  378.5 1.9 copy.44
  (383 shorter events, 111.9 us)
Async XLA Ops:
  7.2 80.7 %all-gather.2.cloned.1.call-start = ((), (), s32[]{:S(2)}) async-start(), calls=%async_computation | async-start | bytes 8912896 | tf_op jit(solution)/shard_map/all_gather | solution.py:66
  9.0 27.1 %collective-permute-start.1 = (bf16[2,8,1,128,128]{4,3,0,1,2:T(8,128)(2,1)S(1)}, bf16[2,8,1,128,128]{4,3,0,1,2:T(8,128)(2,1)S(1)}, u32[]{:S(2)}, u32[]{:S(2)}) collective-permute-start(bf16[2,8,1,128,128]{4,3,0,1,2:T(8,128)(2,1)S(1)} %copy.51), channel_id=1, source_target_pairs={{0,1},{1,0},{2,3},{3,2},{4,5},{5,4},{6,7},{7,6},{8,9},{9,8},{10,11... | collective-permute-start | bytes 1572872 | tf_op jit(solution)/shard_map/ppermute | solution.py:10
  12.0 23.3 %collective-permute-start = (s32[2,8,1]{1,2,0:T(1,128)}, s32[2,8,1]{1,2,0:T(1,128)S(1)}, u32[]{:S(2)}, u32[]{:S(2)}) collective-permute-start(s32[2,8,1]{1,2,0:T(1,128)} %param.8), channel_id=1, source_target_pairs={{0,1},{1,0},{2,3},{3,2},{4,5},{5,4},{6,7},{7,6},{8,9},{9,8},{10,11... | collective-permute-start | bytes 200 | tf_op jit(solution)/shard_map/ppermute | solution.py:10
  189.0 3.4 copy-start.1
  190.9 189.6 %copy-start = (bf16[2,8,2,128,128]{4,3,2,1,0:T(8,128)(2,1)}, bf16[2,8,2,128,128]{4,3,2,1,0:T(8,128)(2,1)S(1)}, u32[]{:S(2)}) copy-start(bf16[2,8,2,128,128]{4,3,2,1,0:T(8,128)(2,1)S(1)} %copy.39) | copy-start | bytes 3145732
  190.9 25.5 %collective-permute-start.3 = (bf16[2,8,2,128,128]{4,3,2,1,0:T(8,128)(2,1)S(1)}, bf16[2,8,2,128,128]{4,3,2,1,0:T(8,128)(2,1)S(1)}, u32[]{:S(2)}, u32[]{:S(2)}) collective-permute-start(bf16[2,8,2,128,128]{4,3,2,1,0:T(8,128)(2,1)S(1)} %copy.39), channel_id=1, source_target_pairs={{0,1},{1,0},{2,3},{3,2},{4,5},{5,4},{6,7},{7,6},{8,9},{9,8},{10,11... | collective-permute-start | bytes 3145736 | tf_op jit(solution)/shard_map/ppermute | solution.py:10
  192.4 23.9 %collective-permute-start.2 = (s32[2,8,2]{1,2,0:T(2,128)S(1)}, s32[2,8,2]{1,2,0:T(2,128)S(1)}, u32[]{:S(2)}, u32[]{:S(2)}) collective-permute-start(s32[2,8,2]{1,2,0:T(2,128)S(1)} %copy-done.1), channel_id=1, source_target_pairs={{0,1},{1,0},{2,3},{3,2},{4,5},{5,4},{6,7},{7,6},{8,9},{9,8},{10,11... | collective-permute-start | bytes 392 | tf_op jit(solution)/shard_map/ppermute | solution.py:10
Sparse Core Ops, SparseCore 0:
  10.2 77.6 all-gather.1
where the time goes:
time: 392 us; the launch traced here: 389 us
  local copies, waits for them, and re-layouts  120 us (31%)
  matrix products  114 us (29%)
  waiting for transfers between devices  75.7 us (19%)
  other arithmetic  36.1 us (9%)
  blocking collectives  22.4 us (6%)
  between operations  14.1 us (4%)
  starting transfers between devices  5.24 us (1%)
    dot_general x32, matrix products, one_slab(): jnp.einsum('iamn,iaqtnk->iqtmk', a_tiles, selected, preferred_element_typ...  114 us
    all_gather x1, waiting for transfers between devices, shards(): lax.all_gather(x_tiles, 'row', axis=0, tiled=True)  51.7 us
    another operation x32, local copies, waits for them, and re-layouts  36 us
    dynamic_slice x32, local copies, waits for them, and re-layouts, one_slab(): lax.dynamic_slice_in_dim(piece_tiles, step * slab_rows, slab_rows, 0)  34.6 us
    another operation x64, other arithmetic  29.3 us
    ppermute x4, waiting for transfers between devices, shifted(): return lax.ppermute(value, axis, pairs)  23.3 us
    all_gather x1, blocking collectives, shards(): lax.all_gather(x_cols, 'row', axis=0, tiled=True)  22.4 us
    gather x32, local copies, waits for them, and re-layouts, one_slab(): b_rows = jnp.take(b_tiles, a_cols, axis=0)  22.3 us
  transfers between devices with their start and end apart: 5, of which 2 were waited for; matrix products, arithmetic and copies ran while one was open for 1% of the time, Pallas kernels for 0%

commit v1 on v0

v1 whole, which is shorter than its diff:
```python
import functools

import jax
import jax.numpy as jnp
from jax import lax
from jax.experimental import pallas as pl
from jax.experimental.pallas import tpu as pltpu
from jax.sharding import PartitionSpec as P

CORES = 2
FLAG_ROWS = 16


def chunk_sizes(panels):
    last = max(1, (panels * 3) // 8)
    return (panels - last, last)


def ring_chip(position, chips):
    up = 2 * position
    down = 2 * (chips - 1 - position) + 1
    if isinstance(position, int):
        return up if position < chips // 2 else down
    return jnp.where(position < chips // 2, up, down)


def ring_pairs(rows):
    chips = rows // CORES
    pairs = []
    for position in range(chips):
        for core in range(CORES):
            step = 1 if core == 0 else -1
            source = ring_chip(position, chips) * CORES + core
            target = ring_chip((position + step) % chips, chips) * CORES + core
            pairs.append((source, target))
    return pairs


def slot_of(slab, row, rows):
    chips = rows // CORES

    def place(chip):
        return jnp.where(chip % 2 == 0, chip // 2, chips - 1 - chip // 2)

    core = row % CORES
    step = 1 - 2 * core
    distance = (place(slab // CORES) - place(row // CORES)) * step
    distance = lax.rem(distance + chips, chips)
    return jnp.where(slab % CORES == core, distance, chips + distance)


def slab_of(slot, row, rows):
    chips = rows // CORES
    core = row % CORES
    chip = row // CORES
    place = jnp.where(chip % 2 == 0, chip // 2, chips - 1 - chip // 2)
    step = 1 - 2 * core
    position = lax.rem(place + step * (slot % chips) + chips, chips)
    other = core if slot < chips else 1 - core
    return ring_chip(position, chips) * CORES + other


def expand(payload, count, width, tile, out, row0, col0):
    base = count * tile
    flags = payload[base : base + FLAG_ROWS, :]
    per_row = count // width
    for local in range(width):
        for panel in range(per_row):
            index = local * per_row + panel
            block = payload[index * tile : (index + 1) * tile, :]
            right = block * flags[index : index + 1, :]
            left = block - right
            rows = slice(row0 + local * tile, row0 + (local + 1) * tile)
            column = col0 + panel * 2 * tile
            out[rows, column : column + tile] = left
            out[rows, column + tile : column + 2 * tile] = right


def pack_kernel(sizes, cols_ref, x_ref, *outs):
    width, panels, tile = x_ref.shape[0], x_ref.shape[1], x_ref.shape[-1]
    first = 0
    for size, out in zip(sizes, outs):
        row_ids = lax.broadcasted_iota(jnp.int32, (FLAG_ROWS, tile), 0)
        flags = jnp.zeros((FLAG_ROWS, tile), jnp.float32)
        for local in range(width):
            for panel in range(size):
                index = local * size + panel
                out[index * tile : (index + 1) * tile, :] = x_ref[local, first + panel, 0]
                flag = cols_ref[local, first + panel].astype(jnp.float32)
                flags = jnp.where(row_ids == index, flag, flags)
        base = width * size * tile
        out[base : base + FLAG_ROWS, :] = flags.astype(jnp.bfloat16)
        first += size


def left_kernel(sizes, rows, groups, width, tile, *refs):
    out = refs[-1]
    dense = width * tile
    row, mine = lax.axis_index("row"), lax.axis_index("col")
    panels = sum(sizes)
    index = 0
    for shift in range(groups):
        group = lax.rem(mine - shift + groups, groups)
        first = 0
        for size in sizes:
            payload = refs[index]
            index += 1
            base = width * size * tile
            flags = payload[base : base + FLAG_ROWS, :]
            for panel in range(size):
                slot = slot_of(group * panels + first + panel, row, rows)
                for local in range(width):
                    where = local * size + panel
                    block = payload[where * tile : (where + 1) * tile, :]
                    right = block * flags[where : where + 1, :]
                    part = slice(local * tile, (local + 1) * tile)
                    start = pl.multiple_of(slot * dense, dense)
                    out[part, pl.ds(start, tile)] = block - right
                    out[part, pl.ds(start + tile, tile)] = right
            first += size


def square_kernel(size, width, tile, left_ref, *refs):
    pieces, out, right = refs[:-2], refs[-2], refs[-1]
    dense = width * tile
    for slot, piece in enumerate(pieces):
        expand(piece, width * size, width, tile, right, slot * dense, 0)
    out[...] = jnp.dot(
        left_ref[...], right[...], preferred_element_type=jnp.float32
    ).astype(out.dtype)


def place_panels(source, size, first, group, panels, row, rows, dense, out):
    for panel in range(size):
        slot = slot_of(group * panels + first + panel, row, rows)
        out[:, pl.ds(pl.multiple_of(slot * dense, dense), dense)] = source[
            :, panel * dense : (panel + 1) * dense
        ]


def add_slots(pieces, sizes, width, tile, wanted, squares, right, acc):
    dense = width * tile
    for slot, parts in enumerate(pieces):

        @pl.when(wanted(slot))
        def _(slot=slot, parts=parts):
            column = 0
            for size, part in zip(sizes, parts):
                expand(part, width * size, width, tile, right, 0, column)
                column += size * dense
            acc[...] += jnp.dot(
                squares[:, slot * dense : (slot + 1) * dense],
                right[...],
                preferred_element_type=jnp.float32,
            )


def early(slot, sizes, groups, row, rows, mine):
    panels = sum(sizes)
    slab = slab_of(slot, row, rows)
    return (slab // panels == mine) | (lax.rem(slab, panels) < panels - sizes[-1])


def order(keep, left, right):
    first = keep == 0
    return jnp.where(first, left, right), jnp.where(first, right, left)


def cube_kernel(sizes, rows, groups, width, tile, keep_ref, *refs):
    chunks = len(sizes)
    own = refs[:chunks]
    received = refs[chunks : chunks + (groups - 1) * (chunks - 1)]
    flat = refs[chunks + (groups - 1) * (chunks - 1) : -4]
    acc, square, squares, right = refs[-4:]
    pieces = [flat[i * chunks : (i + 1) * chunks] for i in range(rows)]
    dense = width * tile
    row, mine = lax.axis_index("row"), lax.axis_index("col")
    panels = sum(sizes)
    first = 0
    for size, source in zip(sizes, own):
        place_panels(source, size, first, mine, panels, row, rows, dense, squares)
        for panel in range(size):
            for local in range(width):
                part = slice(local * tile, (local + 1) * tile)
                column = panel * dense
                a, b = order(
                    keep_ref[local, first + panel, 0],
                    source[part, column : column + tile],
                    source[part, column + tile : column + 2 * tile],
                )
                square[local, first + panel, 0] = a
                square[local, first + panel, 1] = b
        first += size
    index = 0
    for shift in range(1, groups):
        group = lax.rem(mine - shift + groups, groups)
        first = 0
        for size in sizes[:-1]:
            place_panels(received[index], size, first, group, panels, row, rows, dense, squares)
            first += size
            index += 1
    acc[...] = jnp.zeros_like(acc)
    wanted = functools.partial(
        early, sizes=sizes, groups=groups, row=row, rows=rows, mine=mine
    )
    add_slots(pieces, sizes, width, tile, wanted, squares, right, acc)


def final_kernel(sizes, rows, groups, width, tile, keep_ref, acc_in, *refs):
    chunks = len(sizes)
    own = refs[:chunks]
    received = refs[chunks : chunks + groups - 1]
    flat = refs[chunks + groups - 1 : -4]
    purified, squares, right, acc = refs[-4:]
    pieces = [flat[i * chunks : (i + 1) * chunks] for i in range(rows)]
    dense = width * tile
    row, mine = lax.axis_index("row"), lax.axis_index("col")
    panels = sum(sizes)
    for shift in range(1, groups):
        group = lax.rem(mine - shift + groups, groups)
        place_panels(
            received[shift - 1],
            sizes[-1],
            panels - sizes[-1],
            group,
            panels,
            row,
            rows,
            dense,
            squares,
        )
    acc[...] = acc_in[...]

    def wanted(slot):
        return jnp.logical_not(early(slot, sizes, groups, row, rows, mine))

    add_slots(pieces, sizes, width, tile, wanted, squares, right, acc)
    first = 0
    for size, source in zip(sizes, own):
        for panel in range(size):
            for local in range(width):
                part = slice(local * tile, (local + 1) * tile)
                column = panel * dense
                target = (first + panel) * dense
                value = 3.0 * source[part, column : column + dense].astype(
                    jnp.float32
                ) - 2.0 * acc[part, target : target + dense]
                value = value.astype(purified.dtype)
                a, b = order(
                    keep_ref[local, first + panel, 0], value[:, :tile], value[:, tile:]
                )
                purified[local, first + panel, 0] = a
                purified[local, first + panel, 1] = b
        first += size


def vmem(count):
    return [pl.BlockSpec(memory_space=pltpu.VMEM)] * count


def smem():
    return pl.BlockSpec(memory_space=pltpu.SMEM)


def params(mib):
    return pltpu.CompilerParams(vmem_limit_bytes=mib * 1024 * 1024)


def shards(rows, groups, x_tiles, x_cols, keep_cols):
    width, panels, tile = x_tiles.shape[0], x_tiles.shape[1], x_tiles.shape[-1]
    dense = width * tile
    sizes = chunk_sizes(panels)
    chips = rows // CORES
    forward = ring_pairs(rows)
    backward = [(target, source) for source, target in forward]
    sibling = [(device, device ^ 1) for device in range(rows)]
    bf16, f32 = jnp.bfloat16, jnp.float32

    def across(value, shift):
        pairs = [(group, (group + shift) % groups) for group in range(groups)]
        return lax.ppermute(value, "col", pairs)

    payloads = pl.pallas_call(
        functools.partial(pack_kernel, sizes),
        out_shape=[
            jax.ShapeDtypeStruct((width * size * tile + FLAG_ROWS, tile), bf16) for size in sizes
        ],
        in_specs=[smem()] + vmem(1),
        out_specs=vmem(len(sizes)),
        name="pack",
    )(x_cols.reshape(width, panels), x_tiles)

    lefts = list(payloads)
    for shift in range(1, groups):
        lefts += [across(payload, shift) for payload in payloads]
    left = pl.pallas_call(
        functools.partial(left_kernel, sizes, rows, groups, width, tile),
        out_shape=jax.ShapeDtypeStruct((dense, rows * dense), bf16),
        in_specs=vmem(len(lefts)),
        out_specs=vmem(1)[0],
        compiler_params=params(16),
        name="left",
    )(*lefts)

    pieces = [[None] * len(sizes) for _ in range(rows)]
    squares, received = [], []
    for chunk, payload in enumerate(payloads):
        size = sizes[chunk]
        mine = [None] * chips
        mine[0] = payload
        ahead = behind = payload
        for hop in range(1, chips // 2 + 1):
            ahead = lax.ppermute(ahead, "row", forward)
            mine[chips - hop] = ahead
            if hop < chips - chips // 2:
                behind = lax.ppermute(behind, "row", backward)
                mine[hop] = behind
        for slot in range(chips):
            pieces[slot][chunk] = mine[slot]
            mirrored = (chips - slot) % chips
            pieces[chips + mirrored][chunk] = lax.ppermute(mine[slot], "row", sibling)
        square = pl.pallas_call(
            functools.partial(square_kernel, size, width, tile),
            out_shape=jax.ShapeDtypeStruct((dense, size * dense), bf16),
            in_specs=vmem(1 + rows),
            out_specs=vmem(1)[0],
            scratch_shapes=[pltpu.VMEM((rows * dense, size * dense), bf16)],
            compiler_params=params(40),
            name="square",
        )(left, *[piece[chunk] for piece in pieces])
        squares.append(square)
        received.append([across(square, shift) for shift in range(1, groups)])

    flat = [part for piece in pieces for part in piece]
    already = [part[shift] for shift in range(groups - 1) for part in received[:-1]]
    acc, square_out = pl.pallas_call(
        functools.partial(cube_kernel, sizes, rows, groups, width, tile),
        out_shape=[
            jax.ShapeDtypeStruct((dense, panels * dense), f32),
            jax.ShapeDtypeStruct((width, panels, 2, tile, tile), bf16),
        ],
        in_specs=[smem()] + vmem(len(squares) + len(already) + len(flat)),
        out_specs=vmem(2),
        scratch_shapes=[
            pltpu.VMEM((dense, rows * dense), bf16),
            pltpu.VMEM((dense, panels * dense), bf16),
        ],
        compiler_params=params(40),
        name="cube",
    )(keep_cols, *squares, *already, *flat)

    purified = pl.pallas_call(
        functools.partial(final_kernel, sizes, rows, groups, width, tile),
        out_shape=jax.ShapeDtypeStruct((width, panels, 2, tile, tile), bf16),
        in_specs=[smem()] + vmem(1 + len(squares) + groups - 1 + len(flat)),
        out_specs=vmem(1)[0],
        scratch_shapes=[
            pltpu.VMEM((dense, rows * dense), bf16),
            pltpu.VMEM((dense, panels * dense), bf16),
            pltpu.VMEM((dense, panels * dense), f32),
        ],
        compiler_params=params(40),
        name="final",
    )(keep_cols, acc, *squares, *received[-1], *flat)
    return (square_out, purified)


def solution(mesh):
    in_specs = (P("row", "col", None, None, None), P("row", "col", None), P("row", "col", None))
    out_specs = (P("row", "col", None, None, None), P("row", "col", None, None, None))
    body = functools.partial(shards, mesh.shape["row"], mesh.shape["col"])
    return jax.shard_map(body, mesh=mesh, in_specs=in_specs, out_specs=out_specs, check_vma=False)
```

time: 392 us -> 117 us (0.30)
  matrix products: 114 us -> 0 us
  local copies, waits for them, and re-layouts: 120 us -> 25 us
  other arithmetic: 36.1 us -> 0 us
  waiting for transfers between devices: 75.7 us -> 45.5 us
  blocking collectives: 22.4 us -> 0 us
  Pallas kernels: 0 us -> 21.5 us
  starting transfers between devices: 5.24 us -> 23.5 us
  between operations: 14.1 us -> 0.96 us
    dot_general x32 -> x0, matrix products: 114 us -> none  [one_slab(): jnp.einsum('iamn,iaqtnk->iqtmk', a_tiles, selected, preferred_element_typ...]
    all_gather x1 -> x0, waiting for transfers between devices: 51.7 us -> none  [shards(): lax.all_gather(x_tiles, 'row', axis=0, tiled=True)]
    gather x64 -> x0, local copies, waits for them, and re-layouts: 40.2 us -> none  [the longest x32 22.3 us: one_slab(): b_rows = jnp.take(b_tiles, a_cols, axis=0)]
    another operation x32 -> x0, local copies, waits for them, and re-layouts: 36 us -> none
    dynamic_slice x64 -> x0, local copies, waits for them, and re-layouts: 34.9 us -> none  [the longest x32 34.6 us: one_slab(): lax.dynamic_slice_in_dim(piece_tiles, step * slab_rows, slab_rows, 0)]
    another operation x68 -> x0, other arithmetic: 31.7 us -> none
    unnamed x8 -> x107, local copies, waits for them, and re-layouts: 2.05 us -> 25 us
    all_gather x1 -> x0, blocking collectives: 22.4 us -> none  [shards(): lax.all_gather(x_cols, 'row', axis=0, tiled=True)]
  transfers between devices with their start and end apart: 5 -> 34, of which waited for: 2 -> 13; matrix products, arithmetic and copies ran while one was open for 1% -> 0% of each run, Pallas kernels for 0% -> 13%
where the time goes in v1:
time: 117 us; the launch traced here: 116 us
  waiting for transfers between devices  45.5 us (39%)
  local copies, waits for them, and re-layouts  25 us (21%)
  starting transfers between devices  23.5 us (20%)
  Pallas kernels  21.5 us (18%)
    unnamed x107, local copies, waits for them, and re-layouts  25 us
    ppermute x8, waiting for transfers between devices, shards(): ahead = lax.ppermute(ahead, 'row', forward)  18.8 us
    ppermute x6, waiting for transfers between devices, shards(): behind = lax.ppermute(behind, 'row', backward)  13.5 us
    ppermute x4, waiting for transfers between devices, across(): return lax.ppermute(value, 'col', pairs)  10.6 us
    pallas_call x1, Pallas kernels, shards(): pl.pallas_call(functools.partial(cube_kernel, sizes, rows, groups, width,...  9.62 us
    ppermute x8, starting transfers between devices, shards(): ahead = lax.ppermute(ahead, 'row', forward)  8.16 us
    ppermute x6, starting transfers between devices, shards(): behind = lax.ppermute(behind, 'row', backward)  6.75 us
    ppermute x4, starting transfers between devices, across(): return lax.ppermute(value, 'col', pairs)  5.79 us
  transfers between devices with their start and end apart: 34, of which 13 were waited for; matrix products, arithmetic and copies ran while one was open for 0% of the time, Pallas kernels for 13%

profile of v1, /device:TPU:0, one launch (start us, length us, event | category | flops | bytes accessed | tf_op | source)
XLA Modules:
  0.0 116.5 jit_solution(9324903426562307452)
XLA Ops:
  0.6 1.9 %pack.1 = (bf16[1296,128]{1,0:T(8,128)(2,1)}, bf16[784,128]{1,0:T(8,128)(2,1)}) custom-call(s32[2,8]{1,0:T(2,128)} %bitcast.1, bf16[2,8,1,128,128]{4,3,2,1,0:T(8,128)(2,1)} %x_ref.1), custom_call_target="tpu_custom_call" | custom-call | tf_op jit(solution)/shard_map/pack/pallas_call | solution.py:283
  2.5 3.0 %collective-permute-start.5 = (bf16[1296,128]{1,0:T(8,128)(2,1)}, bf16[1296,128]{1,0:T(8,128)(2,1)S(1)}, u32[]{:S(2)}, u32[]{:S(2)}) collective-permute-start(bf16[1296,128]{1,0:T(8,128)(2,1)} %get-tuple-element.6.refs_0_.refs_3_), channel_id=1, source_target_pairs={{0,8},{2,6},{8,16},{10,2},{16,24},{18,10},{24,28},{26,18},{28,20},... | collective-permute-start | bytes 995336 | tf_op jit(solution)/shard_map/ppermute | solution.py:313
  5.5 2.0 %collective-permute-start.1 = (bf16[784,128]{1,0:T(8,128)(2,1)}, bf16[784,128]{1,0:T(8,128)(2,1)S(1)}, u32[]{:S(2)}, u32[]{:S(2)}) collective-permute-start(bf16[784,128]{1,0:T(8,128)(2,1)} %get-tuple-element.7.refs_1_.refs_0_.refs_4_), channel_id=1, source_target_pairs={{0,1},{1,0},{2,3},{3,2},{4,5},{5,4},{6,7},{7,6},{8,9},{9,8},{10,11... | collective-permute-start | bytes 602120 | tf_op jit(solution)/shard_map/ppermute | solution.py:281
  7.5 6.3 %collective-permute-done.5.refs_7_.refs_17_ = bf16[1296,128]{1,0:T(8,128)(2,1)S(1)} collective-permute-done((bf16[1296,128]{1,0:T(8,128)(2,1)}, bf16[1296,128]{1,0:T(8,128)(2,1)S(1)}, u32[]{:S(2)}, u32[]{:S(2)}) %collective-permute-start.5) | collective-permute-done | bytes 331808 | tf_op jit(solution)/shard_map/ppermute | solution.py:313
  13.8 1.5 %collective-permute-start.6 = (bf16[1296,128]{1,0:T(8,128)(2,1)S(1)}, bf16[1296,128]{1,0:T(8,128)(2,1)S(1)}, u32[]{:S(2)}, u32[]{:S(2)}) collective-permute-start(bf16[1296,128]{1,0:T(8,128)(2,1)S(1)} %collective-permute-done.5.refs_7_.refs_17_), channel_id=1, source_target_pairs={{0,8},{2,6},{8,16},{10,2},{16,24},{18,10},{24,28},{26,18},{28,20},... | collective-permute-start | bytes 995336 | tf_op jit(solution)/shard_map/ppermute | solution.py:313
  15.3 0.9 collective-permute-start.17
  16.2 1.1 collective-permute-start.20
  17.3 1.7 %collective-permute-start = (bf16[1296,128]{1,0:T(8,128)(2,1)}, bf16[1296,128]{1,0:T(8,128)(2,1)S(1)}, u32[]{:S(2)}, u32[]{:S(2)}) collective-permute-start(bf16[1296,128]{1,0:T(8,128)(2,1)} %get-tuple-element.6.refs_0_.refs_3_), channel_id=1, source_target_pairs={{0,1},{1,0},{2,3},{3,2},{4,5},{5,4},{6,7},{7,6},{8,9},{9,8},{10,11... | collective-permute-start | bytes 995336 | tf_op jit(solution)/shard_map/ppermute | solution.py:281
  19.0 3.1 %collective-permute-done.17.refs_1_.refs_6_ = bf16[784,128]{1,0:T(8,128)(2,1)S(1)} collective-permute-done((bf16[784,128]{1,0:T(8,128)(2,1)}, bf16[784,128]{1,0:T(8,128)(2,1)S(1)}, u32[]{:S(2)}, u32[]{:S(2)}) %collective-permute-start.17) | collective-permute-done | bytes 200736 | tf_op jit(solution)/shard_map/ppermute | solution.py:316
  22.1 2.3 %collective-permute-done.20.refs_7_.refs_18_ = bf16[784,128]{1,0:T(8,128)(2,1)S(1)} collective-permute-done((bf16[784,128]{1,0:T(8,128)(2,1)}, bf16[784,128]{1,0:T(8,128)(2,1)S(1)}, u32[]{:S(2)}, u32[]{:S(2)}) %collective-permute-start.20) | collective-permute-done | bytes 200736 | tf_op jit(solution)/shard_map/ppermute | solution.py:313
  24.4 1.3 %collective-permute-start.3 = (bf16[1296,128]{1,0:T(8,128)(2,1)S(1)}, bf16[1296,128]{1,0:T(8,128)(2,1)S(1)}, u32[]{:S(2)}, u32[]{:S(2)}) collective-permute-start(bf16[1296,128]{1,0:T(8,128)(2,1)S(1)} %collective-permute-done.2.refs_1_.refs_5_), channel_id=1, source_target_pairs={{8,0},{6,2},{16,8},{2,10},{24,16},{10,18},{28,24},{18,26},{20,28},... | collective-permute-start | bytes 995336 | tf_op jit(solution)/shard_map/ppermute | solution.py:316
  25.7 0.8 collective-permute-start.7
  26.5 1.2 %collective-permute-start.18 = (bf16[784,128]{1,0:T(8,128)(2,1)S(1)}, bf16[784,128]{1,0:T(8,128)(2,1)S(1)}, u32[]{:S(2)}, u32[]{:S(2)}) collective-permute-start(bf16[784,128]{1,0:T(8,128)(2,1)S(1)} %collective-permute-done.17.refs_1_.refs_6_), channel_id=1, source_target_pairs={{8,0},{6,2},{16,8},{2,10},{24,16},{10,18},{28,24},{18,26},{20,28},... | collective-permute-start | bytes 602120 | tf_op jit(solution)/shard_map/ppermute | solution.py:316
  27.7 0.8 collective-permute-start.21
  28.5 10.4 %collective-permute-done.18.refs_2_.refs_8_ = bf16[784,128]{1,0:T(8,128)(2,1)S(1)} collective-permute-done((bf16[784,128]{1,0:T(8,128)(2,1)S(1)}, bf16[784,128]{1,0:T(8,128)(2,1)S(1)}, u32[]{:S(2)}, u32[]{:S(2)}) %collective-permute-start.18) | collective-permute-done | bytes 200736 | tf_op jit(solution)/shard_map/ppermute | solution.py:316
  39.0 1.7 %collective-permute-start.4 = (bf16[1296,128]{1,0:T(8,128)(2,1)S(1)}, bf16[1296,128]{1,0:T(8,128)(2,1)S(1)}, u32[]{:S(2)}, u32[]{:S(2)}) collective-permute-start(bf16[1296,128]{1,0:T(8,128)(2,1)S(1)} %collective-permute-done.3.refs_2_.refs_7_), channel_id=1, source_target_pairs={{8,0},{6,2},{16,8},{2,10},{24,16},{10,18},{28,24},{18,26},{20,28},... | collective-permute-start | bytes 995336 | tf_op jit(solution)/shard_map/ppermute | solution.py:316
  40.7 0.4 collective-permute-start.8
  41.2 10.2 %collective-permute-done.22.refs_5_.refs_14_ = bf16[784,128]{1,0:T(8,128)(2,1)S(1)} collective-permute-done((bf16[784,128]{1,0:T(8,128)(2,1)S(1)}, bf16[784,128]{1,0:T(8,128)(2,1)S(1)}, u32[]{:S(2)}, u32[]{:S(2)}) %collective-permute-start.22) | collective-permute-done | bytes 200736 | tf_op jit(solution)/shard_map/ppermute | solution.py:313
  51.5 0.4 collective-permute-start.15
  52.0 0.4 collective-permute-start.14
  52.5 0.5 collective-permute-done.11.refs_10_.refs_23_
  53.1 0.3 collective-permute-done.15.refs_14_.refs_31_
  53.6 0.3 collective-permute-done.12.refs_11_.refs_25_
  53.9 1.7 %collective-permute-start.19 = (bf16[784,128]{1,0:T(8,128)(2,1)S(1)}, bf16[784,128]{1,0:T(8,128)(2,1)S(1)}, u32[]{:S(2)}, u32[]{:S(2)}) collective-permute-start(bf16[784,128]{1,0:T(8,128)(2,1)S(1)} %collective-permute-done.18.refs_2_.refs_8_), channel_id=1, source_target_pairs={{8,0},{6,2},{16,8},{2,10},{24,16},{10,18},{28,24},{18,26},{20,28},... | collective-permute-start | bytes 602120 | tf_op jit(solution)/shard_map/ppermute | solution.py:316
  55.6 0.4 collective-permute-start.23
  56.1 1.0 copy-done
  57.0 0.9 copy-done.2
  58.0 0.8 left.1.left_ref
  58.9 3.0 %square.2.refs_0_ = bf16[256,1280]{1,0:T(8,128)(2,1)S(1)} custom-call(bf16[256,4096]{1,0:T(8,128)(2,1)S(1)} %left.1.left_ref, bf16[1296,128]{1,0:T(8,128)(2,1)S(1)} %copy-done.1, bf16[1296,128]{1,0:T(8,128)(2,1)S(1)} %collective-permute-done.2.refs_1_.refs_5_, bf16[1296,128]{1,0:T(8,128)(2,1)S(1)} %collective-permute-done.3.refs_2_.refs_7_, ...), custom_call_target="tpu_custom_call" | custom-call | tf_op jit(solution)/shard_map/square/pallas_call | solution.py:322
  62.1 1.6 %collective-permute-start.32 = (bf16[256,1280]{1,0:T(8,128)(2,1)S(1)}, bf16[256,1280]{1,0:T(8,128)(2,1)}, u32[]{:S(2)}, u32[]{:S(2)}) collective-permute-start(bf16[256,1280]{1,0:T(8,128)(2,1)S(1)} %square.2.refs_0_), channel_id=1, source_target_pairs={{0,1},{1,0},{2,3},{3,2},{4,5},{5,4},{6,7},{7,6},{8,9},{9,8},{10,11... | collective-permute-start | bytes 1966088 | tf_op jit(solution)/shard_map/ppermute | solution.py:281
  63.7 0.8 collective-permute-start.30
  64.6 0.4 collective-permute-start.29
  65.1 0.5 collective-permute-done.30.refs_14_.refs_32_
  65.6 0.4 collective-permute-done.27.refs_11_.refs_26_
  66.2 0.3 collective-permute-done.28.refs_12_.refs_28_
  66.6 1.9 %square.3.refs_1_ = bf16[256,768]{1,0:T(8,128)(2,1)S(1)} custom-call(bf16[256,4096]{1,0:T(8,128)(2,1)S(1)} %left.1.left_ref, bf16[784,128]{1,0:T(8,128)(2,1)S(1)} %copy-done.3, bf16[784,128]{1,0:T(8,128)(2,1)S(1)} %collective-permute-done.17.refs_1_.refs_6_, bf16[784,128]{1,0:T(8,128)(2,1)S(1)} %collective-permute-done.18.refs_2_.refs_8_, ...), custom_call_target="tpu_custom_call" | custom-call | tf_op jit(solution)/shard_map/square/pallas_call | solution.py:322
  68.6 0.6 collective-permute-start.33
  69.2 10.6 %collective-permute-done.32.refs_2_ = bf16[256,1280]{1,0:T(8,128)(2,1)} collective-permute-done((bf16[256,1280]{1,0:T(8,128)(2,1)S(1)}, bf16[256,1280]{1,0:T(8,128)(2,1)}, u32[]{:S(2)}, u32[]{:S(2)}) %collective-permute-start.32) | collective-permute-done | bytes 655392 | tf_op jit(solution)/shard_map/ppermute | solution.py:281
  79.8 1.0 copy-done.5
  80.8 1.0 copy-done.7
  81.8 1.0 copy-done.9
  82.7 1.0 copy-done.11
  83.7 1.0 copy-done.13
  84.7 1.0 copy-done.15
  85.7 1.0 copy-done.17
  86.6 1.0 copy-done.19
  87.6 1.0 copy-done.21
  88.6 1.0 copy-done.23
  89.6 0.9 copy-done.25
  90.5 0.9 copy-done.27
  91.4 0.9 copy-done.29
  92.4 0.9 copy-done.31
  93.3 0.9 copy-done.33
  94.2 0.9 copy-done.35
  95.1 0.9 copy-done.37
  96.1 0.9 copy-done.39
  97.0 0.9 copy-done.41
  97.9 0.9 copy-done.43
  98.9 0.9 copy-done.45
  99.8 0.9 copy-done.47
  100.7 0.9 copy-done.49
  101.6 0.9 copy-done.51
  102.6 9.6 %cube.1 = (f32[256,2048]{1,0:T(8,128)S(1)}, bf16[2,8,2,128,128]{4,3,2,1,0:T(8,128)(2,1)}) custom-call(s32[2,8,2]{2,1,0:T(8,128)S(1)} %copy.5.keep_ref, bf16[256,1280]{1,0:T(8,128)(2,1)S(1)} %square.2.refs_0_, bf16[256,768]{1,0:T(8,128)(2,1)S(1)} %square.3.refs_1_, bf16[256,1280]{1,0:T(8,128)(2,1)} %collective-permute-done.32.refs_2_, ...), custom_call_target="tpu_custom_call" | custom-call | tf_op jit(solution)/shard_map/cube/pallas_call | solution.py:336
  112.2 4.3 %final.1 = bf16[2,8,2,128,128]{4,3,2,1,0:T(8,128)(2,1)} custom-call(s32[2,8,2]{2,1,0:T(8,128)S(1)} %copy.5.keep_ref, f32[256,2048]{1,0:T(8,128)S(1)} %get-tuple-element.9.acc_in, bf16[256,1280]{1,0:T(8,128)(2,1)S(1)} %square.2.refs_0_, bf16[256,768]{1,0:T(8,128)(2,1)S(1)} %square.3.refs_1_, bf16[256,768]{1,0:T(8,128)(2,1)} %collective-permute-done.33.refs_2_, ...), custom_call_target="tpu_custom_call" | custom-call | tf_op jit(solution)/shard_map/final/pallas_call | solution.py:352
  (117 shorter events, 1.7 us)
Async XLA Ops:
  2.5 11.2 %collective-permute-start.5 = (bf16[1296,128]{1,0:T(8,128)(2,1)}, bf16[1296,128]{1,0:T(8,128)(2,1)S(1)}, u32[]{:S(2)}, u32[]{:S(2)}) collective-permute-start(bf16[1296,128]{1,0:T(8,128)(2,1)} %get-tuple-element.6.refs_0_.refs_3_), channel_id=1, source_target_pairs={{0,8},{2,6},{8,16},{10,2},{16,24},{18,10},{24,28},{26,18},{28,20},... | collective-permute-start | bytes 995336 | tf_op jit(solution)/shard_map/ppermute | solution.py:313
  5.5 18.9 %collective-permute-start.2 = (bf16[1296,128]{1,0:T(8,128)(2,1)}, bf16[1296,128]{1,0:T(8,128)(2,1)S(1)}, u32[]{:S(2)}, u32[]{:S(2)}) collective-permute-start(bf16[1296,128]{1,0:T(8,128)(2,1)} %get-tuple-element.6.refs_0_.refs_3_), channel_id=1, source_target_pairs={{8,0},{6,2},{16,8},{2,10},{24,16},{10,18},{28,24},{18,26},{20,28},... | collective-permute-start | bytes 995336 | tf_op jit(solution)/shard_map/ppermute | solution.py:316
  5.5 11.8 %collective-permute-start.1 = (bf16[784,128]{1,0:T(8,128)(2,1)}, bf16[784,128]{1,0:T(8,128)(2,1)S(1)}, u32[]{:S(2)}, u32[]{:S(2)}) collective-permute-start(bf16[784,128]{1,0:T(8,128)(2,1)} %get-tuple-element.7.refs_1_.refs_0_.refs_4_), channel_id=1, source_target_pairs={{0,1},{1,0},{2,3},{3,2},{4,5},{5,4},{6,7},{7,6},{8,9},{9,8},{10,11... | collective-permute-start | bytes 602120 | tf_op jit(solution)/shard_map/ppermute | solution.py:281
  13.8 11.9 %collective-permute-start.6 = (bf16[1296,128]{1,0:T(8,128)(2,1)S(1)}, bf16[1296,128]{1,0:T(8,128)(2,1)S(1)}, u32[]{:S(2)}, u32[]{:S(2)}) collective-permute-start(bf16[1296,128]{1,0:T(8,128)(2,1)S(1)} %collective-permute-done.5.refs_7_.refs_17_), channel_id=1, source_target_pairs={{0,8},{2,6},{8,16},{10,2},{16,24},{18,10},{24,28},{26,18},{28,20},... | collective-permute-start | bytes 995336 | tf_op jit(solution)/shard_map/ppermute | solution.py:313
  15.3 6.8 %collective-permute-start.17 = (bf16[784,128]{1,0:T(8,128)(2,1)}, bf16[784,128]{1,0:T(8,128)(2,1)S(1)}, u32[]{:S(2)}, u32[]{:S(2)}) collective-permute-start(bf16[784,128]{1,0:T(8,128)(2,1)} %get-tuple-element.7.refs_1_.refs_0_.refs_4_), channel_id=1, source_target_pairs={{8,0},{6,2},{16,8},{2,10},{24,16},{10,18},{28,24},{18,26},{20,28},... | collective-permute-start | bytes 602120 | tf_op jit(solution)/shard_map/ppermute | solution.py:316
  16.2 8.2 %collective-permute-start.20 = (bf16[784,128]{1,0:T(8,128)(2,1)}, bf16[784,128]{1,0:T(8,128)(2,1)S(1)}, u32[]{:S(2)}, u32[]{:S(2)}) collective-permute-start(bf16[784,128]{1,0:T(8,128)(2,1)} %get-tuple-element.7.refs_1_.refs_0_.refs_4_), channel_id=1, source_target_pairs={{0,8},{2,6},{8,16},{10,2},{16,24},{18,10},{24,28},{26,18},{28,20},... | collective-permute-start | bytes 602120 | tf_op jit(solution)/shard_map/ppermute | solution.py:313
  17.3 10.4 %collective-permute-start = (bf16[1296,128]{1,0:T(8,128)(2,1)}, bf16[1296,128]{1,0:T(8,128)(2,1)S(1)}, u32[]{:S(2)}, u32[]{:S(2)}) collective-permute-start(bf16[1296,128]{1,0:T(8,128)(2,1)} %get-tuple-element.6.refs_0_.refs_3_), channel_id=1, source_target_pairs={{0,1},{1,0},{2,3},{3,2},{4,5},{5,4},{6,7},{7,6},{8,9},{9,8},{10,11... | collective-permute-start | bytes 995336 | tf_op jit(solution)/shard_map/ppermute | solution.py:281
  22.1 4.4 %collective-permute-start.24 = (bf16[784,128]{1,0:T(8,128)(2,1)}, bf16[784,128]{1,0:T(8,128)(2,1)S(1)}, u32[]{:S(2)}, u32[]{:S(2)}) collective-permute-start(bf16[784,128]{1,0:T(8,128)(2,1)} %get-tuple-element.7.refs_1_.refs_0_.refs_4_), channel_id=1, source_target_pairs={{0,2},{2,0},{4,6},{6,4},{8,10},{10,8},{12,14},{14,12},{16,18},{18,... | collective-permute-start | bytes 602120 | tf_op jit(solution)/shard_map/ppermute | solution.py:321
  24.4 42.1 %copy-start.24 = (bf16[784,128]{1,0:T(8,128)(2,1)}, bf16[784,128]{1,0:T(8,128)(2,1)S(1)}, u32[]{:S(2)}) copy-start(bf16[784,128]{1,0:T(8,128)(2,1)S(1)} %collective-permute-done.20.refs_7_.refs_18_) | copy-start | bytes 602116
  24.4 4.1 %collective-permute-start.9 = (bf16[1296,128]{1,0:T(8,128)(2,1)}, bf16[1296,128]{1,0:T(8,128)(2,1)S(1)}, u32[]{:S(2)}, u32[]{:S(2)}) collective-permute-start(bf16[1296,128]{1,0:T(8,128)(2,1)} %get-tuple-element.6.refs_0_.refs_3_), channel_id=1, source_target_pairs={{0,2},{2,0},{4,6},{6,4},{8,10},{10,8},{12,14},{14,12},{16,18},{18,... | collective-permute-start | bytes 995336 | tf_op jit(solution)/shard_map/ppermute | solution.py:321
  24.4 14.6 %collective-permute-start.3 = (bf16[1296,128]{1,0:T(8,128)(2,1)S(1)}, bf16[1296,128]{1,0:T(8,128)(2,1)S(1)}, u32[]{:S(2)}, u32[]{:S(2)}) collective-permute-start(bf16[1296,128]{1,0:T(8,128)(2,1)S(1)} %collective-permute-done.2.refs_1_.refs_5_), channel_id=1, source_target_pairs={{8,0},{6,2},{16,8},{2,10},{24,16},{10,18},{28,24},{18,26},{20,28},... | collective-permute-start | bytes 995336 | tf_op jit(solution)/shard_map/ppermute | solution.py:316
  25.7 15.0 %collective-permute-start.7 = (bf16[1296,128]{1,0:T(8,128)(2,1)S(1)}, bf16[1296,128]{1,0:T(8,128)(2,1)S(1)}, u32[]{:S(2)}, u32[]{:S(2)}) collective-permute-start(bf16[1296,128]{1,0:T(8,128)(2,1)S(1)} %collective-permute-done.6.refs_6_.refs_15_), channel_id=1, source_target_pairs={{0,8},{2,6},{8,16},{10,2},{16,24},{18,10},{24,28},{26,18},{28,20},... | collective-permute-start | bytes 995336 | tf_op jit(solution)/shard_map/ppermute | solution.py:313
  26.5 40.0 %copy-start.26 = (bf16[784,128]{1,0:T(8,128)(2,1)}, bf16[784,128]{1,0:T(8,128)(2,1)S(1)}, u32[]{:S(2)}) copy-start(bf16[784,128]{1,0:T(8,128)(2,1)S(1)} %collective-permute-done.24.refs_8_.refs_20_) | copy-start | bytes 602116
  26.5 12.5 %collective-permute-start.18 = (bf16[784,128]{1,0:T(8,128)(2,1)S(1)}, bf16[784,128]{1,0:T(8,128)(2,1)S(1)}, u32[]{:S(2)}, u32[]{:S(2)}) collective-permute-start(bf16[784,128]{1,0:T(8,128)(2,1)S(1)} %collective-permute-done.17.refs_1_.refs_6_), channel_id=1, source_target_pairs={{8,0},{6,2},{16,8},{2,10},{24,16},{10,18},{28,24},{18,26},{20,28},... | collective-permute-start | bytes 602120 | tf_op jit(solution)/shard_map/ppermute | solution.py:316
  27.7 13.4 %collective-permute-start.21 = (bf16[784,128]{1,0:T(8,128)(2,1)S(1)}, bf16[784,128]{1,0:T(8,128)(2,1)S(1)}, u32[]{:S(2)}, u32[]{:S(2)}) collective-permute-start(bf16[784,128]{1,0:T(8,128)(2,1)S(1)} %collective-permute-done.20.refs_7_.refs_18_), channel_id=1, source_target_pairs={{0,8},{2,6},{8,16},{10,2},{16,24},{18,10},{24,28},{26,18},{28,20},... | collective-permute-start | bytes 602120 | tf_op jit(solution)/shard_map/ppermute | solution.py:313
  28.5 22.9 %collective-permute-start.10 = (bf16[1296,128]{1,0:T(8,128)(2,1)S(1)}, bf16[1296,128]{1,0:T(8,128)(2,1)S(1)}, u32[]{:S(2)}, u32[]{:S(2)}) collective-permute-start(bf16[1296,128]{1,0:T(8,128)(2,1)S(1)} %collective-permute-done.5.refs_7_.refs_17_), channel_id=1, source_target_pairs={{0,2},{2,0},{4,6},{6,4},{8,10},{10,8},{12,14},{14,12},{16,18},{18,... | collective-permute-start | bytes 995336 | tf_op jit(solution)/shard_map/ppermute | solution.py:321
  39.0 27.5 %copy-start.28 = (bf16[784,128]{1,0:T(8,128)(2,1)}, bf16[784,128]{1,0:T(8,128)(2,1)S(1)}, u32[]{:S(2)}) copy-start(bf16[784,128]{1,0:T(8,128)(2,1)S(1)} %collective-permute-done.18.refs_2_.refs_8_) | copy-start | bytes 602116
  39.0 12.9 %collective-permute-start.16 = (bf16[1296,128]{1,0:T(8,128)(2,1)S(1)}, bf16[1296,128]{1,0:T(8,128)(2,1)S(1)}, u32[]{:S(2)}, u32[]{:S(2)}) collective-permute-start(bf16[1296,128]{1,0:T(8,128)(2,1)S(1)} %collective-permute-done.2.refs_1_.refs_5_), channel_id=1, source_target_pairs={{0,2},{2,0},{4,6},{6,4},{8,10},{10,8},{12,14},{14,12},{16,18},{18,... | collective-permute-start | bytes 995336 | tf_op jit(solution)/shard_map/ppermute | solution.py:321
  39.0 13.0 %collective-permute-start.4 = (bf16[1296,128]{1,0:T(8,128)(2,1)S(1)}, bf16[1296,128]{1,0:T(8,128)(2,1)S(1)}, u32[]{:S(2)}, u32[]{:S(2)}) collective-permute-start(bf16[1296,128]{1,0:T(8,128)(2,1)S(1)} %collective-permute-done.3.refs_2_.refs_7_), channel_id=1, source_target_pairs={{8,0},{6,2},{16,8},{2,10},{24,16},{10,18},{28,24},{18,26},{20,28},... | collective-permute-start | bytes 995336 | tf_op jit(solution)/shard_map/ppermute | solution.py:316
  40.7 21.3 %copy-start.4 = (bf16[1296,128]{1,0:T(8,128)(2,1)}, bf16[1296,128]{1,0:T(8,128)(2,1)S(1)}, u32[]{:S(2)}) copy-start(bf16[1296,128]{1,0:T(8,128)(2,1)S(1)} %collective-permute-done.7.refs_5_.refs_13_) | copy-start | bytes 995332
  40.7 11.7 %collective-permute-start.8 = (bf16[1296,128]{1,0:T(8,128)(2,1)S(1)}, bf16[1296,128]{1,0:T(8,128)(2,1)S(1)}, u32[]{:S(2)}, u32[]{:S(2)}) collective-permute-start(bf16[1296,128]{1,0:T(8,128)(2,1)S(1)} %collective-permute-done.7.refs_5_.refs_13_), channel_id=1, source_target_pairs={{0,8},{2,6},{8,16},{10,2},{16,24},{18,10},{24,28},{26,18},{28,20},... | collective-permute-start | bytes 995336 | tf_op jit(solution)/shard_map/ppermute | solution.py:313
  41.1 25.4 %copy-start.30 = (bf16[784,128]{1,0:T(8,128)(2,1)}, bf16[784,128]{1,0:T(8,128)(2,1)S(1)}, u32[]{:S(2)}) copy-start(bf16[784,128]{1,0:T(8,128)(2,1)S(1)} %collective-permute-done.21.refs_6_.refs_16_) | copy-start | bytes 602116
  41.1 10.3 %collective-permute-start.22 = (bf16[784,128]{1,0:T(8,128)(2,1)S(1)}, bf16[784,128]{1,0:T(8,128)(2,1)S(1)}, u32[]{:S(2)}, u32[]{:S(2)}) collective-permute-start(bf16[784,128]{1,0:T(8,128)(2,1)S(1)} %collective-permute-done.21.refs_6_.refs_16_), channel_id=1, source_target_pairs={{0,8},{2,6},{8,16},{10,2},{16,24},{18,10},{24,28},{26,18},{28,20},... | collective-permute-start | bytes 602120 | tf_op jit(solution)/shard_map/ppermute | solution.py:313
  51.4 15.2 %copy-start.32 = (bf16[784,128]{1,0:T(8,128)(2,1)}, bf16[784,128]{1,0:T(8,128)(2,1)S(1)}, u32[]{:S(2)}) copy-start(bf16[784,128]{1,0:T(8,128)(2,1)S(1)} %collective-permute-done.22.refs_5_.refs_14_) | copy-start | bytes 602116
  51.4 1.6 %collective-permute-start.11 = (bf16[1296,128]{1,0:T(8,128)(2,1)S(1)}, bf16[1296,128]{1,0:T(8,128)(2,1)S(1)}, u32[]{:S(2)}, u32[]{:S(2)}) collective-permute-start(bf16[1296,128]{1,0:T(8,128)(2,1)S(1)} %collective-permute-done.6.refs_6_.refs_15_), channel_id=1, source_target_pairs={{0,2},{2,0},{4,6},{6,4},{8,10},{10,8},{12,14},{14,12},{16,18},{18,... | collective-permute-start | bytes 995336 | tf_op jit(solution)/shard_map/ppermute | solution.py:321
  51.5 10.5 %copy-start.6 = (bf16[1296,128]{1,0:T(8,128)(2,1)}, bf16[1296,128]{1,0:T(8,128)(2,1)S(1)}, u32[]{:S(2)}) copy-start(bf16[1296,128]{1,0:T(8,128)(2,1)S(1)} %collective-permute-done.10.refs_9_.refs_21_) | copy-start | bytes 995332
  51.5 2.0 %collective-permute-start.15 = (bf16[1296,128]{1,0:T(8,128)(2,1)S(1)}, bf16[1296,128]{1,0:T(8,128)(2,1)S(1)}, u32[]{:S(2)}, u32[]{:S(2)}) collective-permute-start(bf16[1296,128]{1,0:T(8,128)(2,1)S(1)} %collective-permute-done.3.refs_2_.refs_7_), channel_id=1, source_target_pairs={{0,2},{2,0},{4,6},{6,4},{8,10},{10,8},{12,14},{14,12},{16,18},{18,... | collective-permute-start | bytes 995336 | tf_op jit(solution)/shard_map/ppermute | solution.py:321
  51.9 10.1 %copy-start.8 = (bf16[1296,128]{1,0:T(8,128)(2,1)}, bf16[1296,128]{1,0:T(8,128)(2,1)S(1)}, u32[]{:S(2)}) copy-start(bf16[1296,128]{1,0:T(8,128)(2,1)S(1)} %collective-permute-done.16.refs_15_.refs_33_) | copy-start | bytes 995332
  51.9 2.1 %collective-permute-start.12 = (bf16[1296,128]{1,0:T(8,128)(2,1)S(1)}, bf16[1296,128]{1,0:T(8,128)(2,1)S(1)}, u32[]{:S(2)}, u32[]{:S(2)}) collective-permute-start(bf16[1296,128]{1,0:T(8,128)(2,1)S(1)} %collective-permute-done.7.refs_5_.refs_13_), channel_id=1, source_target_pairs={{0,2},{2,0},{4,6},{6,4},{8,10},{10,8},{12,14},{14,12},{16,18},{18,... | collective-permute-start | bytes 995336 | tf_op jit(solution)/shard_map/ppermute | solution.py:321
  52.0 10.0 %copy-start.10 = (bf16[1296,128]{1,0:T(8,128)(2,1)}, bf16[1296,128]{1,0:T(8,128)(2,1)S(1)}, u32[]{:S(2)}) copy-start(bf16[1296,128]{1,0:T(8,128)(2,1)S(1)} %collective-permute-done.4.refs_3_.refs_9_) | copy-start | bytes 995332
  52.0 3.6 %collective-permute-start.14 = (bf16[1296,128]{1,0:T(8,128)(2,1)S(1)}, bf16[1296,128]{1,0:T(8,128)(2,1)S(1)}, u32[]{:S(2)}, u32[]{:S(2)}) collective-permute-start(bf16[1296,128]{1,0:T(8,128)(2,1)S(1)} %collective-permute-done.4.refs_3_.refs_9_), channel_id=1, source_target_pairs={{0,2},{2,0},{4,6},{6,4},{8,10},{10,8},{12,14},{14,12},{16,18},{18,... | collective-permute-start | bytes 995336 | tf_op jit(solution)/shard_map/ppermute | solution.py:321
  52.4 9.6 %copy-start.12 = (bf16[1296,128]{1,0:T(8,128)(2,1)}, bf16[1296,128]{1,0:T(8,128)(2,1)S(1)}, u32[]{:S(2)}) copy-start(bf16[1296,128]{1,0:T(8,128)(2,1)S(1)} %collective-permute-done.8.refs_4_.refs_11_) | copy-start | bytes 995332
  52.4 3.2 %collective-permute-start.13 = (bf16[1296,128]{1,0:T(8,128)(2,1)S(1)}, bf16[1296,128]{1,0:T(8,128)(2,1)S(1)}, u32[]{:S(2)}, u32[]{:S(2)}) collective-permute-start(bf16[1296,128]{1,0:T(8,128)(2,1)S(1)} %collective-permute-done.8.refs_4_.refs_11_), channel_id=1, source_target_pairs={{0,2},{2,0},{4,6},{6,4},{8,10},{10,8},{12,14},{14,12},{16,18},{18,... | collective-permute-start | bytes 995336 | tf_op jit(solution)/shard_map/ppermute | solution.py:321
  53.0 9.0 %copy-start.14 = (bf16[1296,128]{1,0:T(8,128)(2,1)}, bf16[1296,128]{1,0:T(8,128)(2,1)S(1)}, u32[]{:S(2)}) copy-start(bf16[1296,128]{1,0:T(8,128)(2,1)S(1)} %collective-permute-done.11.refs_10_.refs_23_) | copy-start | bytes 995332
  53.0 9.1 %collective-permute-start.25 = (bf16[784,128]{1,0:T(8,128)(2,1)S(1)}, bf16[784,128]{1,0:T(8,128)(2,1)S(1)}, u32[]{:S(2)}, u32[]{:S(2)}) collective-permute-start(bf16[784,128]{1,0:T(8,128)(2,1)S(1)} %collective-permute-done.20.refs_7_.refs_18_), channel_id=1, source_target_pairs={{0,2},{2,0},{4,6},{6,4},{8,10},{10,8},{12,14},{14,12},{16,18},{18,... | collective-permute-start | bytes 602120 | tf_op jit(solution)/shard_map/ppermute | solution.py:321
  53.5 8.6 %copy-start.16 = (bf16[1296,128]{1,0:T(8,128)(2,1)}, bf16[1296,128]{1,0:T(8,128)(2,1)S(1)}, u32[]{:S(2)}) copy-start(bf16[1296,128]{1,0:T(8,128)(2,1)S(1)} %collective-permute-done.15.refs_14_.refs_31_) | copy-start | bytes 995332
  53.5 10.2 %collective-permute-start.31 = (bf16[784,128]{1,0:T(8,128)(2,1)S(1)}, bf16[784,128]{1,0:T(8,128)(2,1)S(1)}, u32[]{:S(2)}, u32[]{:S(2)}) collective-permute-start(bf16[784,128]{1,0:T(8,128)(2,1)S(1)} %collective-permute-done.17.refs_1_.refs_6_), channel_id=1, source_target_pairs={{0,2},{2,0},{4,6},{6,4},{8,10},{10,8},{12,14},{14,12},{16,18},{18,... | collective-permute-start | bytes 602120 | tf_op jit(solution)/shard_map/ppermute | solution.py:321
  53.9 8.1 %copy-start.18 = (bf16[1296,128]{1,0:T(8,128)(2,1)}, bf16[1296,128]{1,0:T(8,128)(2,1)S(1)}, u32[]{:S(2)}) copy-start(bf16[1296,128]{1,0:T(8,128)(2,1)S(1)} %collective-permute-done.12.refs_11_.refs_25_) | copy-start | bytes 995332
  53.9 10.5 %collective-permute-start.19 = (bf16[784,128]{1,0:T(8,128)(2,1)S(1)}, bf16[784,128]{1,0:T(8,128)(2,1)S(1)}, u32[]{:S(2)}, u32[]{:S(2)}) collective-permute-start(bf16[784,128]{1,0:T(8,128)(2,1)S(1)} %collective-permute-done.18.refs_2_.refs_8_), channel_id=1, source_target_pairs={{8,0},{6,2},{16,8},{2,10},{24,16},{10,18},{28,24},{18,26},{20,28},... | collective-permute-start | bytes 602120 | tf_op jit(solution)/shard_map/ppermute | solution.py:316
  55.6 6.5 %copy-start.20 = (bf16[1296,128]{1,0:T(8,128)(2,1)}, bf16[1296,128]{1,0:T(8,128)(2,1)S(1)}, u32[]{:S(2)}) copy-start(bf16[1296,128]{1,0:T(8,128)(2,1)S(1)} %collective-permute-done.14.refs_13_.refs_29_) | copy-start | bytes 995332
  55.6 9.0 %collective-permute-start.26 = (bf16[784,128]{1,0:T(8,128)(2,1)S(1)}, bf16[784,128]{1,0:T(8,128)(2,1)S(1)}, u32[]{:S(2)}, u32[]{:S(2)}) collective-permute-start(bf16[784,128]{1,0:T(8,128)(2,1)S(1)} %collective-permute-done.21.refs_6_.refs_16_), channel_id=1, source_target_pairs={{0,2},{2,0},{4,6},{6,4},{8,10},{10,8},{12,14},{14,12},{16,18},{18,... | collective-permute-start | bytes 602120 | tf_op jit(solution)/shard_map/ppermute | solution.py:321
  55.6 6.4 %copy-start.22 = (bf16[1296,128]{1,0:T(8,128)(2,1)}, bf16[1296,128]{1,0:T(8,128)(2,1)S(1)}, u32[]{:S(2)}) copy-start(bf16[1296,128]{1,0:T(8,128)(2,1)S(1)} %collective-permute-done.13.refs_12_.refs_27_) | copy-start | bytes 995332
  55.6 9.4 %collective-permute-start.23 = (bf16[784,128]{1,0:T(8,128)(2,1)S(1)}, bf16[784,128]{1,0:T(8,128)(2,1)S(1)}, u32[]{:S(2)}, u32[]{:S(2)}) collective-permute-start(bf16[784,128]{1,0:T(8,128)(2,1)S(1)} %collective-permute-done.22.refs_5_.refs_14_), channel_id=1, source_target_pairs={{0,8},{2,6},{8,16},{10,2},{16,24},{18,10},{24,28},{26,18},{28,20},... | collective-permute-start | bytes 602120 | tf_op jit(solution)/shard_map/ppermute | solution.py:313
  58.9 7.6 %copy-start.3 = (bf16[784,128]{1,0:T(8,128)(2,1)S(1)}, bf16[784,128]{1,0:T(8,128)(2,1)}, u32[]{:S(2)}) copy-start(bf16[784,128]{1,0:T(8,128)(2,1)} %get-tuple-element.7.refs_1_.refs_0_.refs_4_) | copy-start | bytes 602116
  62.1 7.1 %copy-start.52 = (s32[2,8,2]{1,2,0:T(2,128)S(1)}, s32[2,8,2]{1,2,0:T(2,128)}, u32[]{:S(2)}) copy-start(s32[2,8,2]{1,2,0:T(2,128)} %param.5) | copy-start | bytes 388
  62.1 6.4 %copy-start.34 = (bf16[784,128]{1,0:T(8,128)(2,1)}, bf16[784,128]{1,0:T(8,128)(2,1)S(1)}, u32[]{:S(2)}) copy-start(bf16[784,128]{1,0:T(8,128)(2,1)S(1)} %collective-permute-done.25.refs_9_.refs_22_) | copy-start | bytes 602116
  62.1 17.7 %collective-permute-start.32 = (bf16[256,1280]{1,0:T(8,128)(2,1)S(1)}, bf16[256,1280]{1,0:T(8,128)(2,1)}, u32[]{:S(2)}, u32[]{:S(2)}) collective-permute-start(bf16[256,1280]{1,0:T(8,128)(2,1)S(1)} %square.2.refs_0_), channel_id=1, source_target_pairs={{0,1},{1,0},{2,3},{3,2},{4,5},{5,4},{6,7},{7,6},{8,9},{9,8},{10,11... | collective-permute-start | bytes 1966088 | tf_op jit(solution)/shard_map/ppermute | solution.py:281
  63.7 4.8 %copy-start.36 = (bf16[784,128]{1,0:T(8,128)(2,1)}, bf16[784,128]{1,0:T(8,128)(2,1)S(1)}, u32[]{:S(2)}) copy-start(bf16[784,128]{1,0:T(8,128)(2,1)S(1)} %collective-permute-done.31.refs_15_.refs_34_) | copy-start | bytes 602116
  63.7 1.9 %collective-permute-start.30 = (bf16[784,128]{1,0:T(8,128)(2,1)S(1)}, bf16[784,128]{1,0:T(8,128)(2,1)S(1)}, u32[]{:S(2)}, u32[]{:S(2)}) collective-permute-start(bf16[784,128]{1,0:T(8,128)(2,1)S(1)} %collective-permute-done.18.refs_2_.refs_8_), channel_id=1, source_target_pairs={{0,2},{2,0},{4,6},{6,4},{8,10},{10,8},{12,14},{14,12},{16,18},{18,... | collective-permute-start | bytes 602120 | tf_op jit(solution)/shard_map/ppermute | solution.py:321
  64.5 4.0 %copy-start.38 = (bf16[784,128]{1,0:T(8,128)(2,1)}, bf16[784,128]{1,0:T(8,128)(2,1)S(1)}, u32[]{:S(2)}) copy-start(bf16[784,128]{1,0:T(8,128)(2,1)S(1)} %collective-permute-done.19.refs_3_.refs_10_) | copy-start | bytes 602116
  64.5 1.4 %collective-permute-start.27 = (bf16[784,128]{1,0:T(8,128)(2,1)S(1)}, bf16[784,128]{1,0:T(8,128)(2,1)S(1)}, u32[]{:S(2)}, u32[]{:S(2)}) collective-permute-start(bf16[784,128]{1,0:T(8,128)(2,1)S(1)} %collective-permute-done.22.refs_5_.refs_14_), channel_id=1, source_target_pairs={{0,2},{2,0},{4,6},{6,4},{8,10},{10,8},{12,14},{14,12},{16,18},{18,... | collective-permute-start | bytes 602120 | tf_op jit(solution)/shard_map/ppermute | solution.py:321
  64.6 4.0 %copy-start.40 = (bf16[784,128]{1,0:T(8,128)(2,1)}, bf16[784,128]{1,0:T(8,128)(2,1)S(1)}, u32[]{:S(2)}) copy-start(bf16[784,128]{1,0:T(8,128)(2,1)S(1)} %collective-permute-done.26.refs_10_.refs_24_) | copy-start | bytes 602116
  64.6 1.6 %collective-permute-start.29 = (bf16[784,128]{1,0:T(8,128)(2,1)S(1)}, bf16[784,128]{1,0:T(8,128)(2,1)S(1)}, u32[]{:S(2)}, u32[]{:S(2)}) collective-permute-start(bf16[784,128]{1,0:T(8,128)(2,1)S(1)} %collective-permute-done.19.refs_3_.refs_10_), channel_id=1, source_target_pairs={{0,2},{2,0},{4,6},{6,4},{8,10},{10,8},{12,14},{14,12},{16,18},{18,... | collective-permute-start | bytes 602120 | tf_op jit(solution)/shard_map/ppermute | solution.py:321
  65.0 3.5 %copy-start.42 = (bf16[784,128]{1,0:T(8,128)(2,1)}, bf16[784,128]{1,0:T(8,128)(2,1)S(1)}, u32[]{:S(2)}) copy-start(bf16[784,128]{1,0:T(8,128)(2,1)S(1)} %collective-permute-done.23.refs_4_.refs_12_) | copy-start | bytes 602116
  65.0 1.5 %collective-permute-start.28 = (bf16[784,128]{1,0:T(8,128)(2,1)S(1)}, bf16[784,128]{1,0:T(8,128)(2,1)S(1)}, u32[]{:S(2)}, u32[]{:S(2)}) collective-permute-start(bf16[784,128]{1,0:T(8,128)(2,1)S(1)} %collective-permute-done.23.refs_4_.refs_12_), channel_id=1, source_target_pairs={{0,2},{2,0},{4,6},{6,4},{8,10},{10,8},{12,14},{14,12},{16,18},{18,... | collective-permute-start | bytes 602120 | tf_op jit(solution)/shard_map/ppermute | solution.py:321
  65.5 3.0 %copy-start.44 = (bf16[784,128]{1,0:T(8,128)(2,1)}, bf16[784,128]{1,0:T(8,128)(2,1)S(1)}, u32[]{:S(2)}) copy-start(bf16[784,128]{1,0:T(8,128)(2,1)S(1)} %collective-permute-done.30.refs_14_.refs_32_) | copy-start | bytes 602116
  65.9 2.6 %copy-start.46 = (bf16[784,128]{1,0:T(8,128)(2,1)}, bf16[784,128]{1,0:T(8,128)(2,1)S(1)}, u32[]{:S(2)}) copy-start(bf16[784,128]{1,0:T(8,128)(2,1)S(1)} %collective-permute-done.27.refs_11_.refs_26_) | copy-start | bytes 602116
  66.2 2.4 %copy-start.48 = (bf16[784,128]{1,0:T(8,128)(2,1)}, bf16[784,128]{1,0:T(8,128)(2,1)S(1)}, u32[]{:S(2)}) copy-start(bf16[784,128]{1,0:T(8,128)(2,1)S(1)} %collective-permute-done.29.refs_13_.refs_30_) | copy-start | bytes 602116
  66.5 2.0 %copy-start.50 = (bf16[784,128]{1,0:T(8,128)(2,1)}, bf16[784,128]{1,0:T(8,128)(2,1)S(1)}, u32[]{:S(2)}) copy-start(bf16[784,128]{1,0:T(8,128)(2,1)S(1)} %collective-permute-done.28.refs_12_.refs_28_) | copy-start | bytes 602116
  68.6 43.6 %collective-permute-start.33 = (bf16[256,768]{1,0:T(8,128)(2,1)S(1)}, bf16[256,768]{1,0:T(8,128)(2,1)}, u32[]{:S(2)}, u32[]{:S(2)}) collective-permute-start(bf16[256,768]{1,0:T(8,128)(2,1)S(1)} %square.3.refs_1_), channel_id=1, source_target_pairs={{0,1},{1,0},{2,3},{3,2},{4,5},{5,4},{6,7},{7,6},{8,9},{9,8},{10,11... | collective-permute-start | bytes 1179656 | tf_op jit(solution)/shard_map/ppermute | solution.py:281
  79.8 1.0 copy-start.5
  80.8 1.0 copy-start.7
  81.8 1.0 copy-start.9
  82.7 1.0 copy-start.11
  (23 other events, 21.7 us)

commit v2 on v0

v2 whole, which is shorter than its diff:
```python
import functools

import jax
import jax.numpy as jnp
from jax import lax
from jax.experimental import pallas as pl
from jax.experimental.pallas import tpu as pltpu
from jax.sharding import PartitionSpec as P

CORES = 2
FLAG_ROWS = 16


def chunk_sizes(panels):
    last = max(1, (panels * 3) // 8)
    return (panels - last, last)


def hop_groups(chips):
    last = chips // 2
    return ((0, 1), tuple(range(2, last)), (last,))


def ring_chip(position, chips):
    up = 2 * position
    down = 2 * (chips - 1 - position) + 1
    if isinstance(position, int):
        return up if position < chips // 2 else down
    return jnp.where(position < chips // 2, up, down)


def ring_place(chip, chips):
    return jnp.where(chip % 2 == 0, chip // 2, chips - 1 - chip // 2)


def ring_pairs(rows):
    chips = rows // CORES
    pairs = []
    for position in range(chips):
        for core in range(CORES):
            step = 1 if core == 0 else -1
            source = ring_chip(position, chips) * CORES + core
            target = ring_chip((position + step) % chips, chips) * CORES + core
            pairs.append((source, target))
    return pairs


def hop_slabs(hop, chips):
    return 2 if hop == 0 or 2 * hop == chips else 4


def slot_of(slab, row, rows):
    chips = rows // CORES
    core = row % CORES
    other = jnp.where(slab % CORES == core, 0, 1)
    step = (1 - 2 * core) * (2 * other - 1)
    distance = (ring_place(slab // CORES, chips) - ring_place(row // CORES, chips)) * step
    hop = lax.rem(distance + chips, chips)
    near = 2 + 4 * (hop - 1)
    far = 2 + 4 * (chips - hop - 1) + 2
    return jnp.where(hop == 0, 0, jnp.where(hop <= chips // 2, near, far)) + other


def slab_of(slot, row, rows):
    chips = rows // CORES
    core = row % CORES
    other = slot % 2
    hop = 0 if slot < 2 else (slot - 2) // 4 + 1
    if slot >= 2 and (slot - 2) % 4 >= 2:
        hop = chips - hop
    step = (1 - 2 * core) * (2 * other - 1)
    position = lax.rem(ring_place(row // CORES, chips) + step * hop + chips, chips)
    return ring_chip(position, chips) * CORES + (1 - core if other else core)


def lane_flags(values, rows, size, first, lanes):
    width, panels = values.shape
    row = lax.broadcasted_iota(jnp.int32, (rows, panels), 0)
    lane = lax.broadcasted_iota(jnp.int32, (rows, panels), 1)
    total = jnp.zeros((rows, 1), jnp.int32)
    for local in range(width):
        start = local * size
        here = (row >= start) & (row < start + size) & (lane == first + row - start)
        picked = jnp.where(here, jnp.broadcast_to(values[local : local + 1, :], here.shape), 0)
        total += jnp.sum(picked, axis=1, keepdims=True)
    return jnp.broadcast_to(total.astype(jnp.float32), (rows, lanes))


def pack_kernel(size, first, cols_ref, x_ref, *refs):
    out = refs[-1]
    width, tile = x_ref.shape[0], x_ref.shape[-1]
    for local in range(width):
        for panel in range(size):
            index = local * size + panel
            out[index * tile : (index + 1) * tile, :] = x_ref[local, first + panel, 0]
    base = width * size * tile
    flags = lane_flags(cols_ref[...], FLAG_ROWS, size, first, tile)
    out[base : base + FLAG_ROWS, :] = flags.astype(jnp.bfloat16)


def halves(payload, flags, index, tile):
    block = payload[index * tile : (index + 1) * tile, :]
    right = block * flags[index : index + 1, :]
    return block - right, right


def left_kernel(sizes, rows, groups, width, tile, keep_ref, *refs):
    out, kept = refs[-2:]
    dense = width * tile
    row, mine = lax.axis_index("row"), lax.axis_index("col")
    panels = sum(sizes)
    index = 0
    for shift in range(groups):
        group = lax.rem(mine - shift + groups, groups)
        first = 0
        for size in sizes:
            payload = refs[index]
            index += 1
            base = width * size * tile
            flags = payload[base : base + FLAG_ROWS, :]
            for panel in range(size):
                slot = slot_of(group * panels + first + panel, row, rows)
                start = pl.multiple_of(slot * dense, dense)
                for local in range(width):
                    left, right = halves(payload, flags, local * size + panel, tile)
                    part = slice(local * tile, (local + 1) * tile)
                    out[part, pl.ds(start, tile)] = left
                    out[part, pl.ds(start + tile, tile)] = right
            first += size
    kept[...] = lane_flags(keep_ref[...], kept.shape[0], panels, 0, tile)


def square_kernel(size, width, tile, start, count, first, *refs):
    left_ref, pieces = refs[0], refs[1 : 1 + count]
    out, right = refs[-2:]
    dense = width * tile
    for index, piece in enumerate(pieces):
        base = width * size * tile
        flags = piece[base : base + FLAG_ROWS, :]
        for local in range(width):
            part = slice(index * dense + local * tile, index * dense + (local + 1) * tile)
            for panel in range(size):
                a, b = halves(piece, flags, local * size + panel, tile)
                column = panel * dense
                right[part, column : column + tile] = a
                right[part, column + tile : column + 2 * tile] = b
    total = jnp.dot(
        left_ref[:, start * dense : (start + count) * dense],
        right[...],
        preferred_element_type=jnp.float32,
    )
    if not first:
        total += refs[1 + count][...]
    out[...] = total.astype(out.dtype)


def cube_kernel(sizes, rows, groups, width, tile, spans, kept, *refs):
    chunks = len(sizes)
    dense = width * tile
    panels = sum(sizes)
    own = refs[:chunks]
    received = refs[chunks : chunks + (groups - 1) * (chunks - 1)]
    rights = refs[chunks + (groups - 1) * (chunks - 1) : -4]
    acc, square, later, squares = refs[-4:]
    row, mine = lax.axis_index("row"), lax.axis_index("col")

    def place(source, size, first, group):
        for panel in range(size):
            slot = slot_of(group * panels + first + panel, row, rows)
            value = 0 if source is None else source[:, panel * dense : (panel + 1) * dense]
            value = jnp.zeros((dense, dense), jnp.bfloat16) if source is None else value
            squares[:, pl.ds(pl.multiple_of(slot * dense, dense), dense)] = value

    index = 0
    for shift in range(groups):
        group = lax.rem(mine - shift + groups, groups)
        first = 0
        for chunk, size in enumerate(sizes):
            if shift == 0:
                place(own[chunk], size, first, group)
            elif chunk < chunks - 1:
                place(received[index], size, first, group)
                index += 1
            else:
                place(None, size, first, group)
            first += size

    column = 0
    for chunk, size in enumerate(sizes):
        total = None
        for part, (start, count) in enumerate(spans):
            product = jnp.dot(
                squares[:, start * dense : (start + count) * dense],
                rights[chunk * len(spans) + part][...],
                preferred_element_type=jnp.float32,
            )
            total = product if total is None else total + product
        acc[:, column : column + size * dense] = total
        column += size * dense

    last = sizes[-1]
    for part, (start, count) in enumerate(spans):
        for index in range(count):
            slab = slab_of(start + index, row, rows)
            group, panel = slab // panels, lax.rem(slab, panels)
            shift = lax.rem(mine - group + groups, groups)

            @pl.when((shift > 0) & (panel >= panels - last))
            def _(part=part, index=index, shift=shift, panel=panel):
                where = (shift - 1) * last + panel - (panels - last)
                target = pl.ds(pl.multiple_of(where * dense, dense), dense)
                column = 0
                for chunk, size in enumerate(sizes):
                    later[target, column : column + size * dense] = rights[
                        chunk * len(spans) + part
                    ][index * dense : (index + 1) * dense, :]
                    column += size * dense

    first = 0
    for size, source in zip(sizes, own):
        for panel in range(size):
            for local in range(width):
                part = slice(local * tile, (local + 1) * tile)
                column = panel * dense
                a, b = ordered(
                    kept,
                    local * panels + first + panel,
                    source[part, column : column + dense].astype(jnp.float32),
                    tile,
                )
                square[local, first + panel, 0] = a.astype(square.dtype)
                square[local, first + panel, 1] = b.astype(square.dtype)
        first += size


def ordered(kept, index, value, tile):
    left, right = value[:, :tile], value[:, tile:]
    swap = jnp.broadcast_to(kept[index : index + 1, :] > 0.5, left.shape)
    return jnp.where(swap, right, left), jnp.where(swap, left, right)


def final_kernel(sizes, groups, width, tile, kept, acc, later, *refs):
    chunks = len(sizes)
    own = refs[:chunks]
    received = refs[chunks : chunks + groups - 1]
    purified = refs[-1]
    dense = width * tile
    panels = sum(sizes)
    span = sizes[-1] * dense
    first = 0
    for size, source in zip(sizes, own):
        columns = slice(first * dense, (first + size) * dense)
        total = acc[:, columns]
        for shift in range(groups - 1):
            total += jnp.dot(
                received[shift][...],
                later[shift * span : (shift + 1) * span, columns],
                preferred_element_type=jnp.float32,
            )
        value = 3.0 * source[...].astype(jnp.float32) - 2.0 * total
        for panel in range(size):
            for local in range(width):
                part = value[
                    local * tile : (local + 1) * tile, panel * dense : (panel + 1) * dense
                ]
                a, b = ordered(kept, local * panels + first + panel, part, tile)
                purified[local, first + panel, 0] = a.astype(purified.dtype)
                purified[local, first + panel, 1] = b.astype(purified.dtype)
        first += size


def vmem(count):
    return [pl.BlockSpec(memory_space=pltpu.VMEM)] * count


def anywhere(count):
    return [pl.BlockSpec(memory_space=pl.ANY)] * count


def params(mib):
    return pltpu.CompilerParams(vmem_limit_bytes=mib * 1024 * 1024)


def shards(rows, groups, x_tiles, x_cols, keep_cols):
    width, panels, tile = x_tiles.shape[0], x_tiles.shape[1], x_tiles.shape[-1]
    dense = width * tile
    sizes = chunk_sizes(panels)
    chips = rows // CORES
    forward = ring_pairs(rows)
    backward = [(target, source) for source, target in forward]
    sibling = [(device, device ^ 1) for device in range(rows)]
    bf16, f32 = jnp.bfloat16, jnp.float32

    def across(value, shift):
        pairs = [(group, (group + shift) % groups) for group in range(groups)]
        return lax.ppermute(value, "col", pairs)

    cols = x_cols.reshape(width, panels)
    spans, start = [], 0
    for group in hop_groups(chips):
        count = sum(hop_slabs(hop, chips) for hop in group)
        spans.append((start, count))
        start += count

    def pack(chunk, *after):
        size = sizes[chunk]
        return pl.pallas_call(
            functools.partial(pack_kernel, size, sum(sizes[:chunk])),
            out_shape=jax.ShapeDtypeStruct((width * size * tile + FLAG_ROWS, tile), bf16),
            in_specs=vmem(2) + anywhere(len(after)),
            out_specs=vmem(1)[0],
            compiler_params=params(4),
            name="pack",
        )(cols, x_tiles, *after)

    payloads = [pack(chunk) for chunk in range(len(sizes))]
    lefts = list(payloads)
    for shift in range(1, groups):
        lefts += [across(payload, shift) for payload in payloads]
    kept_rows = -(-width * panels // 8) * 8
    left, kept = pl.pallas_call(
        functools.partial(left_kernel, sizes, rows, groups, width, tile),
        out_shape=[
            jax.ShapeDtypeStruct((dense, rows * dense), bf16),
            jax.ShapeDtypeStruct((kept_rows, tile), f32),
        ],
        in_specs=vmem(1 + len(lefts)),
        out_specs=vmem(2),
        compiler_params=params(4),
        name="left",
    )(keep_cols[:, :, 0], *lefts)

    squares, received, rights = [], [], []
    gate = None
    for chunk, payload in enumerate(payloads):
        size = sizes[chunk]
        if gate is not None:
            payload, gate = lax.optimization_barrier((payload, gate))
        ahead = behind = payload
        total = None
        for group, (start, count) in zip(hop_groups(chips), spans):
            pieces = []
            for hop in group:
                if hop > 0:
                    ahead = lax.ppermute(ahead, "row", forward)
                pieces += [ahead, lax.ppermute(ahead, "row", sibling)]
                if 0 < hop < chips - chips // 2:
                    behind = lax.ppermute(behind, "row", backward)
                    pieces += [behind, lax.ppermute(behind, "row", sibling)]
            last = start + count == rows
            operands = [left] + pieces + ([] if total is None else [total])
            total, right = pl.pallas_call(
                functools.partial(
                    square_kernel, size, width, tile, start, count, total is None
                ),
                out_shape=[
                    jax.ShapeDtypeStruct((dense, size * dense), bf16 if last else f32),
                    jax.ShapeDtypeStruct((count * dense, size * dense), bf16),
                ],
                in_specs=vmem(len(operands)),
                out_specs=vmem(2),
                compiler_params=params(4),
                name="square",
            )(*operands)
            rights.append(right)
            gate = behind
        squares.append(total)
        received.append([across(total, shift) for shift in range(1, groups)])

    already = [part[shift] for shift in range(groups - 1) for part in received[:-1]]
    later_rows = (groups - 1) * sizes[-1] * dense
    acc, square_out, later = pl.pallas_call(
        functools.partial(cube_kernel, sizes, rows, groups, width, tile, spans),
        out_shape=[
            jax.ShapeDtypeStruct((dense, panels * dense), f32),
            jax.ShapeDtypeStruct((width, panels, 2, tile, tile), bf16),
            jax.ShapeDtypeStruct((later_rows, panels * dense), bf16),
        ],
        in_specs=vmem(1 + len(squares) + len(already) + len(rights)),
        out_specs=vmem(3),
        scratch_shapes=[pltpu.VMEM((dense, rows * dense), bf16)],
        compiler_params=params(8),
        name="cube",
    )(kept, *squares, *already, *rights)

    purified = pl.pallas_call(
        functools.partial(final_kernel, sizes, groups, width, tile),
        out_shape=jax.ShapeDtypeStruct((width, panels, 2, tile, tile), bf16),
        in_specs=vmem(3 + len(squares) + groups - 1),
        out_specs=vmem(1)[0],
        compiler_params=params(8),
        name="final",
    )(kept, acc, later, *squares, *received[-1])
    return (square_out, purified)


def solution(mesh):
    in_specs = (P("row", "col", None, None, None), P("row", "col", None), P("row", "col", None))
    out_specs = (P("row", "col", None, None, None), P("row", "col", None, None, None))
    body = functools.partial(shards, mesh.shape["row"], mesh.shape["col"])
    return jax.shard_map(body, mesh=mesh, in_specs=in_specs, out_specs=out_specs, check_vma=False)
```

time: 392 us -> 91.8 us (0.23)
  local copies, waits for them, and re-layouts: 120 us -> 2.4 us
  matrix products: 114 us -> 0 us
  other arithmetic: 36.1 us -> 0 us
  waiting for transfers between devices: 75.7 us -> 48.8 us
  blocking collectives: 22.4 us -> 0 us
  starting transfers between devices: 5.24 us -> 23.4 us
  Pallas kernels: 0 us -> 15.6 us
  between operations: 14.1 us -> 0.77 us
    dot_general x32 -> x0, matrix products: 114 us -> none  [one_slab(): jnp.einsum('iamn,iaqtnk->iqtmk', a_tiles, selected, preferred_element_typ...]
    all_gather x1 -> x0, waiting for transfers between devices: 51.7 us -> none  [shards(): lax.all_gather(x_tiles, 'row', axis=0, tiled=True)]
    gather x64 -> x0, local copies, waits for them, and re-layouts: 40.2 us -> none  [the longest x32 22.3 us: one_slab(): b_rows = jnp.take(b_tiles, a_cols, axis=0)]
    another operation x32 -> x0, local copies, waits for them, and re-layouts: 36 us -> none
    dynamic_slice x64 -> x0, local copies, waits for them, and re-layouts: 34.9 us -> none  [the longest x32 34.6 us: one_slab(): lax.dynamic_slice_in_dim(piece_tiles, step * slab_rows, slab_rows, 0)]
    another operation x68 -> x0, other arithmetic: 31.7 us -> none
    ppermute x4 -> x34, waiting for transfers between devices: 23.3 us -> 48.8 us  [the longest x6 18.6 us: shards(): behind = lax.ppermute(behind, 'row', backward)]
    all_gather x1 -> x0, blocking collectives: 22.4 us -> none  [shards(): lax.all_gather(x_cols, 'row', axis=0, tiled=True)]
  transfers between devices with their start and end apart: 5 -> 34, of which waited for: 2 -> 11; matrix products, arithmetic and copies ran while one was open for 1% -> 1% of each run, Pallas kernels for 0% -> 15%
where the time goes in v2:
time: 91.8 us; the launch traced here: 90.9 us
  waiting for transfers between devices  48.8 us (53%)
  starting transfers between devices  23.4 us (25%)
  Pallas kernels  15.6 us (17%)
  local copies, waits for them, and re-layouts  2.4 us (3%)
    ppermute x6, waiting for transfers between devices, shards(): behind = lax.ppermute(behind, 'row', backward)  18.6 us
    ppermute x4, waiting for transfers between devices, across(): return lax.ppermute(value, 'col', pairs)  15.2 us
    ppermute x8, waiting for transfers between devices, shards(): ahead = lax.ppermute(ahead, 'row', forward)  14.7 us
    ppermute x8, starting transfers between devices, shards(): ahead = lax.ppermute(ahead, 'row', forward)  10.8 us
    pallas_call x1, Pallas kernels, shards(): pl.pallas_call(functools.partial(cube_kernel, sizes, rows, groups, width,...  6.84 us
    pallas_call x6, Pallas kernels, shards(): pl.pallas_call(functools.partial(square_kernel, size, width, tile, start,...  5.95 us
    ppermute x6, starting transfers between devices, shards(): behind = lax.ppermute(behind, 'row', backward)  5.66 us
    ppermute x4, starting transfers between devices, across(): return lax.ppermute(value, 'col', pairs)  4.16 us
  transfers between devices with their start and end apart: 34, of which 11 were waited for; matrix products, arithmetic and copies ran while one was open for 1% of the time, Pallas kernels for 15%

profile of v2, /device:TPU:0, one launch (start us, length us, event | category | flops | bytes accessed | tf_op | source)
XLA Modules:
  0.0 90.9 jit_solution(4626861549643610338)
XLA Ops:
  0.6 1.0 %copy-done = bf16[2,8,1,128,128]{4,3,2,1,0:T(8,128)(2,1)S(1)} copy-done((bf16[2,8,1,128,128]{4,3,2,1,0:T(8,128)(2,1)S(1)}, bf16[2,8,1,128,128]{4,3,2,1,0:T(8,128)(2,1)}, u32[]{:S(2)}) %copy-start) | copy-done | bytes 524312
  1.7 0.7 copy-done.1
  2.4 0.1 pack.2.refs_0_.refs_1_
  2.4 3.0 %collective-permute-start.8 = (bf16[1296,128]{1,0:T(8,128)(2,1)S(1)}, bf16[1296,128]{1,0:T(8,128)(2,1)S(1)}, u32[]{:S(2)}, u32[]{:S(2)}) collective-permute-start(bf16[1296,128]{1,0:T(8,128)(2,1)S(1)} %pack.2.refs_0_.refs_1_), channel_id=1, source_target_pairs={{8,0},{6,2},{16,8},{2,10},{24,16},{10,18},{28,24},{18,26},{20,28},... | collective-permute-start | bytes 995336 | tf_op jit(solution)/shard_map/ppermute | solution.py:348
  5.4 0.2 collective-permute-start.2
  5.6 8.0 %collective-permute-done.8.refs_5_ = bf16[1296,128]{1,0:T(8,128)(2,1)S(1)} collective-permute-done((bf16[1296,128]{1,0:T(8,128)(2,1)S(1)}, bf16[1296,128]{1,0:T(8,128)(2,1)S(1)}, u32[]{:S(2)}, u32[]{:S(2)}) %collective-permute-start.8) | collective-permute-done | bytes 331808 | tf_op jit(solution)/shard_map/ppermute | solution.py:348
  13.6 1.4 %collective-permute-start.9 = (bf16[1296,128]{1,0:T(8,128)(2,1)S(1)}, bf16[1296,128]{1,0:T(8,128)(2,1)S(1)}, u32[]{:S(2)}, u32[]{:S(2)}) collective-permute-start(bf16[1296,128]{1,0:T(8,128)(2,1)S(1)} %collective-permute-done.8.refs_5_), channel_id=1, source_target_pairs={{8,0},{6,2},{16,8},{2,10},{24,16},{10,18},{28,24},{18,26},{20,28},... | collective-permute-start | bytes 995336 | tf_op jit(solution)/shard_map/ppermute | solution.py:348
  15.1 1.0 %collective-permute-start.3 = (bf16[1296,128]{1,0:T(8,128)(2,1)S(1)}, bf16[1296,128]{1,0:T(8,128)(2,1)S(1)}, u32[]{:S(2)}, u32[]{:S(2)}) collective-permute-start(bf16[1296,128]{1,0:T(8,128)(2,1)S(1)} %collective-permute-done.2.refs_3_), channel_id=1, source_target_pairs={{0,8},{2,6},{8,16},{10,2},{16,24},{18,10},{24,28},{26,18},{28,20},... | collective-permute-start | bytes 995336 | tf_op jit(solution)/shard_map/ppermute | solution.py:345
  16.0 2.0 %collective-permute-start = (bf16[1296,128]{1,0:T(8,128)(2,1)S(1)}, bf16[1296,128]{1,0:T(8,128)(2,1)S(1)}, u32[]{:S(2)}, u32[]{:S(2)}) collective-permute-start(bf16[1296,128]{1,0:T(8,128)(2,1)S(1)} %pack.2.refs_0_.refs_1_), channel_id=1, source_target_pairs={{0,1},{1,0},{2,3},{3,2},{4,5},{5,4},{6,7},{7,6},{8,9},{9,8},{10,11... | collective-permute-start | bytes 995336 | tf_op jit(solution)/shard_map/ppermute | solution.py:296
  18.0 0.1 pack.3.refs_1_
  18.1 0.1 collective-permute-start.1
  18.2 0.0 collective-permute-start.14
  18.3 5.9 %collective-permute-done.9.refs_3_ = bf16[1296,128]{1,0:T(8,128)(2,1)S(1)} collective-permute-done((bf16[1296,128]{1,0:T(8,128)(2,1)S(1)}, bf16[1296,128]{1,0:T(8,128)(2,1)S(1)}, u32[]{:S(2)}, u32[]{:S(2)}) %collective-permute-start.9) | collective-permute-done | bytes 331808 | tf_op jit(solution)/shard_map/ppermute | solution.py:348
  24.1 2.0 %collective-permute-start.4 = (bf16[1296,128]{1,0:T(8,128)(2,1)S(1)}, bf16[1296,128]{1,0:T(8,128)(2,1)S(1)}, u32[]{:S(2)}, u32[]{:S(2)}) collective-permute-start(bf16[1296,128]{1,0:T(8,128)(2,1)S(1)} %collective-permute-done.3.refs_1_), channel_id=1, source_target_pairs={{0,8},{2,6},{8,16},{10,2},{16,24},{18,10},{24,28},{26,18},{28,20},... | collective-permute-start | bytes 995336 | tf_op jit(solution)/shard_map/ppermute | solution.py:345
  26.1 2.2 %collective-permute-done.1.refs_3_ = bf16[784,128]{1,0:T(8,128)(2,1)S(1)} collective-permute-done((bf16[784,128]{1,0:T(8,128)(2,1)S(1)}, bf16[784,128]{1,0:T(8,128)(2,1)S(1)}, u32[]{:S(2)}, u32[]{:S(2)}) %collective-permute-start.1) | collective-permute-done | bytes 200736 | tf_op jit(solution)/shard_map/ppermute | solution.py:296
  28.4 0.5 collective-permute-start.16
  28.9 0.0 collective-permute-done.14.refs_2_
  28.9 0.1 collective-permute-start.10
  28.9 4.5 %collective-permute-done.12.refs_7_ = bf16[1296,128]{1,0:T(8,128)(2,1)S(1)} collective-permute-done((bf16[1296,128]{1,0:T(8,128)(2,1)S(1)}, bf16[1296,128]{1,0:T(8,128)(2,1)S(1)}, u32[]{:S(2)}, u32[]{:S(2)}) %collective-permute-start.12) | collective-permute-done | bytes 331808 | tf_op jit(solution)/shard_map/ppermute | solution.py:348
  33.4 1.4 %collective-permute-start.5 = (bf16[1296,128]{1,0:T(8,128)(2,1)S(1)}, bf16[1296,128]{1,0:T(8,128)(2,1)S(1)}, u32[]{:S(2)}, u32[]{:S(2)}) collective-permute-start(bf16[1296,128]{1,0:T(8,128)(2,1)S(1)} %collective-permute-done.4.refs_5_), channel_id=1, source_target_pairs={{0,8},{2,6},{8,16},{10,2},{16,24},{18,10},{24,28},{26,18},{28,20},... | collective-permute-start | bytes 995336 | tf_op jit(solution)/shard_map/ppermute | solution.py:345
  34.8 1.6 %collective-permute-start.17 = (bf16[784,128]{1,0:T(8,128)(2,1)S(1)}, bf16[784,128]{1,0:T(8,128)(2,1)S(1)}, u32[]{:S(2)}, u32[]{:S(2)}) collective-permute-start(bf16[784,128]{1,0:T(8,128)(2,1)S(1)} %pack.3.refs_1_), channel_id=1, source_target_pairs={{0,8},{2,6},{8,16},{10,2},{16,24},{18,10},{24,28},{26,18},{28,20},... | collective-permute-start | bytes 602120 | tf_op jit(solution)/shard_map/ppermute | solution.py:345
  36.4 0.0 collective-permute-done.16.refs_6_
  36.4 0.4 collective-permute-start.23
  36.9 0.0 collective-permute-done.10.refs_4_
  36.9 0.0 collective-permute-start.29
  36.9 7.6 %collective-permute-done.17.refs_3_ = bf16[784,128]{1,0:T(8,128)(2,1)S(1)} collective-permute-done((bf16[784,128]{1,0:T(8,128)(2,1)S(1)}, bf16[784,128]{1,0:T(8,128)(2,1)S(1)}, u32[]{:S(2)}, u32[]{:S(2)}) %collective-permute-start.17) | collective-permute-done | bytes 200736 | tf_op jit(solution)/shard_map/ppermute | solution.py:345
  44.5 1.7 %collective-permute-start.18 = (bf16[784,128]{1,0:T(8,128)(2,1)S(1)}, bf16[784,128]{1,0:T(8,128)(2,1)S(1)}, u32[]{:S(2)}, u32[]{:S(2)}) collective-permute-start(bf16[784,128]{1,0:T(8,128)(2,1)S(1)} %collective-permute-done.17.refs_3_), channel_id=1, source_target_pairs={{0,8},{2,6},{8,16},{10,2},{16,24},{18,10},{24,28},{26,18},{28,20},... | collective-permute-start | bytes 602120 | tf_op jit(solution)/shard_map/ppermute | solution.py:345
  46.2 0.0 collective-permute-done.7.refs_2_
  46.2 0.5 collective-permute-start.13
  46.7 0.0 collective-permute-done.5.refs_1_
  46.7 0.1 collective-permute-start.6
  46.8 0.0 collective-permute-done.29.refs_2_
  46.8 0.4 collective-permute-start.24
  47.1 3.4 %collective-permute-done.18.refs_1_ = bf16[784,128]{1,0:T(8,128)(2,1)S(1)} collective-permute-done((bf16[784,128]{1,0:T(8,128)(2,1)S(1)}, bf16[784,128]{1,0:T(8,128)(2,1)S(1)}, u32[]{:S(2)}, u32[]{:S(2)}) %collective-permute-start.18) | collective-permute-done | bytes 200736 | tf_op jit(solution)/shard_map/ppermute | solution.py:345
  50.6 1.7 %collective-permute-start.19 = (bf16[784,128]{1,0:T(8,128)(2,1)S(1)}, bf16[784,128]{1,0:T(8,128)(2,1)S(1)}, u32[]{:S(2)}, u32[]{:S(2)}) collective-permute-start(bf16[784,128]{1,0:T(8,128)(2,1)S(1)} %collective-permute-done.18.refs_1_), channel_id=1, source_target_pairs={{0,8},{2,6},{8,16},{10,2},{16,24},{18,10},{24,28},{26,18},{28,20},... | collective-permute-start | bytes 602120 | tf_op jit(solution)/shard_map/ppermute | solution.py:345
  52.3 0.5 collective-permute-start.31
  52.8 0.2 collective-permute-done.24.refs_3_
  53.0 0.4 collective-permute-start.27
  53.4 3.7 %collective-permute-done.19.refs_5_ = bf16[784,128]{1,0:T(8,128)(2,1)S(1)} collective-permute-done((bf16[784,128]{1,0:T(8,128)(2,1)S(1)}, bf16[784,128]{1,0:T(8,128)(2,1)S(1)}, u32[]{:S(2)}, u32[]{:S(2)}) %collective-permute-start.19) | collective-permute-done | bytes 200736 | tf_op jit(solution)/shard_map/ppermute | solution.py:345
  57.1 1.3 %collective-permute-start.20 = (bf16[784,128]{1,0:T(8,128)(2,1)S(1)}, bf16[784,128]{1,0:T(8,128)(2,1)S(1)}, u32[]{:S(2)}, u32[]{:S(2)}) collective-permute-start(bf16[784,128]{1,0:T(8,128)(2,1)S(1)} %collective-permute-done.19.refs_5_), channel_id=1, source_target_pairs={{0,8},{2,6},{8,16},{10,2},{16,24},{18,10},{24,28},{26,18},{28,20},... | collective-permute-start | bytes 602120 | tf_op jit(solution)/shard_map/ppermute | solution.py:345
  58.4 0.7 slice.3
  59.0 0.6 left.1
  59.7 1.3 %square.6 = (f32[256,1280]{1,0:T(8,128)S(1)}, bf16[1536,1280]{1,0:T(8,128)(2,1)S(1)}) custom-call(bf16[256,4096]{1,0:T(8,128)(2,1)S(1)} %get-tuple-element.21.refs_0_, bf16[1296,128]{1,0:T(8,128)(2,1)S(1)} %pack.2.refs_0_.refs_1_, bf16[1296,128]{1,0:T(8,128)(2,1)S(1)} %collective-permute-done.14.refs_2_, ...), custom_call_target="tpu_custom_call" | custom-call | tf_op jit(solution)/shard_map/square/pallas_call | solution.py:352
  60.9 1.8 %square.7 = (f32[256,1280]{1,0:T(8,128)S(1)}, bf16[2048,1280]{1,0:T(8,128)(2,1)S(1)}) custom-call(bf16[256,4096]{1,0:T(8,128)(2,1)S(1)} %get-tuple-element.21.refs_0_, bf16[1296,128]{1,0:T(8,128)(2,1)S(1)} %collective-permute-done.3.refs_1_, bf16[1296,128]{1,0:T(8,128)(2,1)S(1)} %collective-permute-done.7.refs_2_, ...), custom_call_target="tpu_custom_call" | custom-call | tf_op jit(solution)/shard_map/square/pallas_call | solution.py:352
  62.7 0.6 square.8
  63.3 0.0 collective-permute-done.30.refs_4_
  63.3 1.2 %collective-permute-start.32 = (bf16[256,1280]{1,0:T(8,128)(2,1)S(1)}, bf16[256,1280]{1,0:T(8,128)(2,1)S(1)}, u32[]{:S(2)}, u32[]{:S(2)}) collective-permute-start(bf16[256,1280]{1,0:T(8,128)(2,1)S(1)} %get-tuple-element.24.refs_0_), channel_id=1, source_target_pairs={{0,1},{1,0},{2,3},{3,2},{4,5},{5,4},{6,7},{7,6},{8,9},{9,8},{10,11... | collective-permute-start | bytes 1966088 | tf_op jit(solution)/shard_map/ppermute | solution.py:296
  64.5 0.0 collective-permute-done.31.refs_6_
  64.5 0.4 collective-permute-start.25
  64.9 0.1 collective-permute-start.26
  65.0 0.0 collective-permute-done.22.refs_2_
  65.0 0.4 collective-permute-start.28
  65.4 0.1 collective-permute-start.21
  65.5 0.9 square.9
  66.4 0.0 collective-permute-done.25.refs_4_
  66.4 0.0 collective-permute-done.26.refs_6_
  66.4 0.2 collective-permute-done.28.refs_8_
  66.6 1.1 %square.10 = (f32[256,768]{1,0:T(8,128)S(1)}, bf16[2048,768]{1,0:T(8,128)(2,1)S(1)}) custom-call(bf16[256,4096]{1,0:T(8,128)(2,1)S(1)} %get-tuple-element.21.refs_0_, bf16[784,128]{1,0:T(8,128)(2,1)S(1)} %collective-permute-done.18.refs_1_, bf16[784,128]{1,0:T(8,128)(2,1)S(1)} %collective-permute-done.22.refs_2_, ...), custom_call_target="tpu_custom_call" | custom-call | tf_op jit(solution)/shard_map/square/pallas_call | solution.py:352
  67.7 0.4 square.11
  68.1 0.9 collective-permute-start.33
  69.0 11.9 %collective-permute-done.32.refs_2_ = bf16[256,1280]{1,0:T(8,128)(2,1)S(1)} collective-permute-done((bf16[256,1280]{1,0:T(8,128)(2,1)S(1)}, bf16[256,1280]{1,0:T(8,128)(2,1)S(1)}, u32[]{:S(2)}, u32[]{:S(2)}) %collective-permute-start.32) | collective-permute-done | bytes 655392 | tf_op jit(solution)/shard_map/ppermute | solution.py:296
  80.9 6.8 %cube.1 = (f32[256,2048]{1,0:T(8,128)S(1)}, bf16[2,8,2,128,128]{4,3,2,1,0:T(8,128)(2,1)}, bf16[768,2048]{1,0:T(8,128)(2,1)S(1)}) custom-call(f32[16,128]{1,0:T(8,128)S(1)} %get-tuple-element.20.kept, bf16[256,1280]{1,0:T(8,128)(2,1)S(1)} %get-tuple-element.24.refs_0_, bf16[256,768]{1,0:T(8,128)(2,1)S(1)} %get-tuple-element.28.refs_1_, ...), custom_call_target="tpu_custom_call" | custom-call | tf_op jit(solution)/shard_map/cube/pallas_call | solution.py:372
  87.7 1.1 %collective-permute-done.33.refs_2_ = bf16[256,768]{1,0:T(8,128)(2,1)S(1)} collective-permute-done((bf16[256,768]{1,0:T(8,128)(2,1)S(1)}, bf16[256,768]{1,0:T(8,128)(2,1)S(1)}, u32[]{:S(2)}, u32[]{:S(2)}) %collective-permute-start.33) | collective-permute-done | bytes 393248 | tf_op jit(solution)/shard_map/ppermute | solution.py:296
  88.9 2.1 %final.1 = bf16[2,8,2,128,128]{4,3,2,1,0:T(8,128)(2,1)} custom-call(f32[16,128]{1,0:T(8,128)S(1)} %get-tuple-element.20.kept, f32[256,2048]{1,0:T(8,128)S(1)} %get-tuple-element.36.acc, bf16[768,2048]{1,0:T(8,128)(2,1)S(1)} %get-tuple-element.37.later, bf16[256,1280]{1,0:T(8,128)(2,1)S(1)} %get-tuple-element.24.refs_0_, ...), custom_call_target="tpu_custom_call" | custom-call | tf_op jit(solution)/shard_map/final/pallas_call | solution.py:386
  (20 shorter events, 0.1 us)
Async XLA Ops:
  0.6 1.0 %copy-start = (bf16[2,8,1,128,128]{4,3,2,1,0:T(8,128)(2,1)S(1)}, bf16[2,8,1,128,128]{4,3,2,1,0:T(8,128)(2,1)}, u32[]{:S(2)}) copy-start(bf16[2,8,1,128,128]{4,3,2,1,0:T(8,128)(2,1)} %x_ref.3) | copy-start | bytes 1572868
  1.7 0.7 copy-start.1
  2.4 11.2 %collective-permute-start.8 = (bf16[1296,128]{1,0:T(8,128)(2,1)S(1)}, bf16[1296,128]{1,0:T(8,128)(2,1)S(1)}, u32[]{:S(2)}, u32[]{:S(2)}) collective-permute-start(bf16[1296,128]{1,0:T(8,128)(2,1)S(1)} %pack.2.refs_0_.refs_1_), channel_id=1, source_target_pairs={{8,0},{6,2},{16,8},{2,10},{24,16},{10,18},{28,24},{18,26},{20,28},... | collective-permute-start | bytes 995336 | tf_op jit(solution)/shard_map/ppermute | solution.py:348
  5.4 9.6 %collective-permute-start.2 = (bf16[1296,128]{1,0:T(8,128)(2,1)S(1)}, bf16[1296,128]{1,0:T(8,128)(2,1)S(1)}, u32[]{:S(2)}, u32[]{:S(2)}) collective-permute-start(bf16[1296,128]{1,0:T(8,128)(2,1)S(1)} %pack.2.refs_0_.refs_1_), channel_id=1, source_target_pairs={{0,8},{2,6},{8,16},{10,2},{16,24},{18,10},{24,28},{26,18},{28,20},... | collective-permute-start | bytes 995336 | tf_op jit(solution)/shard_map/ppermute | solution.py:345
  13.6 10.5 %collective-permute-start.9 = (bf16[1296,128]{1,0:T(8,128)(2,1)S(1)}, bf16[1296,128]{1,0:T(8,128)(2,1)S(1)}, u32[]{:S(2)}, u32[]{:S(2)}) collective-permute-start(bf16[1296,128]{1,0:T(8,128)(2,1)S(1)} %collective-permute-done.8.refs_5_), channel_id=1, source_target_pairs={{8,0},{6,2},{16,8},{2,10},{24,16},{10,18},{28,24},{18,26},{20,28},... | collective-permute-start | bytes 995336 | tf_op jit(solution)/shard_map/ppermute | solution.py:348
  15.1 9.0 %collective-permute-start.3 = (bf16[1296,128]{1,0:T(8,128)(2,1)S(1)}, bf16[1296,128]{1,0:T(8,128)(2,1)S(1)}, u32[]{:S(2)}, u32[]{:S(2)}) collective-permute-start(bf16[1296,128]{1,0:T(8,128)(2,1)S(1)} %collective-permute-done.2.refs_3_), channel_id=1, source_target_pairs={{0,8},{2,6},{8,16},{10,2},{16,24},{18,10},{24,28},{26,18},{28,20},... | collective-permute-start | bytes 995336 | tf_op jit(solution)/shard_map/ppermute | solution.py:345
  16.0 12.3 %collective-permute-start = (bf16[1296,128]{1,0:T(8,128)(2,1)S(1)}, bf16[1296,128]{1,0:T(8,128)(2,1)S(1)}, u32[]{:S(2)}, u32[]{:S(2)}) collective-permute-start(bf16[1296,128]{1,0:T(8,128)(2,1)S(1)} %pack.2.refs_0_.refs_1_), channel_id=1, source_target_pairs={{0,1},{1,0},{2,3},{3,2},{4,5},{5,4},{6,7},{7,6},{8,9},{9,8},{10,11... | collective-permute-start | bytes 995336 | tf_op jit(solution)/shard_map/ppermute | solution.py:296
  18.1 10.3 %collective-permute-start.1 = (bf16[784,128]{1,0:T(8,128)(2,1)S(1)}, bf16[784,128]{1,0:T(8,128)(2,1)S(1)}, u32[]{:S(2)}, u32[]{:S(2)}) collective-permute-start(bf16[784,128]{1,0:T(8,128)(2,1)S(1)} %pack.3.refs_1_), channel_id=1, source_target_pairs={{0,1},{1,0},{2,3},{3,2},{4,5},{5,4},{6,7},{7,6},{8,9},{9,8},{10,11... | collective-permute-start | bytes 602120 | tf_op jit(solution)/shard_map/ppermute | solution.py:296
  18.2 10.6 %collective-permute-start.14 = (bf16[1296,128]{1,0:T(8,128)(2,1)S(1)}, bf16[1296,128]{1,0:T(8,128)(2,1)S(1)}, u32[]{:S(2)}, u32[]{:S(2)}) collective-permute-start(bf16[1296,128]{1,0:T(8,128)(2,1)S(1)} %pack.2.refs_0_.refs_1_), channel_id=1, source_target_pairs={{0,2},{2,0},{4,6},{6,4},{8,10},{10,8},{12,14},{14,12},{16,18},{18,... | collective-permute-start | bytes 995336 | tf_op jit(solution)/shard_map/ppermute | solution.py:346
  24.1 9.3 %collective-permute-start.12 = (bf16[1296,128]{1,0:T(8,128)(2,1)S(1)}, bf16[1296,128]{1,0:T(8,128)(2,1)S(1)}, u32[]{:S(2)}, u32[]{:S(2)}) collective-permute-start(bf16[1296,128]{1,0:T(8,128)(2,1)S(1)} %collective-permute-done.9.refs_3_), channel_id=1, source_target_pairs={{8,0},{6,2},{16,8},{2,10},{24,16},{10,18},{28,24},{18,26},{20,28},... | collective-permute-start | bytes 995336 | tf_op jit(solution)/shard_map/ppermute | solution.py:348
  24.1 9.3 %collective-permute-start.4 = (bf16[1296,128]{1,0:T(8,128)(2,1)S(1)}, bf16[1296,128]{1,0:T(8,128)(2,1)S(1)}, u32[]{:S(2)}, u32[]{:S(2)}) collective-permute-start(bf16[1296,128]{1,0:T(8,128)(2,1)S(1)} %collective-permute-done.3.refs_1_), channel_id=1, source_target_pairs={{0,8},{2,6},{8,16},{10,2},{16,24},{18,10},{24,28},{26,18},{28,20},... | collective-permute-start | bytes 995336 | tf_op jit(solution)/shard_map/ppermute | solution.py:345
  28.4 6.5 %collective-permute-start.15 = (bf16[1296,128]{1,0:T(8,128)(2,1)S(1)}, bf16[1296,128]{1,0:T(8,128)(2,1)S(1)}, u32[]{:S(2)}, u32[]{:S(2)}) collective-permute-start(bf16[1296,128]{1,0:T(8,128)(2,1)S(1)} %collective-permute-done.2.refs_3_), channel_id=1, source_target_pairs={{0,2},{2,0},{4,6},{6,4},{8,10},{10,8},{12,14},{14,12},{16,18},{18,... | collective-permute-start | bytes 995336 | tf_op jit(solution)/shard_map/ppermute | solution.py:346
  28.4 8.1 %collective-permute-start.16 = (bf16[1296,128]{1,0:T(8,128)(2,1)S(1)}, bf16[1296,128]{1,0:T(8,128)(2,1)S(1)}, u32[]{:S(2)}, u32[]{:S(2)}) collective-permute-start(bf16[1296,128]{1,0:T(8,128)(2,1)S(1)} %collective-permute-done.8.refs_5_), channel_id=1, source_target_pairs={{0,2},{2,0},{4,6},{6,4},{8,10},{10,8},{12,14},{14,12},{16,18},{18,... | collective-permute-start | bytes 995336 | tf_op jit(solution)/shard_map/ppermute | solution.py:349
  28.9 8.0 %collective-permute-start.10 = (bf16[1296,128]{1,0:T(8,128)(2,1)S(1)}, bf16[1296,128]{1,0:T(8,128)(2,1)S(1)}, u32[]{:S(2)}, u32[]{:S(2)}) collective-permute-start(bf16[1296,128]{1,0:T(8,128)(2,1)S(1)} %collective-permute-done.9.refs_3_), channel_id=1, source_target_pairs={{0,2},{2,0},{4,6},{6,4},{8,10},{10,8},{12,14},{14,12},{16,18},{18,... | collective-permute-start | bytes 995336 | tf_op jit(solution)/shard_map/ppermute | solution.py:349
  33.4 12.8 %collective-permute-start.7 = (bf16[1296,128]{1,0:T(8,128)(2,1)S(1)}, bf16[1296,128]{1,0:T(8,128)(2,1)S(1)}, u32[]{:S(2)}, u32[]{:S(2)}) collective-permute-start(bf16[1296,128]{1,0:T(8,128)(2,1)S(1)} %collective-permute-done.3.refs_1_), channel_id=1, source_target_pairs={{0,2},{2,0},{4,6},{6,4},{8,10},{10,8},{12,14},{14,12},{16,18},{18,... | collective-permute-start | bytes 995336 | tf_op jit(solution)/shard_map/ppermute | solution.py:346
  33.4 13.3 %collective-permute-start.5 = (bf16[1296,128]{1,0:T(8,128)(2,1)S(1)}, bf16[1296,128]{1,0:T(8,128)(2,1)S(1)}, u32[]{:S(2)}, u32[]{:S(2)}) collective-permute-start(bf16[1296,128]{1,0:T(8,128)(2,1)S(1)} %collective-permute-done.4.refs_5_), channel_id=1, source_target_pairs={{0,8},{2,6},{8,16},{10,2},{16,24},{18,10},{24,28},{26,18},{28,20},... | collective-permute-start | bytes 995336 | tf_op jit(solution)/shard_map/ppermute | solution.py:345
  34.8 9.7 %collective-permute-start.17 = (bf16[784,128]{1,0:T(8,128)(2,1)S(1)}, bf16[784,128]{1,0:T(8,128)(2,1)S(1)}, u32[]{:S(2)}, u32[]{:S(2)}) collective-permute-start(bf16[784,128]{1,0:T(8,128)(2,1)S(1)} %pack.3.refs_1_), channel_id=1, source_target_pairs={{0,8},{2,6},{8,16},{10,2},{16,24},{18,10},{24,28},{26,18},{28,20},... | collective-permute-start | bytes 602120 | tf_op jit(solution)/shard_map/ppermute | solution.py:345
  36.4 9.8 %collective-permute-start.23 = (bf16[784,128]{1,0:T(8,128)(2,1)S(1)}, bf16[784,128]{1,0:T(8,128)(2,1)S(1)}, u32[]{:S(2)}, u32[]{:S(2)}) collective-permute-start(bf16[784,128]{1,0:T(8,128)(2,1)S(1)} %pack.3.refs_1_), channel_id=1, source_target_pairs={{8,0},{6,2},{16,8},{2,10},{24,16},{10,18},{28,24},{18,26},{20,28},... | collective-permute-start | bytes 602120 | tf_op jit(solution)/shard_map/ppermute | solution.py:348
  36.9 9.9 %collective-permute-start.29 = (bf16[784,128]{1,0:T(8,128)(2,1)S(1)}, bf16[784,128]{1,0:T(8,128)(2,1)S(1)}, u32[]{:S(2)}, u32[]{:S(2)}) collective-permute-start(bf16[784,128]{1,0:T(8,128)(2,1)S(1)} %pack.3.refs_1_), channel_id=1, source_target_pairs={{0,2},{2,0},{4,6},{6,4},{8,10},{10,8},{12,14},{14,12},{16,18},{18,... | collective-permute-start | bytes 602120 | tf_op jit(solution)/shard_map/ppermute | solution.py:346
  44.5 6.1 %collective-permute-start.18 = (bf16[784,128]{1,0:T(8,128)(2,1)S(1)}, bf16[784,128]{1,0:T(8,128)(2,1)S(1)}, u32[]{:S(2)}, u32[]{:S(2)}) collective-permute-start(bf16[784,128]{1,0:T(8,128)(2,1)S(1)} %collective-permute-done.17.refs_3_), channel_id=1, source_target_pairs={{0,8},{2,6},{8,16},{10,2},{16,24},{18,10},{24,28},{26,18},{28,20},... | collective-permute-start | bytes 602120 | tf_op jit(solution)/shard_map/ppermute | solution.py:345
  46.2 6.1 %collective-permute-start.11 = (bf16[1296,128]{1,0:T(8,128)(2,1)S(1)}, bf16[1296,128]{1,0:T(8,128)(2,1)S(1)}, u32[]{:S(2)}, u32[]{:S(2)}) collective-permute-start(bf16[1296,128]{1,0:T(8,128)(2,1)S(1)} %collective-permute-done.4.refs_5_), channel_id=1, source_target_pairs={{0,2},{2,0},{4,6},{6,4},{8,10},{10,8},{12,14},{14,12},{16,18},{18,... | collective-permute-start | bytes 995336 | tf_op jit(solution)/shard_map/ppermute | solution.py:346
  46.2 6.1 %collective-permute-start.13 = (bf16[1296,128]{1,0:T(8,128)(2,1)S(1)}, bf16[1296,128]{1,0:T(8,128)(2,1)S(1)}, u32[]{:S(2)}, u32[]{:S(2)}) collective-permute-start(bf16[1296,128]{1,0:T(8,128)(2,1)S(1)} %collective-permute-done.12.refs_7_), channel_id=1, source_target_pairs={{0,2},{2,0},{4,6},{6,4},{8,10},{10,8},{12,14},{14,12},{16,18},{18,... | collective-permute-start | bytes 995336 | tf_op jit(solution)/shard_map/ppermute | solution.py:349
  46.7 10.4 %collective-permute-start.6 = (bf16[1296,128]{1,0:T(8,128)(2,1)S(1)}, bf16[1296,128]{1,0:T(8,128)(2,1)S(1)}, u32[]{:S(2)}, u32[]{:S(2)}) collective-permute-start(bf16[1296,128]{1,0:T(8,128)(2,1)S(1)} %collective-permute-done.5.refs_1_), channel_id=1, source_target_pairs={{0,2},{2,0},{4,6},{6,4},{8,10},{10,8},{12,14},{14,12},{16,18},{18,... | collective-permute-start | bytes 995336 | tf_op jit(solution)/shard_map/ppermute | solution.py:346
  46.8 6.2 %collective-permute-start.24 = (bf16[784,128]{1,0:T(8,128)(2,1)S(1)}, bf16[784,128]{1,0:T(8,128)(2,1)S(1)}, u32[]{:S(2)}, u32[]{:S(2)}) collective-permute-start(bf16[784,128]{1,0:T(8,128)(2,1)S(1)} %collective-permute-done.23.refs_5_), channel_id=1, source_target_pairs={{8,0},{6,2},{16,8},{2,10},{24,16},{10,18},{28,24},{18,26},{20,28},... | collective-permute-start | bytes 602120 | tf_op jit(solution)/shard_map/ppermute | solution.py:348
  50.6 6.5 %collective-permute-start.19 = (bf16[784,128]{1,0:T(8,128)(2,1)S(1)}, bf16[784,128]{1,0:T(8,128)(2,1)S(1)}, u32[]{:S(2)}, u32[]{:S(2)}) collective-permute-start(bf16[784,128]{1,0:T(8,128)(2,1)S(1)} %collective-permute-done.18.refs_1_), channel_id=1, source_target_pairs={{0,8},{2,6},{8,16},{10,2},{16,24},{18,10},{24,28},{26,18},{28,20},... | collective-permute-start | bytes 602120 | tf_op jit(solution)/shard_map/ppermute | solution.py:345
  52.3 11.0 %collective-permute-start.30 = (bf16[784,128]{1,0:T(8,128)(2,1)S(1)}, bf16[784,128]{1,0:T(8,128)(2,1)S(1)}, u32[]{:S(2)}, u32[]{:S(2)}) collective-permute-start(bf16[784,128]{1,0:T(8,128)(2,1)S(1)} %collective-permute-done.17.refs_3_), channel_id=1, source_target_pairs={{0,2},{2,0},{4,6},{6,4},{8,10},{10,8},{12,14},{14,12},{16,18},{18,... | collective-permute-start | bytes 602120 | tf_op jit(solution)/shard_map/ppermute | solution.py:346
  52.3 12.2 %collective-permute-start.31 = (bf16[784,128]{1,0:T(8,128)(2,1)S(1)}, bf16[784,128]{1,0:T(8,128)(2,1)S(1)}, u32[]{:S(2)}, u32[]{:S(2)}) collective-permute-start(bf16[784,128]{1,0:T(8,128)(2,1)S(1)} %collective-permute-done.23.refs_5_), channel_id=1, source_target_pairs={{0,2},{2,0},{4,6},{6,4},{8,10},{10,8},{12,14},{14,12},{16,18},{18,... | collective-permute-start | bytes 602120 | tf_op jit(solution)/shard_map/ppermute | solution.py:349
  53.0 11.9 %collective-permute-start.27 = (bf16[784,128]{1,0:T(8,128)(2,1)S(1)}, bf16[784,128]{1,0:T(8,128)(2,1)S(1)}, u32[]{:S(2)}, u32[]{:S(2)}) collective-permute-start(bf16[784,128]{1,0:T(8,128)(2,1)S(1)} %collective-permute-done.24.refs_3_), channel_id=1, source_target_pairs={{8,0},{6,2},{16,8},{2,10},{24,16},{10,18},{28,24},{18,26},{20,28},... | collective-permute-start | bytes 602120 | tf_op jit(solution)/shard_map/ppermute | solution.py:348
  57.1 8.0 %collective-permute-start.22 = (bf16[784,128]{1,0:T(8,128)(2,1)S(1)}, bf16[784,128]{1,0:T(8,128)(2,1)S(1)}, u32[]{:S(2)}, u32[]{:S(2)}) collective-permute-start(bf16[784,128]{1,0:T(8,128)(2,1)S(1)} %collective-permute-done.18.refs_1_), channel_id=1, source_target_pairs={{0,2},{2,0},{4,6},{6,4},{8,10},{10,8},{12,14},{14,12},{16,18},{18,... | collective-permute-start | bytes 602120 | tf_op jit(solution)/shard_map/ppermute | solution.py:346
  57.1 8.3 %collective-permute-start.20 = (bf16[784,128]{1,0:T(8,128)(2,1)S(1)}, bf16[784,128]{1,0:T(8,128)(2,1)S(1)}, u32[]{:S(2)}, u32[]{:S(2)}) collective-permute-start(bf16[784,128]{1,0:T(8,128)(2,1)S(1)} %collective-permute-done.19.refs_5_), channel_id=1, source_target_pairs={{0,8},{2,6},{8,16},{10,2},{16,24},{18,10},{24,28},{26,18},{28,20},... | collective-permute-start | bytes 602120 | tf_op jit(solution)/shard_map/ppermute | solution.py:345
  63.3 17.6 %collective-permute-start.32 = (bf16[256,1280]{1,0:T(8,128)(2,1)S(1)}, bf16[256,1280]{1,0:T(8,128)(2,1)S(1)}, u32[]{:S(2)}, u32[]{:S(2)}) collective-permute-start(bf16[256,1280]{1,0:T(8,128)(2,1)S(1)} %get-tuple-element.24.refs_0_), channel_id=1, source_target_pairs={{0,1},{1,0},{2,3},{3,2},{4,5},{5,4},{6,7},{7,6},{8,9},{9,8},{10,11... | collective-permute-start | bytes 1966088 | tf_op jit(solution)/shard_map/ppermute | solution.py:296
  64.5 1.9 %collective-permute-start.25 = (bf16[784,128]{1,0:T(8,128)(2,1)S(1)}, bf16[784,128]{1,0:T(8,128)(2,1)S(1)}, u32[]{:S(2)}, u32[]{:S(2)}) collective-permute-start(bf16[784,128]{1,0:T(8,128)(2,1)S(1)} %collective-permute-done.24.refs_3_), channel_id=1, source_target_pairs={{0,2},{2,0},{4,6},{6,4},{8,10},{10,8},{12,14},{14,12},{16,18},{18,... | collective-permute-start | bytes 602120 | tf_op jit(solution)/shard_map/ppermute | solution.py:349
  64.9 1.5 %collective-permute-start.26 = (bf16[784,128]{1,0:T(8,128)(2,1)S(1)}, bf16[784,128]{1,0:T(8,128)(2,1)S(1)}, u32[]{:S(2)}, u32[]{:S(2)}) collective-permute-start(bf16[784,128]{1,0:T(8,128)(2,1)S(1)} %collective-permute-done.19.refs_5_), channel_id=1, source_target_pairs={{0,2},{2,0},{4,6},{6,4},{8,10},{10,8},{12,14},{14,12},{16,18},{18,... | collective-permute-start | bytes 602120 | tf_op jit(solution)/shard_map/ppermute | solution.py:346
  65.0 1.6 %collective-permute-start.28 = (bf16[784,128]{1,0:T(8,128)(2,1)S(1)}, bf16[784,128]{1,0:T(8,128)(2,1)S(1)}, u32[]{:S(2)}, u32[]{:S(2)}) collective-permute-start(bf16[784,128]{1,0:T(8,128)(2,1)S(1)} %collective-permute-done.27.refs_7_), channel_id=1, source_target_pairs={{0,2},{2,0},{4,6},{6,4},{8,10},{10,8},{12,14},{14,12},{16,18},{18,... | collective-permute-start | bytes 602120 | tf_op jit(solution)/shard_map/ppermute | solution.py:349
  65.4 2.3 %collective-permute-start.21 = (bf16[784,128]{1,0:T(8,128)(2,1)S(1)}, bf16[784,128]{1,0:T(8,128)(2,1)S(1)}, u32[]{:S(2)}, u32[]{:S(2)}) collective-permute-start(bf16[784,128]{1,0:T(8,128)(2,1)S(1)} %collective-permute-done.20.refs_1_), channel_id=1, source_target_pairs={{0,2},{2,0},{4,6},{6,4},{8,10},{10,8},{12,14},{14,12},{16,18},{18,... | collective-permute-start | bytes 602120 | tf_op jit(solution)/shard_map/ppermute | solution.py:346
  68.1 20.7 %collective-permute-start.33 = (bf16[256,768]{1,0:T(8,128)(2,1)S(1)}, bf16[256,768]{1,0:T(8,128)(2,1)S(1)}, u32[]{:S(2)}, u32[]{:S(2)}) collective-permute-start(bf16[256,768]{1,0:T(8,128)(2,1)S(1)} %get-tuple-element.28.refs_1_), channel_id=1, source_target_pairs={{0,1},{1,0},{2,3},{3,2},{4,5},{5,4},{6,7},{7,6},{8,9},{9,8},{10,11... | collective-permute-start | bytes 1179656 | tf_op jit(solution)/shard_map/ppermute | solution.py:296

commit v3 on v2

v3 whole, which is shorter than its diff:
```python
import functools

import jax
import jax.numpy as jnp
from jax import lax
from jax.experimental import pallas as pl
from jax.experimental.pallas import tpu as pltpu
from jax.sharding import PartitionSpec as P

CORES = 2
FLAG_ROWS = 16


def chunk_sizes(panels):
    last = max(1, panels // 2)
    return (panels - last, last)


def part_sizes(sizes):
    return sizes


def hop_groups(chips, chunk):
    last = chips // 2
    return (tuple(range(last - 1)), (last - 1, last))


def spans_of(chips, chunk):
    spans, start = [], 0
    for group in hop_groups(chips, chunk):
        count = sum(1 if hop == 0 or 2 * hop == chips else 2 for hop in group)
        spans.append((start, count))
        start += count
    return spans


def ring_chip(position, chips):
    up = 2 * position
    down = 2 * (chips - 1 - position) + 1
    if isinstance(position, int):
        return up if position < chips // 2 else down
    return jnp.where(position < chips // 2, up, down)


def ring_place(chip, chips):
    return jnp.where(chip % 2 == 0, chip // 2, chips - 1 - chip // 2)


def ring_pairs(rows):
    chips = rows // CORES
    pairs = []
    for position in range(chips):
        for core in range(CORES):
            step = 1 if core == 0 else -1
            source = ring_chip(position, chips) * CORES + core
            target = ring_chip((position + step) % chips, chips) * CORES + core
            pairs.append((source, target))
    return pairs


def slot_of(slab, row, rows):
    chips = rows // CORES
    core = row % CORES
    other = jnp.where(slab % CORES == core, 0, 1)
    step = (1 - 2 * core) * (2 * other - 1)
    distance = (ring_place(slab // CORES, chips) - ring_place(row // CORES, chips)) * step
    hop = lax.rem(distance + chips, chips)
    near = 2 * hop - 1
    far = 2 * (chips - hop)
    place = jnp.where(hop == 0, 0, jnp.where(hop <= chips // 2, near, far))
    return place + chips * other


def slab_of(slot, row, rows):
    chips = rows // CORES
    core = row % CORES
    other, place = slot // chips, slot % chips
    hop = (place + 1) // 2
    if place > 0 and place % 2 == 0:
        hop = chips - hop
    step = (1 - 2 * core) * (2 * other - 1)
    position = lax.rem(ring_place(row // CORES, chips) + step * hop + chips, chips)
    return ring_chip(position, chips) * CORES + (1 - core if other else core)


def lane_flags(values, rows, size, first, lanes):
    width, panels = values.shape
    row = lax.broadcasted_iota(jnp.int32, (rows, panels), 0)
    lane = lax.broadcasted_iota(jnp.int32, (rows, panels), 1)
    total = jnp.zeros((rows, 1), jnp.int32)
    for local in range(width):
        start = local * size
        here = (row >= start) & (row < start + size) & (lane == first + row - start)
        picked = jnp.where(here, jnp.broadcast_to(values[local : local + 1, :], here.shape), 0)
        total += jnp.sum(picked, axis=1, keepdims=True)
    return jnp.broadcast_to(total.astype(jnp.float32), (rows, lanes))


def pack_kernel(sizes, tile, cols_ref, x_ref, *refs):
    outs, (cols, copied, sems) = refs[:-3], refs[-3:]
    width = x_ref.shape[0]
    columns = pltpu.make_async_copy(cols_ref, cols, copied)
    columns.start()
    copies = []
    first = 0
    for size, out in zip(sizes, outs):
        for local in range(width):
            copy = pltpu.make_async_copy(
                x_ref.at[local, pl.ds(first * tile, size * tile), :],
                out.at[pl.ds(local * size * tile, size * tile), :],
                sems.at[len(copies)],
            )
            copy.start()
            copies.append(copy)
        first += size
    columns.wait()
    first = 0
    for size, out in zip(sizes, outs):
        base = width * size * tile
        flags = lane_flags(cols[...], FLAG_ROWS, size, first, tile)
        out[base : base + FLAG_ROWS, :] = flags.astype(jnp.bfloat16)
        first += size
    for copy in copies:
        copy.wait()


def halves(payload, flags, index, tile):
    block = payload[index * tile : (index + 1) * tile, :]
    right = block * flags[index : index + 1, :]
    return block - right, right


def left_kernel(sizes, rows, groups, width, tile, keep_ref, *refs):
    out, kept = refs[-2:]
    dense = width * tile
    row, mine = lax.axis_index("row"), lax.axis_index("col")
    panels = sum(sizes)
    index = 0
    for shift in range(groups):
        group = lax.rem(mine - shift + groups, groups)
        first = 0
        for size in sizes:
            payload = refs[index]
            index += 1
            base = width * size * tile
            flags = payload[base : base + FLAG_ROWS, :]
            for panel in range(size):
                slot = slot_of(group * panels + first + panel, row, rows)
                start = pl.multiple_of(slot * dense, dense)
                for local in range(width):
                    left, right = halves(payload, flags, local * size + panel, tile)
                    part = slice(local * tile, (local + 1) * tile)
                    out[part, pl.ds(start, tile)] = left
                    out[part, pl.ds(start + tile, tile)] = right
            first += size
    keep = keep_ref[...]
    firsts = jnp.concatenate(
        [keep[local * 2 : local * 2 + 1, :] for local in range(width)], axis=0
    )
    kept[...] = lane_flags(firsts, kept.shape[0], panels, 0, tile)


def square_kernel(size, width, tile, own, pieces, spans, more, parts, *refs):
    refs = list(refs)
    left_ref = refs.pop(0)
    dense = width * tile
    right = refs.pop() if pieces else None
    outs = [refs.pop() for _ in parts][::-1]
    products = []
    if pieces:
        for index in range(pieces):
            piece = refs.pop(0)
            base = width * size * tile
            flags = piece[base : base + FLAG_ROWS, :]
            for local in range(width):
                part = slice(index * dense + local * tile, index * dense + (local + 1) * tile)
                for panel in range(size):
                    a, b = halves(piece, flags, local * size + panel, tile)
                    column = panel * dense
                    right[part, column : column + tile] = a
                    right[part, column + tile : column + 2 * tile] = b
        products.append((own, pieces, right))
    for start, count in spans:
        products.append((start, count, refs.pop(0)))
    total = refs.pop(0)[...] if more else None
    for start, count, other in products:
        product = jnp.dot(
            left_ref[:, start * dense : (start + count) * dense],
            other[...],
            preferred_element_type=jnp.float32,
        )
        total = product if total is None else total + product
    first = 0
    for count, out in zip(parts, outs):
        out[...] = total[:, first * dense : (first + count) * dense].astype(out.dtype)
        first += count


def cube_kernel(sizes, parts, rows, groups, width, tile, spans, kept, *refs):
    dense = width * tile
    panels = sum(sizes)
    early = len(parts) - 1
    own = refs[: len(parts)]
    received = refs[len(parts) : len(parts) + (groups - 1) * early]
    flat = list(refs[len(parts) + (groups - 1) * early : -4])
    rights = [[flat.pop(0) for _ in span] for span in spans]
    acc, square, later, squares = refs[-4:]
    row, mine = lax.axis_index("row"), lax.axis_index("col")

    index = 0
    for shift in range(groups):
        group = lax.rem(mine - shift + groups, groups)
        first = 0
        for part, size in enumerate(parts):
            source = None
            if shift == 0:
                source = own[part]
            elif part < early:
                source = received[index]
                index += 1
            for panel in range(size):
                slot = slot_of(group * panels + first + panel, row, rows)
                where = pl.ds(pl.multiple_of(slot * dense, dense), dense)
                if source is None:
                    squares[:, where] = jnp.zeros((dense, dense), squares.dtype)
                else:
                    squares[:, where] = source[:, panel * dense : (panel + 1) * dense]
            first += size

    column = 0
    for chunk, size in enumerate(sizes):
        total = None
        for (start, count), right in zip(spans[chunk], rights[chunk]):
            product = jnp.dot(
                squares[:, start * dense : (start + count) * dense],
                right[...],
                preferred_element_type=jnp.float32,
            )
            total = product if total is None else total + product
        acc[:, column : column + size * dense] = total
        column += size * dense

    last = parts[-1]
    for position in range(rows):
        slab = slab_of(position, row, rows)
        group, panel = slab // panels, lax.rem(slab, panels)
        shift = lax.rem(mine - group + groups, groups)

        @pl.when((shift > 0) & (panel >= panels - last))
        def _(position=position, shift=shift, panel=panel):
            where = (shift - 1) * last + panel - (panels - last)
            target = pl.ds(pl.multiple_of(where * dense, dense), dense)
            column = 0
            for chunk, size in enumerate(sizes):
                for (start, count), right in zip(spans[chunk], rights[chunk]):
                    if start <= position < start + count:
                        place = (position - start) * dense
                        later[target, column : column + size * dense] = right[
                            place : place + dense, :
                        ]
                column += size * dense

    first = 0
    for size, source in zip(parts, own):
        for panel in range(size):
            for local in range(width):
                part = slice(local * tile, (local + 1) * tile)
                column = panel * dense
                a, b = ordered(
                    kept,
                    local * panels + first + panel,
                    source[part, column : column + dense].astype(jnp.float32),
                    tile,
                )
                square[local, first + panel, 0] = a.astype(square.dtype)
                square[local, first + panel, 1] = b.astype(square.dtype)
        first += size


def ordered(kept, index, value, tile):
    left, right = value[:, :tile], value[:, tile:]
    swap = jnp.broadcast_to(kept[index : index + 1, :] > 0.5, left.shape)
    return jnp.where(swap, right, left), jnp.where(swap, left, right)


def final_kernel(parts, groups, width, tile, kept, acc, later, *refs):
    own = refs[: len(parts)]
    received = refs[len(parts) : len(parts) + groups - 1]
    purified = refs[-1]
    dense = width * tile
    panels = sum(parts)
    span = parts[-1] * dense
    first = 0
    for size, source in zip(parts, own):
        columns = slice(first * dense, (first + size) * dense)
        total = acc[:, columns]
        for shift in range(groups - 1):
            total += jnp.dot(
                received[shift][...],
                later[shift * span : (shift + 1) * span, columns],
                preferred_element_type=jnp.float32,
            )
        value = 3.0 * source[...].astype(jnp.float32) - 2.0 * total
        for panel in range(size):
            for local in range(width):
                part = value[
                    local * tile : (local + 1) * tile, panel * dense : (panel + 1) * dense
                ]
                a, b = ordered(kept, local * panels + first + panel, part, tile)
                purified[local, first + panel, 0] = a.astype(purified.dtype)
                purified[local, first + panel, 1] = b.astype(purified.dtype)
        first += size


def vmem(count):
    return [pl.BlockSpec(memory_space=pltpu.VMEM)] * count


def anywhere(count):
    return [pl.BlockSpec(memory_space=pl.ANY)] * count


def after(value, *others):
    return lax.optimization_barrier((value,) + others)[0] if others else value


def params(mib):
    return pltpu.CompilerParams(vmem_limit_bytes=mib * 1024 * 1024)


def shards(rows, groups, x_tiles, x_cols, keep_cols):
    width, panels, tile = x_tiles.shape[0], x_tiles.shape[1], x_tiles.shape[-1]
    dense = width * tile
    sizes = chunk_sizes(panels)
    parts = part_sizes(sizes)
    chips = rows // CORES
    hops = chips // 2
    forward = ring_pairs(rows)
    backward = [(target, source) for source, target in forward]
    sibling = [(device, device ^ 1) for device in range(rows)]
    bf16, f32 = jnp.bfloat16, jnp.float32

    def across(value, shift):
        pairs = [(group, (group + shift) % groups) for group in range(groups)]
        return lax.ppermute(value, "col", pairs)

    payloads = pl.pallas_call(
        functools.partial(pack_kernel, sizes, tile),
        out_shape=[
            jax.ShapeDtypeStruct((width * size * tile + FLAG_ROWS, tile), bf16) for size in sizes
        ],
        in_specs=anywhere(2),
        out_specs=vmem(len(sizes)),
        scratch_shapes=[
            pltpu.VMEM((width, panels), jnp.int32),
            pltpu.SemaphoreType.DMA,
            pltpu.SemaphoreType.DMA((width * len(sizes),)),
        ],
        compiler_params=params(4),
        name="pack",
    )(x_cols.reshape(width, panels), x_tiles.reshape(width, panels * tile, tile))

    lefts = list(payloads)
    for shift in range(1, groups):
        lefts += [across(payload, shift) for payload in payloads]
    kept_rows = -(-width * panels // 8) * 8
    left, kept = pl.pallas_call(
        functools.partial(left_kernel, sizes, rows, groups, width, tile),
        out_shape=[
            jax.ShapeDtypeStruct((dense, rows * dense), bf16),
            jax.ShapeDtypeStruct((kept_rows, tile), f32),
        ],
        in_specs=vmem(1 + len(lefts)),
        out_specs=vmem(2),
        compiler_params=params(4),
        name="left",
    )(jnp.transpose(keep_cols, (0, 2, 1)).reshape(width * 2, panels), *lefts)

    def square_of(size, own, pieces, swapped, total, outs):
        operands = [left] + pieces + [value for _, value in swapped]
        operands += [] if total is None else [total]
        done = len(outs) > 1 or not pieces
        shapes = [jax.ShapeDtypeStruct((dense, n * dense), bf16 if done else f32) for n in outs]
        if pieces:
            shapes.append(jax.ShapeDtypeStruct((len(pieces) * dense, size * dense), bf16))
        return pl.pallas_call(
            functools.partial(
                square_kernel,
                size,
                width,
                tile,
                own,
                len(pieces),
                [span for span, _ in swapped],
                total is not None,
                outs,
            ),
            out_shape=shapes,
            in_specs=vmem(len(operands)),
            out_specs=vmem(len(shapes)),
            compiler_params=params(4),
            name="square",
        )(*operands)

    both_spans, rights, squares, received = [], [], [], []
    for chunk, payload in enumerate(payloads):
        size = sizes[chunk]
        counts = {True: hops - chunk, False: hops - 1 + chunk}
        moved = {True: [payload], False: [payload]}
        for hop in range(1, hops + 1):
            for ahead in (True, False):
                if hop <= counts[ahead]:
                    pairs = forward if ahead else backward
                    moved[ahead].append(lax.ppermute(moved[ahead][-1], "row", pairs))
        spans = spans_of(chips, chunk)
        sib_spans = [(start + chips, count) for start, count in spans]
        own_rights, sib_rights = [], []
        total, swapped = None, []
        for part, group in enumerate(hop_groups(chips, chunk)):
            pieces = []
            for hop in group:
                if hop == 0:
                    pieces.append(payload)
                    continue
                pieces += [moved[key][hop] for key in (True, False) if hop < len(moved[key])]
            total, right = square_of(size, spans[part][0], pieces, swapped, total, [size])
            own_rights.append(right)
            sib_rights.append(lax.ppermute(right, "row", sibling))
            swapped = [(sib_spans[part], sib_rights[-1])]
        (square,) = square_of(size, None, [], swapped, total, [size])
        rights.append(own_rights + sib_rights)
        both_spans.append(spans + sib_spans)
        squares.append(square)
        received.append([across(square, shift) for shift in range(1, groups)])

    dense_rights = [right for some in rights for right in some]
    already = [part[shift] for shift in range(groups - 1) for part in received[:-1]]
    later_rows = (groups - 1) * parts[-1] * dense
    acc, square_out, later = pl.pallas_call(
        functools.partial(cube_kernel, sizes, parts, rows, groups, width, tile, both_spans),
        out_shape=[
            jax.ShapeDtypeStruct((dense, panels * dense), f32),
            jax.ShapeDtypeStruct((width, panels, 2, tile, tile), bf16),
            jax.ShapeDtypeStruct((later_rows, panels * dense), bf16),
        ],
        in_specs=vmem(1 + len(squares) + len(already) + len(dense_rights)),
        out_specs=vmem(3),
        scratch_shapes=[pltpu.VMEM((dense, rows * dense), bf16)],
        compiler_params=params(8),
        name="cube",
    )(kept, *squares, *already, *dense_rights)

    purified = pl.pallas_call(
        functools.partial(final_kernel, parts, groups, width, tile),
        out_shape=jax.ShapeDtypeStruct((width, panels, 2, tile, tile), bf16),
        in_specs=vmem(3 + len(squares) + groups - 1),
        out_specs=vmem(1)[0],
        compiler_params=params(8),
        name="final",
    )(kept, acc, later, *squares, *received[-1])
    return (square_out, purified)


def solution(mesh):
    in_specs = (P("row", "col", None, None, None), P("row", "col", None), P("row", "col", None))
    out_specs = (P("row", "col", None, None, None), P("row", "col", None, None, None))
    body = functools.partial(shards, mesh.shape["row"], mesh.shape["col"])
    return jax.shard_map(body, mesh=mesh, in_specs=in_specs, out_specs=out_specs, check_vma=False)
```

time: 91.8 us -> 83.3 us (0.907)
  waiting for transfers between devices: 48.8 us -> 37.6 us
  starting transfers between devices: 23.4 us -> 26.3 us
    ppermute x30 -> x18, waiting for transfers between devices: 33.5 us -> 23.9 us  [the longest x14 23.4 us: shards(): moved[ahead].append(lax.ppermute(moved[ahead][-1], 'row', pairs))]
    ppermute x4, starting transfers between devices: 4.16 us -> 8.94 us  [across(): return lax.ppermute(value, 'col', pairs)]
    ppermute x30 -> x18, starting transfers between devices: 19.2 us -> 17.3 us  [the longest x14 16.9 us: shards(): moved[ahead].append(lax.ppermute(moved[ahead][-1], 'row', pairs))]
    ppermute x4, waiting for transfers between devices: 15.2 us -> 13.7 us  [across(): return lax.ppermute(value, 'col', pairs)]
    unnamed x4 -> x6, local copies, waits for them, and re-layouts: 1.71 us -> 2.4 us
    pallas_call x10 -> x9, Pallas kernels: 15 us -> 15.5 us  [the longest x1 6.7 us: shards(): pl.pallas_call(functools.partial(cube_kernel, sizes, parts, rows, groups,...]
  transfers between devices with their start and end apart: 34 -> 22, of which waited for: 11 -> 13; matrix products, arithmetic and copies ran while one was open for 1% -> 0% of each run, Pallas kernels for 15% -> 16%
where the time goes in v3:
time: 83.3 us; the launch traced here: 83.1 us
  waiting for transfers between devices  37.6 us (45%)
  starting transfers between devices  26.3 us (32%)
  Pallas kernels  16.1 us (19%)
  local copies, waits for them, and re-layouts  2.4 us (3%)
    ppermute x14, waiting for transfers between devices, shards(): moved[ahead].append(lax.ppermute(moved[ahead][-1], 'row', pairs))  23.4 us
    ppermute x14, starting transfers between devices, shards(): moved[ahead].append(lax.ppermute(moved[ahead][-1], 'row', pairs))  16.9 us
    ppermute x4, waiting for transfers between devices, across(): return lax.ppermute(value, 'col', pairs)  13.7 us
    ppermute x4, starting transfers between devices, across(): return lax.ppermute(value, 'col', pairs)  8.94 us
    pallas_call x1, Pallas kernels, shards(): pl.pallas_call(functools.partial(cube_kernel, sizes, parts, rows, groups,...  6.7 us
    pallas_call x6, Pallas kernels, square_of(): pl.pallas_call(functools.partial(square_kernel, size, width, tile, own, l...  5.63 us
    unnamed x6, local copies, waits for them, and re-layouts  2.4 us
    pallas_call x1, Pallas kernels, shards(): pl.pallas_call(functools.partial(final_kernel, parts, groups, width, tile...  2.36 us
  transfers between devices with their start and end apart: 22, of which 13 were waited for; matrix products, arithmetic and copies ran while one was open for 0% of the time, Pallas kernels for 16%

profile of v3, /device:TPU:0, one launch (start us, length us, event | category | flops | bytes accessed | tf_op | source)
XLA Modules:
  0.0 83.1 jit_solution(5698482357476516015)
XLA Ops:
  0.6 0.0 copy-start
  0.6 1.0 %copy-done = bf16[2,8,1,128,128]{4,3,2,1,0:T(8,128)(2,1)S(1)} copy-done((bf16[2,8,1,128,128]{4,3,2,1,0:T(8,128)(2,1)S(1)}, bf16[2,8,1,128,128]{4,3,2,1,0:T(8,128)(2,1)}, u32[]{:S(2)}) %copy-start) | copy-done | bytes 524312
  1.7 0.0 copy-start.2
  1.7 0.7 copy-done.2
  2.4 0.8 pack.1
  3.2 3.0 %collective-permute-start.5 = (bf16[1040,128]{1,0:T(8,128)(2,1)S(1)}, bf16[1040,128]{1,0:T(8,128)(2,1)S(1)}, u32[]{:S(2)}, u32[]{:S(2)}) collective-permute-start(bf16[1040,128]{1,0:T(8,128)(2,1)S(1)} %get-tuple-element.17.refs_0_.refs_1_), channel_id=1, source_target_pairs={{8,0},{6,2},{16,8},{2,10},{24,16},{10,18},{28,24},{18,26},{20,28},... | collective-permute-start | bytes 798728 | tf_op jit(solution)/shard_map/ppermute | solution.py:414
  6.2 0.2 collective-permute-start.2
  6.3 1.9 %collective-permute-start = (bf16[1040,128]{1,0:T(8,128)(2,1)S(1)}, bf16[1040,128]{1,0:T(8,128)(2,1)S(1)}, u32[]{:S(2)}, u32[]{:S(2)}) collective-permute-start(bf16[1040,128]{1,0:T(8,128)(2,1)S(1)} %get-tuple-element.17.refs_0_.refs_1_), channel_id=1, source_target_pairs={{0,1},{1,0},{2,3},{3,2},{4,5},{5,4},{6,7},{7,6},{8,9},{9,8},{10,11... | collective-permute-start | bytes 798728 | tf_op jit(solution)/shard_map/ppermute | solution.py:345
  8.2 1.5 %collective-permute-start.14 = (bf16[1040,128]{1,0:T(8,128)(2,1)S(1)}, bf16[1040,128]{1,0:T(8,128)(2,1)S(1)}, u32[]{:S(2)}, u32[]{:S(2)}) collective-permute-start(bf16[1040,128]{1,0:T(8,128)(2,1)S(1)} %get-tuple-element.18.refs_1_), channel_id=1, source_target_pairs={{8,0},{6,2},{16,8},{2,10},{24,16},{10,18},{28,24},{18,26},{20,28},... | collective-permute-start | bytes 798728 | tf_op jit(solution)/shard_map/ppermute | solution.py:414
  9.7 0.5 collective-permute-start.11
  10.2 2.7 %collective-permute-done.5.refs_3_ = bf16[1040,128]{1,0:T(8,128)(2,1)S(1)} collective-permute-done((bf16[1040,128]{1,0:T(8,128)(2,1)S(1)}, bf16[1040,128]{1,0:T(8,128)(2,1)S(1)}, u32[]{:S(2)}, u32[]{:S(2)}) %collective-permute-start.5) | collective-permute-done | bytes 266272 | tf_op jit(solution)/shard_map/ppermute | solution.py:414
  12.9 2.3 %collective-permute-start.1 = (bf16[1040,128]{1,0:T(8,128)(2,1)S(1)}, bf16[1040,128]{1,0:T(8,128)(2,1)S(1)}, u32[]{:S(2)}, u32[]{:S(2)}) collective-permute-start(bf16[1040,128]{1,0:T(8,128)(2,1)S(1)} %get-tuple-element.18.refs_1_), channel_id=1, source_target_pairs={{0,1},{1,0},{2,3},{3,2},{4,5},{5,4},{6,7},{7,6},{8,9},{9,8},{10,11... | collective-permute-start | bytes 798728 | tf_op jit(solution)/shard_map/ppermute | solution.py:345
  15.3 0.1 collective-permute-done.2.refs_2_
  15.3 1.7 %collective-permute-start.6 = (bf16[1040,128]{1,0:T(8,128)(2,1)S(1)}, bf16[1040,128]{1,0:T(8,128)(2,1)S(1)}, u32[]{:S(2)}, u32[]{:S(2)}) collective-permute-start(bf16[1040,128]{1,0:T(8,128)(2,1)S(1)} %collective-permute-done.5.refs_3_), channel_id=1, source_target_pairs={{8,0},{6,2},{16,8},{2,10},{24,16},{10,18},{28,24},{18,26},{20,28},... | collective-permute-start | bytes 798728 | tf_op jit(solution)/shard_map/ppermute | solution.py:414
  17.1 0.0 collective-permute-done.refs_2_
  17.1 0.3 collective-permute-start.3
  17.4 1.3 %collective-permute-done.14.refs_3_ = bf16[1040,128]{1,0:T(8,128)(2,1)S(1)} collective-permute-done((bf16[1040,128]{1,0:T(8,128)(2,1)S(1)}, bf16[1040,128]{1,0:T(8,128)(2,1)S(1)}, u32[]{:S(2)}, u32[]{:S(2)}) %collective-permute-start.14) | collective-permute-done | bytes 266272 | tf_op jit(solution)/shard_map/ppermute | solution.py:414
  18.6 2.5 %collective-permute-start.15 = (bf16[1040,128]{1,0:T(8,128)(2,1)S(1)}, bf16[1040,128]{1,0:T(8,128)(2,1)S(1)}, u32[]{:S(2)}, u32[]{:S(2)}) collective-permute-start(bf16[1040,128]{1,0:T(8,128)(2,1)S(1)} %collective-permute-done.14.refs_3_), channel_id=1, source_target_pairs={{8,0},{6,2},{16,8},{2,10},{24,16},{10,18},{28,24},{18,26},{20,28},... | collective-permute-start | bytes 798728 | tf_op jit(solution)/shard_map/ppermute | solution.py:414
  21.1 0.0 collective-permute-done.11.refs_2_
  21.1 0.2 collective-permute-start.12
  21.3 0.0 collective-permute-done.1.refs_3_
  21.3 0.0 copy-start.1
  21.3 0.7 copy-done.1
  22.0 0.6 left.1
  22.6 2.1 %collective-permute-done.6.refs_5_ = bf16[1040,128]{1,0:T(8,128)(2,1)S(1)} collective-permute-done((bf16[1040,128]{1,0:T(8,128)(2,1)S(1)}, bf16[1040,128]{1,0:T(8,128)(2,1)S(1)}, u32[]{:S(2)}, u32[]{:S(2)}) %collective-permute-start.6) | collective-permute-done | bytes 266272 | tf_op jit(solution)/shard_map/ppermute | solution.py:414
  24.7 1.7 %collective-permute-done.3.refs_4_ = bf16[1040,128]{1,0:T(8,128)(2,1)S(1)} collective-permute-done((bf16[1040,128]{1,0:T(8,128)(2,1)S(1)}, bf16[1040,128]{1,0:T(8,128)(2,1)S(1)}, u32[]{:S(2)}, u32[]{:S(2)}) %collective-permute-start.3) | collective-permute-done | bytes 266272 | tf_op jit(solution)/shard_map/ppermute | solution.py:414
  26.4 0.9 %square.6 = (f32[256,1024]{1,0:T(8,128)S(1)}, bf16[1280,1024]{1,0:T(8,128)(2,1)S(1)}) custom-call(bf16[256,4096]{1,0:T(8,128)(2,1)S(1)} %get-tuple-element.20.refs_0_, bf16[1040,128]{1,0:T(8,128)(2,1)S(1)} %get-tuple-element.17.refs_0_.refs_1_, bf16[1040,128]{1,0:T(8,128)(2,1)S(1)} %collective-permute-done.2.refs_2_, ...), custom_call_target="tpu_custom_call" | custom-call | tf_op jit(solution)/shard_map/square/pallas_call | solution.py:386
  27.3 0.1 collective-permute-start.9
  27.4 3.0 %collective-permute-done.15.refs_5_ = bf16[1040,128]{1,0:T(8,128)(2,1)S(1)} collective-permute-done((bf16[1040,128]{1,0:T(8,128)(2,1)S(1)}, bf16[1040,128]{1,0:T(8,128)(2,1)S(1)}, u32[]{:S(2)}, u32[]{:S(2)}) %collective-permute-start.15) | collective-permute-done | bytes 266272 | tf_op jit(solution)/shard_map/ppermute | solution.py:414
  30.4 0.0 collective-permute-done.12.refs_4_
  30.4 0.9 %square.9 = (f32[256,1024]{1,0:T(8,128)S(1)}, bf16[1280,1024]{1,0:T(8,128)(2,1)S(1)}) custom-call(bf16[256,4096]{1,0:T(8,128)(2,1)S(1)} %get-tuple-element.20.refs_0_, bf16[1040,128]{1,0:T(8,128)(2,1)S(1)} %get-tuple-element.18.refs_1_, bf16[1040,128]{1,0:T(8,128)(2,1)S(1)} %collective-permute-done.11.refs_2_, ...), custom_call_target="tpu_custom_call" | custom-call | tf_op jit(solution)/shard_map/square/pallas_call | solution.py:386
  31.3 0.2 collective-permute-start.18
  31.5 2.1 %collective-permute-start.4 = (bf16[1040,128]{1,0:T(8,128)(2,1)S(1)}, bf16[1040,128]{1,0:T(8,128)(2,1)S(1)}, u32[]{:S(2)}, u32[]{:S(2)}) collective-permute-start(bf16[1040,128]{1,0:T(8,128)(2,1)S(1)} %collective-permute-done.3.refs_4_), channel_id=1, source_target_pairs={{0,8},{2,6},{8,16},{10,2},{16,24},{18,10},{24,28},{26,18},{28,20},... | collective-permute-start | bytes 798728 | tf_op jit(solution)/shard_map/ppermute | solution.py:414
  33.6 0.0 collective-permute-start.7
  33.6 1.0 %collective-permute-start.16 = (bf16[1040,128]{1,0:T(8,128)(2,1)S(1)}, bf16[1040,128]{1,0:T(8,128)(2,1)S(1)}, u32[]{:S(2)}, u32[]{:S(2)}) collective-permute-start(bf16[1040,128]{1,0:T(8,128)(2,1)S(1)} %collective-permute-done.15.refs_5_), channel_id=1, source_target_pairs={{8,0},{6,2},{16,8},{2,10},{24,16},{10,18},{28,24},{18,26},{20,28},... | collective-permute-start | bytes 798728 | tf_op jit(solution)/shard_map/ppermute | solution.py:414
  34.6 5.9 %collective-permute-done.4.refs_1_ = bf16[1040,128]{1,0:T(8,128)(2,1)S(1)} collective-permute-done((bf16[1040,128]{1,0:T(8,128)(2,1)S(1)}, bf16[1040,128]{1,0:T(8,128)(2,1)S(1)}, u32[]{:S(2)}, u32[]{:S(2)}) %collective-permute-start.4) | collective-permute-done | bytes 266272 | tf_op jit(solution)/shard_map/ppermute | solution.py:414
  40.5 2.3 %collective-permute-start.8 = (bf16[1040,128]{1,0:T(8,128)(2,1)S(1)}, bf16[1040,128]{1,0:T(8,128)(2,1)S(1)}, u32[]{:S(2)}, u32[]{:S(2)}) collective-permute-start(bf16[1040,128]{1,0:T(8,128)(2,1)S(1)} %collective-permute-done.4.refs_1_), channel_id=1, source_target_pairs={{0,8},{2,6},{8,16},{10,2},{16,24},{18,10},{24,28},{26,18},{28,20},... | collective-permute-start | bytes 798728 | tf_op jit(solution)/shard_map/ppermute | solution.py:414
  42.8 0.0 collective-permute-done.7.refs_2_
  42.8 1.6 %collective-permute-start.13 = (bf16[1040,128]{1,0:T(8,128)(2,1)S(1)}, bf16[1040,128]{1,0:T(8,128)(2,1)S(1)}, u32[]{:S(2)}, u32[]{:S(2)}) collective-permute-start(bf16[1040,128]{1,0:T(8,128)(2,1)S(1)} %collective-permute-done.12.refs_4_), channel_id=1, source_target_pairs={{0,8},{2,6},{8,16},{10,2},{16,24},{18,10},{24,28},{26,18},{28,20},... | collective-permute-start | bytes 798728 | tf_op jit(solution)/shard_map/ppermute | solution.py:414
  44.3 1.3 %collective-permute-done.16.refs_2_ = bf16[1040,128]{1,0:T(8,128)(2,1)S(1)} collective-permute-done((bf16[1040,128]{1,0:T(8,128)(2,1)S(1)}, bf16[1040,128]{1,0:T(8,128)(2,1)S(1)}, u32[]{:S(2)}, u32[]{:S(2)}) %collective-permute-start.16) | collective-permute-done | bytes 266272 | tf_op jit(solution)/shard_map/ppermute | solution.py:414
  45.7 0.2 collective-permute-start.17
  45.8 2.1 %collective-permute-done.8.refs_3_ = bf16[1040,128]{1,0:T(8,128)(2,1)S(1)} collective-permute-done((bf16[1040,128]{1,0:T(8,128)(2,1)S(1)}, bf16[1040,128]{1,0:T(8,128)(2,1)S(1)}, u32[]{:S(2)}, u32[]{:S(2)}) %collective-permute-start.8) | collective-permute-done | bytes 266272 | tf_op jit(solution)/shard_map/ppermute | solution.py:414
  48.0 0.0 collective-permute-done.9.refs_4_.refs_5_
  48.0 1.3 %square.7 = (f32[256,1024]{1,0:T(8,128)S(1)}, bf16[768,1024]{1,0:T(8,128)(2,1)S(1)}) custom-call(bf16[256,4096]{1,0:T(8,128)(2,1)S(1)} %get-tuple-element.20.refs_0_, bf16[1040,128]{1,0:T(8,128)(2,1)S(1)} %collective-permute-done.4.refs_1_, bf16[1040,128]{1,0:T(8,128)(2,1)S(1)} %collective-permute-done.7.refs_2_, ...), custom_call_target="tpu_custom_call" | custom-call | tf_op jit(solution)/shard_map/square/pallas_call | solution.py:386
  49.3 0.1 collective-permute-start.10
  49.4 3.2 %collective-permute-done.13.refs_1_ = bf16[1040,128]{1,0:T(8,128)(2,1)S(1)} collective-permute-done((bf16[1040,128]{1,0:T(8,128)(2,1)S(1)}, bf16[1040,128]{1,0:T(8,128)(2,1)S(1)}, u32[]{:S(2)}, u32[]{:S(2)}) %collective-permute-start.13) | collective-permute-done | bytes 266272 | tf_op jit(solution)/shard_map/ppermute | solution.py:414
  52.6 0.0 collective-permute-done.17.refs_3_
  52.6 0.0 collective-permute-done.18.refs_4_.refs_9_
  52.6 1.3 %square.10 = (f32[256,1024]{1,0:T(8,128)S(1)}, bf16[768,1024]{1,0:T(8,128)(2,1)S(1)}) custom-call(bf16[256,4096]{1,0:T(8,128)(2,1)S(1)} %get-tuple-element.20.refs_0_, bf16[1040,128]{1,0:T(8,128)(2,1)S(1)} %collective-permute-done.13.refs_1_, bf16[1040,128]{1,0:T(8,128)(2,1)S(1)} %collective-permute-done.16.refs_2_, ...), custom_call_target="tpu_custom_call" | custom-call | tf_op jit(solution)/shard_map/square/pallas_call | solution.py:386
  53.9 0.1 collective-permute-start.19
  54.0 0.0 collective-permute-done.10.refs_1_.refs_6_
  54.0 0.6 square.8.refs_0_
  54.6 2.3 %collective-permute-start.20 = (bf16[256,1024]{1,0:T(8,128)(2,1)S(1)}, bf16[256,1024]{1,0:T(8,128)(2,1)S(1)}, u32[]{:S(2)}, u32[]{:S(2)}) collective-permute-start(bf16[256,1024]{1,0:T(8,128)(2,1)S(1)} %square.8.refs_0_), channel_id=1, source_target_pairs={{0,1},{1,0},{2,3},{3,2},{4,5},{5,4},{6,7},{7,6},{8,9},{9,8},{10,11... | collective-permute-start | bytes 1572872 | tf_op jit(solution)/shard_map/ppermute | solution.py:345
  57.0 0.4 collective-permute-done.19.refs_1_.refs_10_
  57.4 0.6 square.11.refs_1_
  58.0 2.3 %collective-permute-start.21 = (bf16[256,1024]{1,0:T(8,128)(2,1)S(1)}, bf16[256,1024]{1,0:T(8,128)(2,1)S(1)}, u32[]{:S(2)}, u32[]{:S(2)}) collective-permute-start(bf16[256,1024]{1,0:T(8,128)(2,1)S(1)} %square.11.refs_1_), channel_id=1, source_target_pairs={{0,1},{1,0},{2,3},{3,2},{4,5},{5,4},{6,7},{7,6},{8,9},{9,8},{10,11... | collective-permute-start | bytes 1572872 | tf_op jit(solution)/shard_map/ppermute | solution.py:345
  60.4 9.4 %collective-permute-done.20.refs_2_ = bf16[256,1024]{1,0:T(8,128)(2,1)S(1)} collective-permute-done((bf16[256,1024]{1,0:T(8,128)(2,1)S(1)}, bf16[256,1024]{1,0:T(8,128)(2,1)S(1)}, u32[]{:S(2)}, u32[]{:S(2)}) %collective-permute-start.20) | collective-permute-done | bytes 524320 | tf_op jit(solution)/shard_map/ppermute | solution.py:345
  69.7 6.7 %cube.1 = (f32[256,2048]{1,0:T(8,128)S(1)}, bf16[2,8,2,128,128]{4,3,2,1,0:T(8,128)(2,1)}, bf16[1024,2048]{1,0:T(8,128)(2,1)S(1)}) custom-call(f32[16,128]{1,0:T(8,128)S(1)} %get-tuple-element.19.kept, bf16[256,1024]{1,0:T(8,128)(2,1)S(1)} %square.8.refs_0_, bf16[256,1024]{1,0:T(8,128)(2,1)S(1)} %square.11.refs_1_, ...), custom_call_target="tpu_custom_call" | custom-call | tf_op jit(solution)/shard_map/cube/pallas_call | solution.py:439
  76.4 4.3 %collective-permute-done.21.refs_2_ = bf16[256,1024]{1,0:T(8,128)(2,1)S(1)} collective-permute-done((bf16[256,1024]{1,0:T(8,128)(2,1)S(1)}, bf16[256,1024]{1,0:T(8,128)(2,1)S(1)}, u32[]{:S(2)}, u32[]{:S(2)}) %collective-permute-start.21) | collective-permute-done | bytes 524320 | tf_op jit(solution)/shard_map/ppermute | solution.py:345
  80.8 2.4 %final.1 = bf16[2,8,2,128,128]{4,3,2,1,0:T(8,128)(2,1)} custom-call(f32[16,128]{1,0:T(8,128)S(1)} %get-tuple-element.19.kept, f32[256,2048]{1,0:T(8,128)S(1)} %get-tuple-element.30.acc, bf16[1024,2048]{1,0:T(8,128)(2,1)S(1)} %get-tuple-element.31.later, bf16[256,1024]{1,0:T(8,128)(2,1)S(1)} %square.8.refs_0_, bf16[256,1024]{1,0:T(8,128)(2,1)S(1)} %square.11.refs_1_, ...), custom_call_target="tpu_custom_call" | custom-call | tf_op jit(solution)/shard_map/final/pallas_call | solution.py:453
Async XLA Ops:
  0.6 1.0 %copy-start = (bf16[2,8,1,128,128]{4,3,2,1,0:T(8,128)(2,1)S(1)}, bf16[2,8,1,128,128]{4,3,2,1,0:T(8,128)(2,1)}, u32[]{:S(2)}) copy-start(bf16[2,8,1,128,128]{4,3,2,1,0:T(8,128)(2,1)} %param.3) | copy-start | bytes 1572868
  1.7 0.7 copy-start.2
  3.2 9.8 %collective-permute-start.5 = (bf16[1040,128]{1,0:T(8,128)(2,1)S(1)}, bf16[1040,128]{1,0:T(8,128)(2,1)S(1)}, u32[]{:S(2)}, u32[]{:S(2)}) collective-permute-start(bf16[1040,128]{1,0:T(8,128)(2,1)S(1)} %get-tuple-element.17.refs_0_.refs_1_), channel_id=1, source_target_pairs={{8,0},{6,2},{16,8},{2,10},{24,16},{10,18},{28,24},{18,26},{20,28},... | collective-permute-start | bytes 798728 | tf_op jit(solution)/shard_map/ppermute | solution.py:414
  6.2 9.2 %collective-permute-start.2 = (bf16[1040,128]{1,0:T(8,128)(2,1)S(1)}, bf16[1040,128]{1,0:T(8,128)(2,1)S(1)}, u32[]{:S(2)}, u32[]{:S(2)}) collective-permute-start(bf16[1040,128]{1,0:T(8,128)(2,1)S(1)} %get-tuple-element.17.refs_0_.refs_1_), channel_id=1, source_target_pairs={{0,8},{2,6},{8,16},{10,2},{16,24},{18,10},{24,28},{26,18},{28,20},... | collective-permute-start | bytes 798728 | tf_op jit(solution)/shard_map/ppermute | solution.py:414
  6.3 10.8 %collective-permute-start = (bf16[1040,128]{1,0:T(8,128)(2,1)S(1)}, bf16[1040,128]{1,0:T(8,128)(2,1)S(1)}, u32[]{:S(2)}, u32[]{:S(2)}) collective-permute-start(bf16[1040,128]{1,0:T(8,128)(2,1)S(1)} %get-tuple-element.17.refs_0_.refs_1_), channel_id=1, source_target_pairs={{0,1},{1,0},{2,3},{3,2},{4,5},{5,4},{6,7},{7,6},{8,9},{9,8},{10,11... | collective-permute-start | bytes 798728 | tf_op jit(solution)/shard_map/ppermute | solution.py:345
  8.2 10.4 %collective-permute-start.14 = (bf16[1040,128]{1,0:T(8,128)(2,1)S(1)}, bf16[1040,128]{1,0:T(8,128)(2,1)S(1)}, u32[]{:S(2)}, u32[]{:S(2)}) collective-permute-start(bf16[1040,128]{1,0:T(8,128)(2,1)S(1)} %get-tuple-element.18.refs_1_), channel_id=1, source_target_pairs={{8,0},{6,2},{16,8},{2,10},{24,16},{10,18},{28,24},{18,26},{20,28},... | collective-permute-start | bytes 798728 | tf_op jit(solution)/shard_map/ppermute | solution.py:414
  9.7 11.4 %collective-permute-start.11 = (bf16[1040,128]{1,0:T(8,128)(2,1)S(1)}, bf16[1040,128]{1,0:T(8,128)(2,1)S(1)}, u32[]{:S(2)}, u32[]{:S(2)}) collective-permute-start(bf16[1040,128]{1,0:T(8,128)(2,1)S(1)} %get-tuple-element.18.refs_1_), channel_id=1, source_target_pairs={{0,8},{2,6},{8,16},{10,2},{16,24},{18,10},{24,28},{26,18},{28,20},... | collective-permute-start | bytes 798728 | tf_op jit(solution)/shard_map/ppermute | solution.py:414
  12.9 8.4 %collective-permute-start.1 = (bf16[1040,128]{1,0:T(8,128)(2,1)S(1)}, bf16[1040,128]{1,0:T(8,128)(2,1)S(1)}, u32[]{:S(2)}, u32[]{:S(2)}) collective-permute-start(bf16[1040,128]{1,0:T(8,128)(2,1)S(1)} %get-tuple-element.18.refs_1_), channel_id=1, source_target_pairs={{0,1},{1,0},{2,3},{3,2},{4,5},{5,4},{6,7},{7,6},{8,9},{9,8},{10,11... | collective-permute-start | bytes 798728 | tf_op jit(solution)/shard_map/ppermute | solution.py:345
  15.3 9.3 %collective-permute-start.6 = (bf16[1040,128]{1,0:T(8,128)(2,1)S(1)}, bf16[1040,128]{1,0:T(8,128)(2,1)S(1)}, u32[]{:S(2)}, u32[]{:S(2)}) collective-permute-start(bf16[1040,128]{1,0:T(8,128)(2,1)S(1)} %collective-permute-done.5.refs_3_), channel_id=1, source_target_pairs={{8,0},{6,2},{16,8},{2,10},{24,16},{10,18},{28,24},{18,26},{20,28},... | collective-permute-start | bytes 798728 | tf_op jit(solution)/shard_map/ppermute | solution.py:414
  17.1 9.3 %collective-permute-start.3 = (bf16[1040,128]{1,0:T(8,128)(2,1)S(1)}, bf16[1040,128]{1,0:T(8,128)(2,1)S(1)}, u32[]{:S(2)}, u32[]{:S(2)}) collective-permute-start(bf16[1040,128]{1,0:T(8,128)(2,1)S(1)} %collective-permute-done.2.refs_2_), channel_id=1, source_target_pairs={{0,8},{2,6},{8,16},{10,2},{16,24},{18,10},{24,28},{26,18},{28,20},... | collective-permute-start | bytes 798728 | tf_op jit(solution)/shard_map/ppermute | solution.py:414
  18.6 11.7 %collective-permute-start.15 = (bf16[1040,128]{1,0:T(8,128)(2,1)S(1)}, bf16[1040,128]{1,0:T(8,128)(2,1)S(1)}, u32[]{:S(2)}, u32[]{:S(2)}) collective-permute-start(bf16[1040,128]{1,0:T(8,128)(2,1)S(1)} %collective-permute-done.14.refs_3_), channel_id=1, source_target_pairs={{8,0},{6,2},{16,8},{2,10},{24,16},{10,18},{28,24},{18,26},{20,28},... | collective-permute-start | bytes 798728 | tf_op jit(solution)/shard_map/ppermute | solution.py:414
  21.1 9.2 %collective-permute-start.12 = (bf16[1040,128]{1,0:T(8,128)(2,1)S(1)}, bf16[1040,128]{1,0:T(8,128)(2,1)S(1)}, u32[]{:S(2)}, u32[]{:S(2)}) collective-permute-start(bf16[1040,128]{1,0:T(8,128)(2,1)S(1)} %collective-permute-done.11.refs_2_), channel_id=1, source_target_pairs={{0,8},{2,6},{8,16},{10,2},{16,24},{18,10},{24,28},{26,18},{28,20},... | collective-permute-start | bytes 798728 | tf_op jit(solution)/shard_map/ppermute | solution.py:414
  21.3 0.7 copy-start.1
  27.3 20.6 %collective-permute-start.9 = (bf16[1280,1024]{1,0:T(8,128)(2,1)S(1)}, bf16[1280,1024]{1,0:T(8,128)(2,1)S(1)}, u32[]{:S(2)}, u32[]{:S(2)}) collective-permute-start(bf16[1280,1024]{1,0:T(8,128)(2,1)S(1)} %get-tuple-element.21.refs_3_), channel_id=1, source_target_pairs={{0,2},{2,0},{4,6},{6,4},{8,10},{10,8},{12,14},{14,12},{16,18},{18,... | collective-permute-start | bytes 7864328 | tf_op jit(solution)/shard_map/ppermute | solution.py:428
  31.3 21.3 %collective-permute-start.18 = (bf16[1280,1024]{1,0:T(8,128)(2,1)S(1)}, bf16[1280,1024]{1,0:T(8,128)(2,1)S(1)}, u32[]{:S(2)}, u32[]{:S(2)}) collective-permute-start(bf16[1280,1024]{1,0:T(8,128)(2,1)S(1)} %get-tuple-element.25.refs_7_), channel_id=1, source_target_pairs={{0,2},{2,0},{4,6},{6,4},{8,10},{10,8},{12,14},{14,12},{16,18},{18,... | collective-permute-start | bytes 7864328 | tf_op jit(solution)/shard_map/ppermute | solution.py:428
  31.5 9.0 %collective-permute-start.4 = (bf16[1040,128]{1,0:T(8,128)(2,1)S(1)}, bf16[1040,128]{1,0:T(8,128)(2,1)S(1)}, u32[]{:S(2)}, u32[]{:S(2)}) collective-permute-start(bf16[1040,128]{1,0:T(8,128)(2,1)S(1)} %collective-permute-done.3.refs_4_), channel_id=1, source_target_pairs={{0,8},{2,6},{8,16},{10,2},{16,24},{18,10},{24,28},{26,18},{28,20},... | collective-permute-start | bytes 798728 | tf_op jit(solution)/shard_map/ppermute | solution.py:414
  33.6 9.2 %collective-permute-start.7 = (bf16[1040,128]{1,0:T(8,128)(2,1)S(1)}, bf16[1040,128]{1,0:T(8,128)(2,1)S(1)}, u32[]{:S(2)}, u32[]{:S(2)}) collective-permute-start(bf16[1040,128]{1,0:T(8,128)(2,1)S(1)} %collective-permute-done.6.refs_5_), channel_id=1, source_target_pairs={{8,0},{6,2},{16,8},{2,10},{24,16},{10,18},{28,24},{18,26},{20,28},... | collective-permute-start | bytes 798728 | tf_op jit(solution)/shard_map/ppermute | solution.py:414
  33.6 12.1 %collective-permute-start.16 = (bf16[1040,128]{1,0:T(8,128)(2,1)S(1)}, bf16[1040,128]{1,0:T(8,128)(2,1)S(1)}, u32[]{:S(2)}, u32[]{:S(2)}) collective-permute-start(bf16[1040,128]{1,0:T(8,128)(2,1)S(1)} %collective-permute-done.15.refs_5_), channel_id=1, source_target_pairs={{8,0},{6,2},{16,8},{2,10},{24,16},{10,18},{28,24},{18,26},{20,28},... | collective-permute-start | bytes 798728 | tf_op jit(solution)/shard_map/ppermute | solution.py:414
  40.5 7.5 %collective-permute-start.8 = (bf16[1040,128]{1,0:T(8,128)(2,1)S(1)}, bf16[1040,128]{1,0:T(8,128)(2,1)S(1)}, u32[]{:S(2)}, u32[]{:S(2)}) collective-permute-start(bf16[1040,128]{1,0:T(8,128)(2,1)S(1)} %collective-permute-done.4.refs_1_), channel_id=1, source_target_pairs={{0,8},{2,6},{8,16},{10,2},{16,24},{18,10},{24,28},{26,18},{28,20},... | collective-permute-start | bytes 798728 | tf_op jit(solution)/shard_map/ppermute | solution.py:414
  42.8 9.8 %collective-permute-start.13 = (bf16[1040,128]{1,0:T(8,128)(2,1)S(1)}, bf16[1040,128]{1,0:T(8,128)(2,1)S(1)}, u32[]{:S(2)}, u32[]{:S(2)}) collective-permute-start(bf16[1040,128]{1,0:T(8,128)(2,1)S(1)} %collective-permute-done.12.refs_4_), channel_id=1, source_target_pairs={{0,8},{2,6},{8,16},{10,2},{16,24},{18,10},{24,28},{26,18},{28,20},... | collective-permute-start | bytes 798728 | tf_op jit(solution)/shard_map/ppermute | solution.py:414
  45.7 7.0 %collective-permute-start.17 = (bf16[1040,128]{1,0:T(8,128)(2,1)S(1)}, bf16[1040,128]{1,0:T(8,128)(2,1)S(1)}, u32[]{:S(2)}, u32[]{:S(2)}) collective-permute-start(bf16[1040,128]{1,0:T(8,128)(2,1)S(1)} %collective-permute-done.16.refs_2_), channel_id=1, source_target_pairs={{8,0},{6,2},{16,8},{2,10},{24,16},{10,18},{28,24},{18,26},{20,28},... | collective-permute-start | bytes 798728 | tf_op jit(solution)/shard_map/ppermute | solution.py:414
  49.3 4.7 %collective-permute-start.10 = (bf16[768,1024]{1,0:T(8,128)(2,1)S(1)}, bf16[768,1024]{1,0:T(8,128)(2,1)S(1)}, u32[]{:S(2)}, u32[]{:S(2)}) collective-permute-start(bf16[768,1024]{1,0:T(8,128)(2,1)S(1)} %get-tuple-element.23.refs_4_), channel_id=1, source_target_pairs={{0,2},{2,0},{4,6},{6,4},{8,10},{10,8},{12,14},{14,12},{16,18},{18,... | collective-permute-start | bytes 4718600 | tf_op jit(solution)/shard_map/ppermute | solution.py:428
  53.9 3.5 %collective-permute-start.19 = (bf16[768,1024]{1,0:T(8,128)(2,1)S(1)}, bf16[768,1024]{1,0:T(8,128)(2,1)S(1)}, u32[]{:S(2)}, u32[]{:S(2)}) collective-permute-start(bf16[768,1024]{1,0:T(8,128)(2,1)S(1)} %get-tuple-element.27.refs_8_), channel_id=1, source_target_pairs={{0,2},{2,0},{4,6},{6,4},{8,10},{10,8},{12,14},{14,12},{16,18},{18,... | collective-permute-start | bytes 4718600 | tf_op jit(solution)/shard_map/ppermute | solution.py:428
  54.6 15.1 %collective-permute-start.20 = (bf16[256,1024]{1,0:T(8,128)(2,1)S(1)}, bf16[256,1024]{1,0:T(8,128)(2,1)S(1)}, u32[]{:S(2)}, u32[]{:S(2)}) collective-permute-start(bf16[256,1024]{1,0:T(8,128)(2,1)S(1)} %square.8.refs_0_), channel_id=1, source_target_pairs={{0,1},{1,0},{2,3},{3,2},{4,5},{5,4},{6,7},{7,6},{8,9},{9,8},{10,11... | collective-permute-start | bytes 1572872 | tf_op jit(solution)/shard_map/ppermute | solution.py:345
  58.0 22.8 %collective-permute-start.21 = (bf16[256,1024]{1,0:T(8,128)(2,1)S(1)}, bf16[256,1024]{1,0:T(8,128)(2,1)S(1)}, u32[]{:S(2)}, u32[]{:S(2)}) collective-permute-start(bf16[256,1024]{1,0:T(8,128)(2,1)S(1)} %square.11.refs_1_), channel_id=1, source_target_pairs={{0,1},{1,0},{2,3},{3,2},{4,5},{5,4},{6,7},{7,6},{8,9},{9,8},{10,11... | collective-permute-start | bytes 1572872 | tf_op jit(solution)/shard_map/ppermute | solution.py:345

commit v4 on v2

--- a/solution.py
+++ b/solution.py
@@ -12,13 +12,22 @@
 
 
 def chunk_sizes(panels):
-    last = max(1, (panels * 3) // 8)
+    last = max(1, panels//2)
     return (panels - last, last)
 
 
 def hop_groups(chips):
     last = chips // 2
     return ((0, 1), tuple(range(2, last)), (last,))
+
+
+def spans_of(groups, chips):
+    spans, start = [], 0
+    for group in groups:
+        count = sum(hop_slabs(hop, chips) for hop in group)
+        spans.append((start, count))
+        start += count
+    return spans
 
 
 def ring_chip(position, chips):
@@ -86,16 +95,32 @@
     return jnp.broadcast_to(total.astype(jnp.float32), (rows, lanes))
 
 
-def pack_kernel(size, first, cols_ref, x_ref, *refs):
-    out = refs[-1]
-    width, tile = x_ref.shape[0], x_ref.shape[-1]
-    for local in range(width):
-        for panel in range(size):
-            index = local * size + panel
-            out[index * tile : (index + 1) * tile, :] = x_ref[local, first + panel, 0]
-    base = width * size * tile
-    flags = lane_flags(cols_ref[...], FLAG_ROWS, size, first, tile)
-    out[base : base + FLAG_ROWS, :] = flags.astype(jnp.bfloat16)
+def pack_kernel(sizes, tile, cols_ref, x_ref, *refs):
+    outs, (cols, copied, sems) = refs[:-3], refs[-3:]
+    width = x_ref.shape[0]
+    columns = pltpu.make_async_copy(cols_ref, cols, copied)
+    columns.start()
+    copies = []
+    first = 0
+    for size, out in zip(sizes, outs):
+        for local in range(width):
+            copy = pltpu.make_async_copy(
+                x_ref.at[local, pl.ds(first * tile, size * tile), :],
+                out.at[pl.ds(local * size * tile, size * tile), :],
+                sems.at[len(copies)],
+            )
+            copy.start()
+            copies.append(copy)
+        first += size
+    columns.wait()
+    first = 0
+    for size, out in zip(sizes, outs):
+        base = width * size * tile
+        flags = lane_flags(cols[...], FLAG_ROWS, size, first, tile)
+        out[base : base + FLAG_ROWS, :] = flags.astype(jnp.bfloat16)
+        first += size
+    for copy in copies:
+        copy.wait()
 
 
 def halves(payload, flags, index, tile):
@@ -127,7 +152,11 @@
                     out[part, pl.ds(start, tile)] = left
                     out[part, pl.ds(start + tile, tile)] = right
             first += size
-    kept[...] = lane_flags(keep_ref[...], kept.shape[0], panels, 0, tile)
+    keep = keep_ref[...]
+    firsts = jnp.concatenate(
+        [keep[local * 2 : local * 2 + 1, :] for local in range(width)], axis=0
+    )
+    kept[...] = lane_flags(firsts, kept.shape[0], panels, 0, tile)
 
 
 def square_kernel(size, width, tile, start, count, first, *refs):
@@ -160,7 +189,8 @@
     panels = sum(sizes)
     own = refs[:chunks]
     received = refs[chunks : chunks + (groups - 1) * (chunks - 1)]
-    rights = refs[chunks + (groups - 1) * (chunks - 1) : -4]
+    flat = list(refs[chunks + (groups - 1) * (chunks - 1) : -4])
+    rights = [[flat.pop(0) for _ in spans[chunk]] for chunk in range(chunks)]
     acc, square, later, squares = refs[-4:]
     row, mine = lax.axis_index("row"), lax.axis_index("col")
 
@@ -188,10 +218,10 @@
     column = 0
     for chunk, size in enumerate(sizes):
         total = None
-        for part, (start, count) in enumerate(spans):
+        for part, (start, count) in enumerate(spans[chunk]):
             product = jnp.dot(
                 squares[:, start * dense : (start + count) * dense],
-                rights[chunk * len(spans) + part][...],
+                rights[chunk][part][...],
                 preferred_element_type=jnp.float32,
             )
             total = product if total is None else total + product
@@ -199,22 +229,24 @@
         column += size * dense
 
     last = sizes[-1]
-    for part, (start, count) in enumerate(spans):
-        for index in range(count):
-            slab = slab_of(start + index, row, rows)
-            group, panel = slab // panels, lax.rem(slab, panels)
-            shift = lax.rem(mine - group + groups, groups)
-
-            @pl.when((shift > 0) & (panel >= panels - last))
-            def _(part=part, index=index, shift=shift, panel=panel):
-                where = (shift - 1) * last + panel - (panels - last)
-                target = pl.ds(pl.multiple_of(where * dense, dense), dense)
-                column = 0
-                for chunk, size in enumerate(sizes):
-                    later[target, column : column + size * dense] = rights[
-                        chunk * len(spans) + part
-                    ][index * dense : (index + 1) * dense, :]
-                    column += size * dense
+    for position in range(rows):
+        slab = slab_of(position, row, rows)
+        group, panel = slab // panels, lax.rem(slab, panels)
+        shift = lax.rem(mine - group + groups, groups)
+
+        @pl.when((shift > 0) & (panel >= panels - last))
+        def _(position=position, shift=shift, panel=panel):
+            where = (shift - 1) * last + panel - (panels - last)
+            target = pl.ds(pl.multiple_of(where * dense, dense), dense)
+            column = 0
+            for chunk, size in enumerate(sizes):
+                for part, (start, count) in enumerate(spans[chunk]):
+                    if start <= position < start + count:
+                        place = (position - start) * dense
+                        later[target, column : column + size * dense] = rights[chunk][part][
+                            place : place + dense, :
+                        ]
+                column += size * dense
 
     first = 0
     for size, source in zip(sizes, own):
@@ -277,6 +309,10 @@
     return [pl.BlockSpec(memory_space=pl.ANY)] * count
 
 
+def after(value, *others):
+    return lax.optimization_barrier((value,) + others)[0] if others else value
+
+
 def params(mib):
     return pltpu.CompilerParams(vmem_limit_bytes=mib * 1024 * 1024)
 
@@ -296,76 +332,118 @@
         return lax.ppermute(value, "col", pairs)
 
     cols = x_cols.reshape(width, panels)
-    spans, start = [], 0
-    for group in hop_groups(chips):
-        count = sum(hop_slabs(hop, chips) for hop in group)
-        spans.append((start, count))
-        start += count
-
-    def pack(chunk, *after):
-        size = sizes[chunk]
+    keeps = jnp.transpose(keep_cols, (0, 2, 1)).reshape(width * 2, panels)
+    kept_rows = -(-width * panels // 8) * 8
+    payloads = pl.pallas_call(
+        functools.partial(pack_kernel, sizes, tile),
+        out_shape=[
+            jax.ShapeDtypeStruct((width * size * tile + FLAG_ROWS, tile), bf16) for size in sizes
+        ],
+        in_specs=anywhere(2),
+        out_specs=vmem(len(sizes)),
+        scratch_shapes=[
+            pltpu.VMEM((width, panels), jnp.int32),
+            pltpu.SemaphoreType.DMA,
+            pltpu.SemaphoreType.DMA((width * len(sizes),)),
+        ],
+        compiler_params=params(4),
+        name="pack",
+    )(cols, x_tiles.reshape(width, panels * tile, tile))
+
+    def sibling_of(value):
+        return lax.ppermute(value, "row", sibling)
+
+    def left_of(lefts):
         return pl.pallas_call(
-            functools.partial(pack_kernel, size, sum(sizes[:chunk])),
-            out_shape=jax.ShapeDtypeStruct((width * size * tile + FLAG_ROWS, tile), bf16),
-            in_specs=vmem(2) + anywhere(len(after)),
-            out_specs=vmem(1)[0],
+            functools.partial(left_kernel, sizes, rows, groups, width, tile),
+            out_shape=[
+                jax.ShapeDtypeStruct((dense, rows * dense), bf16),
+                jax.ShapeDtypeStruct((kept_rows, tile), f32),
+            ],
+            in_specs=vmem(1 + len(lefts)),
+            out_specs=vmem(2),
             compiler_params=params(4),
-            name="pack",
-        )(cols, x_tiles, *after)
-
-    payloads = [pack(chunk) for chunk in range(len(sizes))]
+            name="left",
+        )(keeps, *lefts)
+
+    def square_of(size, span, left, pieces, total, last):
+        start, count = span
+        operands = [left] + pieces + ([] if total is None else [total])
+        return pl.pallas_call(
+            functools.partial(square_kernel, size, width, tile, start, count, total is None),
+            out_shape=[
+                jax.ShapeDtypeStruct((dense, size * dense), bf16 if last else f32),
+                jax.ShapeDtypeStruct((count * dense, size * dense), bf16),
+            ],
+            in_specs=vmem(len(operands)),
+            out_specs=vmem(2),
+            compiler_params=params(4),
+            name="square",
+        )(*operands)
+
+    hops = chips // 2
     lefts = list(payloads)
     for shift in range(1, groups):
         lefts += [across(payload, shift) for payload in payloads]
-    kept_rows = -(-width * panels // 8) * 8
-    left, kept = pl.pallas_call(
-        functools.partial(left_kernel, sizes, rows, groups, width, tile),
-        out_shape=[
-            jax.ShapeDtypeStruct((dense, rows * dense), bf16),
-            jax.ShapeDtypeStruct((kept_rows, tile), f32),
-        ],
-        in_specs=vmem(1 + len(lefts)),
-        out_specs=vmem(2),
-        compiler_params=params(4),
-        name="left",
-    )(keep_cols[:, :, 0], *lefts)
-
-    squares, received, rights = [], [], []
-    gate = None
-    for chunk, payload in enumerate(payloads):
-        size = sizes[chunk]
-        if gate is not None:
-            payload, gate = lax.optimization_barrier((payload, gate))
-        ahead = behind = payload
-        total = None
-        for group, (start, count) in zip(hop_groups(chips), spans):
-            pieces = []
-            for hop in group:
-                if hop > 0:
-                    ahead = lax.ppermute(ahead, "row", forward)
-                pieces += [ahead, lax.ppermute(ahead, "row", sibling)]
-                if 0 < hop < chips - chips // 2:
-                    behind = lax.ppermute(behind, "row", backward)
-                    pieces += [behind, lax.ppermute(behind, "row", sibling)]
-            last = start + count == rows
-            operands = [left] + pieces + ([] if total is None else [total])
-            total, right = pl.pallas_call(
-                functools.partial(
-                    square_kernel, size, width, tile, start, count, total is None
-                ),
-                out_shape=[
-                    jax.ShapeDtypeStruct((dense, size * dense), bf16 if last else f32),
-                    jax.ShapeDtypeStruct((count * dense, size * dense), bf16),
-                ],
-                in_specs=vmem(len(operands)),
-                out_specs=vmem(2),
-                compiler_params=params(4),
-                name="square",
-            )(*operands)
-            rights.append(right)
-            gate = behind
-        squares.append(total)
-        received.append([across(total, shift) for shift in range(1, groups)])
+    left, kept = left_of(lefts)
+    groups_of = hop_groups(chips)
+    spans = [spans_of(groups_of, chips)] * len(sizes)
+    moved = [{True: [payload], False: [payload]} for payload in payloads]
+    swaps = [{} for _ in payloads]
+    rights = [[] for _ in payloads]
+    totals = [[] for _ in payloads]
+    gates = {}
+
+    def swap(chunk, hop, *waits):
+        for key in (True, False):
+            if hop < len(moved[chunk][key]) and (hop > 0 or key):
+                value = moved[chunk][key][hop]
+                swaps[chunk][hop, key] = sibling_of(after(value, *waits))
+
+    def multiply(chunk, part):
+        pieces = []
+        for hop in groups_of[part]:
+            for key in (True, False):
+                if (hop, key) in swaps[chunk]:
+                    pieces += [moved[chunk][key][hop], swaps[chunk][hop, key]]
+        total, right = square_of(
+            sizes[chunk],
+            spans[chunk][part],
+            left,
+            pieces,
+            totals[chunk][-1] if totals[chunk] else None,
+            part == len(groups_of) - 1,
+        )
+        totals[chunk].append(total)
+        rights[chunk].append(right)
+
+    for hop in range(1, hops + 1):
+        if hop == hops:
+            for chunk in range(len(sizes)):
+                for part in range(1):
+                    for past in groups_of[part]:
+                        swap(chunk, past)
+                    multiply(chunk, part)
+                    gates.setdefault(hop, []).append(totals[chunk][-1])
+        for chunk in range(len(sizes)):
+            for ahead in (True, False):
+                if hop == hops and ahead == (chunk == 1):
+                    continue
+                value = after(moved[chunk][ahead][-1], *gates.get(hop, []))
+                moved[chunk][ahead].append(
+                    lax.ppermute(value, "row", forward if ahead else backward)
+                )
+    squares, received = [], []
+    for chunk in range(len(sizes)):
+        for part in range(1, len(groups_of)):
+            for past in groups_of[part]:
+                swap(chunk, past)
+            if chunk > 0 and part == len(groups_of) - 1:
+                totals[chunk][-1] = after(totals[chunk][-1], *received[0])
+            multiply(chunk, part)
+        squares.append(totals[chunk][-1])
+        received.append([across(squares[-1], shift) for shift in range(1, groups)])
+    rights = [right for some in rights for right in some]
 
     already = [part[shift] for shift in range(groups - 1) for part in received[:-1]]
     later_rows = (groups - 1) * sizes[-1] * dense

time: 91.8 us -> 79.4 us (0.86)
  waiting for transfers between devices: 48.8 us -> 30.8 us
  starting transfers between devices: 23.4 us -> 28.8 us
    ppermute x30, waiting for transfers between devices: 33.5 us -> 18.5 us  [the longest x14 17.4 us: shards(): lax.ppermute(value, 'row', forward if ahead else backward)]
    ppermute x30, starting transfers between devices: 19.2 us -> 23.2 us  [the longest x14 20.6 us: shards(): lax.ppermute(value, 'row', forward if ahead else backward)]
    ppermute x4, waiting for transfers between devices: 15.2 us -> 12.3 us  [across(): return lax.ppermute(value, 'col', pairs)]
    ppermute x4, starting transfers between devices: 4.16 us -> 5.61 us  [across(): return lax.ppermute(value, 'col', pairs)]
    unnamed x4 -> x6, local copies, waits for them, and re-layouts: 1.71 us -> 2.39 us
    pallas_call x9 -> x8, Pallas kernels: 6.74 us -> 7.25 us  [the longest x6 5.85 us: square_of(): pl.pallas_call(functools.partial(square_kernel, size, width, tile, start,...]
  transfers between devices with their start and end apart: 34 -> 34, of which waited for: 11 -> 14; matrix products, arithmetic and copies ran while one was open for 1% -> 0% of each run, Pallas kernels for 15% -> 16%
where the time goes in v4:
time: 79.4 us; the launch traced here: 79.1 us
  waiting for transfers between devices  30.8 us (39%)
  starting transfers between devices  28.8 us (36%)
  Pallas kernels  16.3 us (21%)
  local copies, waits for them, and re-layouts  2.39 us (3%)
    ppermute x14, starting transfers between devices, shards(): lax.ppermute(value, 'row', forward if ahead else backward)  20.6 us
    ppermute x14, waiting for transfers between devices, shards(): lax.ppermute(value, 'row', forward if ahead else backward)  17.4 us
    ppermute x4, waiting for transfers between devices, across(): return lax.ppermute(value, 'col', pairs)  12.3 us
    pallas_call x1, Pallas kernels, shards(): pl.pallas_call(functools.partial(cube_kernel, sizes, rows, groups, width,...  6.69 us
    pallas_call x6, Pallas kernels, square_of(): pl.pallas_call(functools.partial(square_kernel, size, width, tile, start,...  5.85 us
    ppermute x4, starting transfers between devices, across(): return lax.ppermute(value, 'col', pairs)  5.61 us
    ppermute x16, starting transfers between devices, sibling_of(): return lax.ppermute(value, 'row', sibling)  2.63 us
    unnamed x6, local copies, waits for them, and re-layouts  2.39 us
  transfers between devices with their start and end apart: 34, of which 14 were waited for; matrix products, arithmetic and copies ran while one was open for 0% of the time, Pallas kernels for 16%

profile of v4, /device:TPU:0, one launch (start us, length us, event | category | flops | bytes accessed | tf_op | source)
XLA Modules:
  0.0 79.1 jit_solution(13376438802180974382)
XLA Ops:
  0.6 1.0 %copy-done = bf16[2,8,1,128,128]{4,3,2,1,0:T(8,128)(2,1)S(1)} copy-done((bf16[2,8,1,128,128]{4,3,2,1,0:T(8,128)(2,1)S(1)}, bf16[2,8,1,128,128]{4,3,2,1,0:T(8,128)(2,1)}, u32[]{:S(2)}) %copy-start) | copy-done | bytes 524312
  1.7 0.7 copy-done.2
  2.4 0.8 %pack.1 = (bf16[1040,128]{1,0:T(8,128)(2,1)S(1)}, bf16[1040,128]{1,0:T(8,128)(2,1)S(1)}) custom-call(s32[2,8]{1,0:T(2,128)S(1)} %bitcast.7, bf16[2,1024,128]{2,1,0:T(8,128)(2,1)S(1)} %bitcast.5), custom_call_target="tpu_custom_call" | custom-call | tf_op jit(solution)/shard_map/pack/pallas_call | solution.py:337
  3.2 3.0 %collective-permute-start.7 = (bf16[1040,128]{1,0:T(8,128)(2,1)S(1)}, bf16[1040,128]{1,0:T(8,128)(2,1)S(1)}, u32[]{:S(2)}, u32[]{:S(2)}) collective-permute-start(bf16[1040,128]{1,0:T(8,128)(2,1)S(1)} %get-tuple-element.24.refs_0_.refs_1_), channel_id=1, source_target_pairs={{8,0},{6,2},{16,8},{2,10},{24,16},{10,18},{28,24},{18,26},{20,28},... | collective-permute-start | bytes 798728 | tf_op jit(solution)/shard_map/ppermute | solution.py:434
  6.2 0.0 collective-permute-start.5
  6.2 1.2 %collective-permute-start.2 = (bf16[1040,128]{1,0:T(8,128)(2,1)S(1)}, bf16[1040,128]{1,0:T(8,128)(2,1)S(1)}, u32[]{:S(2)}, u32[]{:S(2)}) collective-permute-start(bf16[1040,128]{1,0:T(8,128)(2,1)S(1)} %get-tuple-element.24.refs_0_.refs_1_), channel_id=1, source_target_pairs={{0,8},{2,6},{8,16},{10,2},{16,24},{18,10},{24,28},{26,18},{28,20},... | collective-permute-start | bytes 798728 | tf_op jit(solution)/shard_map/ppermute | solution.py:434
  7.4 1.5 %collective-permute-start = (bf16[1040,128]{1,0:T(8,128)(2,1)S(1)}, bf16[1040,128]{1,0:T(8,128)(2,1)S(1)}, u32[]{:S(2)}, u32[]{:S(2)}) collective-permute-start(bf16[1040,128]{1,0:T(8,128)(2,1)S(1)} %get-tuple-element.24.refs_0_.refs_1_), channel_id=1, source_target_pairs={{0,1},{1,0},{2,3},{3,2},{4,5},{5,4},{6,7},{7,6},{8,9},{9,8},{10,11... | collective-permute-start | bytes 798728 | tf_op jit(solution)/shard_map/ppermute | solution.py:332
  8.9 0.8 %collective-permute-start.12 = (bf16[1040,128]{1,0:T(8,128)(2,1)S(1)}, bf16[1040,128]{1,0:T(8,128)(2,1)S(1)}, u32[]{:S(2)}, u32[]{:S(2)}) collective-permute-start(bf16[1040,128]{1,0:T(8,128)(2,1)S(1)} %get-tuple-element.25.refs_1_), channel_id=1, source_target_pairs={{8,0},{6,2},{16,8},{2,10},{24,16},{10,18},{28,24},{18,26},{20,28},... | collective-permute-start | bytes 798728 | tf_op jit(solution)/shard_map/ppermute | solution.py:434
  9.7 2.2 %collective-permute-done.7.refs_5_ = bf16[1040,128]{1,0:T(8,128)(2,1)S(1)} collective-permute-done((bf16[1040,128]{1,0:T(8,128)(2,1)S(1)}, bf16[1040,128]{1,0:T(8,128)(2,1)S(1)}, u32[]{:S(2)}, u32[]{:S(2)}) %collective-permute-start.7) | collective-permute-done | bytes 266272 | tf_op jit(solution)/shard_map/ppermute | solution.py:434
  11.9 3.4 %collective-permute-start.10 = (bf16[1040,128]{1,0:T(8,128)(2,1)S(1)}, bf16[1040,128]{1,0:T(8,128)(2,1)S(1)}, u32[]{:S(2)}, u32[]{:S(2)}) collective-permute-start(bf16[1040,128]{1,0:T(8,128)(2,1)S(1)} %get-tuple-element.25.refs_1_), channel_id=1, source_target_pairs={{0,8},{2,6},{8,16},{10,2},{16,24},{18,10},{24,28},{26,18},{28,20},... | collective-permute-start | bytes 798728 | tf_op jit(solution)/shard_map/ppermute | solution.py:434
  15.4 1.6 %collective-permute-start.1 = (bf16[1040,128]{1,0:T(8,128)(2,1)S(1)}, bf16[1040,128]{1,0:T(8,128)(2,1)S(1)}, u32[]{:S(2)}, u32[]{:S(2)}) collective-permute-start(bf16[1040,128]{1,0:T(8,128)(2,1)S(1)} %get-tuple-element.25.refs_1_), channel_id=1, source_target_pairs={{0,1},{1,0},{2,3},{3,2},{4,5},{5,4},{6,7},{7,6},{8,9},{9,8},{10,11... | collective-permute-start | bytes 798728 | tf_op jit(solution)/shard_map/ppermute | solution.py:332
  16.9 0.0 collective-permute-done.refs_2_
  16.9 0.8 %collective-permute-start.17 = (bf16[1040,128]{1,0:T(8,128)(2,1)S(1)}, bf16[1040,128]{1,0:T(8,128)(2,1)S(1)}, u32[]{:S(2)}, u32[]{:S(2)}) collective-permute-start(bf16[1040,128]{1,0:T(8,128)(2,1)S(1)} %collective-permute-done.7.refs_5_), channel_id=1, source_target_pairs={{8,0},{6,2},{16,8},{2,10},{24,16},{10,18},{28,24},{18,26},{20,28},... | collective-permute-start | bytes 798728 | tf_op jit(solution)/shard_map/ppermute | solution.py:434
  17.7 0.5 collective-permute-done.12.refs_5_
  18.2 2.8 %collective-permute-start.3 = (bf16[1040,128]{1,0:T(8,128)(2,1)S(1)}, bf16[1040,128]{1,0:T(8,128)(2,1)S(1)}, u32[]{:S(2)}, u32[]{:S(2)}) collective-permute-start(bf16[1040,128]{1,0:T(8,128)(2,1)S(1)} %collective-permute-done.2.refs_3_), channel_id=1, source_target_pairs={{0,8},{2,6},{8,16},{10,2},{16,24},{18,10},{24,28},{26,18},{28,20},... | collective-permute-start | bytes 798728 | tf_op jit(solution)/shard_map/ppermute | solution.py:434
  21.0 0.0 collective-permute-done.10.refs_3_
  21.1 0.5 collective-permute-start.13
  21.6 2.6 %collective-permute-done.1.refs_3_ = bf16[1040,128]{1,0:T(8,128)(2,1)S(1)} collective-permute-done((bf16[1040,128]{1,0:T(8,128)(2,1)S(1)}, bf16[1040,128]{1,0:T(8,128)(2,1)S(1)}, u32[]{:S(2)}, u32[]{:S(2)}) %collective-permute-start.1) | collective-permute-done | bytes 266272 | tf_op jit(solution)/shard_map/ppermute | solution.py:332
  24.2 0.0 collective-permute-start.11
  24.2 1.6 %collective-permute-done.17.refs_3_ = bf16[1040,128]{1,0:T(8,128)(2,1)S(1)} collective-permute-done((bf16[1040,128]{1,0:T(8,128)(2,1)S(1)}, bf16[1040,128]{1,0:T(8,128)(2,1)S(1)}, u32[]{:S(2)}, u32[]{:S(2)}) %collective-permute-start.17) | collective-permute-done | bytes 266272 | tf_op jit(solution)/shard_map/ppermute | solution.py:434
  25.8 0.0 collective-permute-done.3.refs_1_
  25.8 1.7 %collective-permute-start.4 = (bf16[1040,128]{1,0:T(8,128)(2,1)S(1)}, bf16[1040,128]{1,0:T(8,128)(2,1)S(1)}, u32[]{:S(2)}, u32[]{:S(2)}) collective-permute-start(bf16[1040,128]{1,0:T(8,128)(2,1)S(1)} %collective-permute-done.3.refs_1_), channel_id=1, source_target_pairs={{0,8},{2,6},{8,16},{10,2},{16,24},{18,10},{24,28},{26,18},{28,20},... | collective-permute-start | bytes 798728 | tf_op jit(solution)/shard_map/ppermute | solution.py:434
  27.5 0.0 collective-permute-done.8.refs_6_
  27.5 0.4 collective-permute-start.22
  27.8 1.7 %collective-permute-start.26 = (bf16[1040,128]{1,0:T(8,128)(2,1)S(1)}, bf16[1040,128]{1,0:T(8,128)(2,1)S(1)}, u32[]{:S(2)}, u32[]{:S(2)}) collective-permute-start(bf16[1040,128]{1,0:T(8,128)(2,1)S(1)} %collective-permute-done.10.refs_3_), channel_id=1, source_target_pairs={{0,8},{2,6},{8,16},{10,2},{16,24},{18,10},{24,28},{26,18},{28,20},... | collective-permute-start | bytes 798728 | tf_op jit(solution)/shard_map/ppermute | solution.py:434
  29.5 0.4 collective-permute-start.20
  29.9 0.7 copy-done.1
  30.5 0.6 left.1
  31.1 1.1 %square.7 = (f32[256,1024]{1,0:T(8,128)S(1)}, bf16[1536,1024]{1,0:T(8,128)(2,1)S(1)}) custom-call(bf16[256,4096]{1,0:T(8,128)(2,1)S(1)} %get-tuple-element.27.refs_0_, bf16[1040,128]{1,0:T(8,128)(2,1)S(1)} %get-tuple-element.25.refs_1_, bf16[1040,128]{1,0:T(8,128)(2,1)S(1)} %collective-permute-done.9.refs_2_, ...), custom_call_target="tpu_custom_call" | custom-call | tf_op jit(solution)/shard_map/square/pallas_call | solution.py:372
  32.2 0.1 collective-permute-start.18
  32.3 1.1 %square.6 = (f32[256,1024]{1,0:T(8,128)S(1)}, bf16[1536,1024]{1,0:T(8,128)(2,1)S(1)}) custom-call(bf16[256,4096]{1,0:T(8,128)(2,1)S(1)} %get-tuple-element.27.refs_0_, bf16[1040,128]{1,0:T(8,128)(2,1)S(1)} %get-tuple-element.24.refs_0_.refs_1_, bf16[1040,128]{1,0:T(8,128)(2,1)S(1)} %collective-permute-done.5.refs_2_, ...), custom_call_target="tpu_custom_call" | custom-call | tf_op jit(solution)/shard_map/square/pallas_call | solution.py:372
  33.4 1.4 %collective-permute-done.4.refs_5_ = bf16[1040,128]{1,0:T(8,128)(2,1)S(1)} collective-permute-done((bf16[1040,128]{1,0:T(8,128)(2,1)S(1)}, bf16[1040,128]{1,0:T(8,128)(2,1)S(1)}, u32[]{:S(2)}, u32[]{:S(2)}) %collective-permute-start.4) | collective-permute-done | bytes 266272 | tf_op jit(solution)/shard_map/ppermute | solution.py:434
  34.7 1.9 %collective-permute-start.14 = (bf16[1040,128]{1,0:T(8,128)(2,1)S(1)}, bf16[1040,128]{1,0:T(8,128)(2,1)S(1)}, u32[]{:S(2)}, u32[]{:S(2)}) collective-permute-start(bf16[1040,128]{1,0:T(8,128)(2,1)S(1)} %collective-permute-done.4.refs_5_), channel_id=1, source_target_pairs={{0,8},{2,6},{8,16},{10,2},{16,24},{18,10},{24,28},{26,18},{28,20},... | collective-permute-start | bytes 798728 | tf_op jit(solution)/shard_map/ppermute | solution.py:434
  36.6 0.2 collective-permute-done.22.refs_3_
  36.8 0.0 collective-permute-start.16
  36.8 3.6 %collective-permute-done.26.refs_1_ = bf16[1040,128]{1,0:T(8,128)(2,1)S(1)} collective-permute-done((bf16[1040,128]{1,0:T(8,128)(2,1)S(1)}, bf16[1040,128]{1,0:T(8,128)(2,1)S(1)}, u32[]{:S(2)}, u32[]{:S(2)}) %collective-permute-start.26) | collective-permute-done | bytes 266272 | tf_op jit(solution)/shard_map/ppermute | solution.py:434
  40.4 0.6 collective-permute-start.23
  41.0 1.5 %collective-permute-done.20.refs_7_ = bf16[1040,128]{1,0:T(8,128)(2,1)S(1)} collective-permute-done((bf16[1040,128]{1,0:T(8,128)(2,1)S(1)}, bf16[1040,128]{1,0:T(8,128)(2,1)S(1)}, u32[]{:S(2)}, u32[]{:S(2)}) %collective-permute-start.20) | collective-permute-done | bytes 266272 | tf_op jit(solution)/shard_map/ppermute | solution.py:434
  42.5 0.5 collective-permute-start.19
  43.0 3.1 %collective-permute-done.14.refs_1_ = bf16[1040,128]{1,0:T(8,128)(2,1)S(1)} collective-permute-done((bf16[1040,128]{1,0:T(8,128)(2,1)S(1)}, bf16[1040,128]{1,0:T(8,128)(2,1)S(1)}, u32[]{:S(2)}, u32[]{:S(2)}) %collective-permute-start.14) | collective-permute-done | bytes 266272 | tf_op jit(solution)/shard_map/ppermute | solution.py:434
  46.2 0.0 collective-permute-start.15
  46.2 0.0 collective-permute-done.16.refs_2_
  46.2 0.5 collective-permute-start.28
  46.7 0.2 collective-permute-done.23.refs_7_
  46.9 1.6 %collective-permute-start.29 = (bf16[1040,128]{1,0:T(8,128)(2,1)S(1)}, bf16[1040,128]{1,0:T(8,128)(2,1)S(1)}, u32[]{:S(2)}, u32[]{:S(2)}) collective-permute-start(bf16[1040,128]{1,0:T(8,128)(2,1)S(1)} %collective-permute-done.26.refs_1_), channel_id=1, source_target_pairs={{0,8},{2,6},{8,16},{10,2},{16,24},{18,10},{24,28},{26,18},{28,20},... | collective-permute-start | bytes 798728 | tf_op jit(solution)/shard_map/ppermute | solution.py:434
  48.5 0.0 collective-permute-done.21.refs_8_
  48.5 0.4 collective-permute-start.24
  48.9 1.4 %square.8 = (f32[256,1024]{1,0:T(8,128)S(1)}, bf16[2048,1024]{1,0:T(8,128)(2,1)S(1)}) custom-call(bf16[256,4096]{1,0:T(8,128)(2,1)S(1)} %get-tuple-element.27.refs_0_, bf16[1040,128]{1,0:T(8,128)(2,1)S(1)} %collective-permute-done.3.refs_1_, bf16[1040,128]{1,0:T(8,128)(2,1)S(1)} %collective-permute-done.16.refs_2_, ...), custom_call_target="tpu_custom_call" | custom-call | tf_op jit(solution)/shard_map/square/pallas_call | solution.py:372
  50.3 0.5 square.9
  50.8 1.2 %collective-permute-start.32 = (bf16[256,1024]{1,0:T(8,128)(2,1)S(1)}, bf16[256,1024]{1,0:T(8,128)(2,1)S(1)}, u32[]{:S(2)}, u32[]{:S(2)}) collective-permute-start(bf16[256,1024]{1,0:T(8,128)(2,1)S(1)} %get-tuple-element.32.refs_0_), channel_id=1, source_target_pairs={{0,1},{1,0},{2,3},{3,2},{4,5},{5,4},{6,7},{7,6},{8,9},{9,8},{10,11... | collective-permute-start | bytes 1572872 | tf_op jit(solution)/shard_map/ppermute | solution.py:332
  52.0 0.5 collective-permute-start.31
  52.5 3.1 %collective-permute-done.29.refs_5_ = bf16[1040,128]{1,0:T(8,128)(2,1)S(1)} collective-permute-done((bf16[1040,128]{1,0:T(8,128)(2,1)S(1)}, bf16[1040,128]{1,0:T(8,128)(2,1)S(1)}, u32[]{:S(2)}, u32[]{:S(2)}) %collective-permute-start.29) | collective-permute-done | bytes 266272 | tf_op jit(solution)/shard_map/ppermute | solution.py:434
  55.6 0.0 collective-permute-start.30
  55.6 0.0 collective-permute-done.24.refs_1_
  55.6 0.5 collective-permute-start.25
  56.1 0.0 collective-permute-done.27.refs_2_
  56.1 1.0 %collective-permute-done.30.refs_6_ = bf16[1040,128]{1,0:T(8,128)(2,1)S(1)} collective-permute-done((bf16[1040,128]{1,0:T(8,128)(2,1)S(1)}, bf16[1040,128]{1,0:T(8,128)(2,1)S(1)}, u32[]{:S(2)}, u32[]{:S(2)}) %collective-permute-start.30) | collective-permute-done | bytes 266272 | tf_op jit(solution)/shard_map/ppermute | solution.py:354
  57.1 1.4 %square.10 = (f32[256,1024]{1,0:T(8,128)S(1)}, bf16[2048,1024]{1,0:T(8,128)(2,1)S(1)}) custom-call(bf16[256,4096]{1,0:T(8,128)(2,1)S(1)} %get-tuple-element.27.refs_0_, bf16[1040,128]{1,0:T(8,128)(2,1)S(1)} %collective-permute-done.26.refs_1_, bf16[1040,128]{1,0:T(8,128)(2,1)S(1)} %collective-permute-done.27.refs_2_, ...), custom_call_target="tpu_custom_call" | custom-call | tf_op jit(solution)/shard_map/square/pallas_call | solution.py:372
  58.5 5.5 %collective-permute-done.32.refs_2_ = bf16[256,1024]{1,0:T(8,128)(2,1)S(1)} collective-permute-done((bf16[256,1024]{1,0:T(8,128)(2,1)S(1)}, bf16[256,1024]{1,0:T(8,128)(2,1)S(1)}, u32[]{:S(2)}, u32[]{:S(2)}) %collective-permute-start.32) | collective-permute-done | bytes 524320 | tf_op jit(solution)/shard_map/ppermute | solution.py:332
  64.0 0.5 square.11
  64.5 1.3 %collective-permute-start.33 = (bf16[256,1024]{1,0:T(8,128)(2,1)S(1)}, bf16[256,1024]{1,0:T(8,128)(2,1)S(1)}, u32[]{:S(2)}, u32[]{:S(2)}) collective-permute-start(bf16[256,1024]{1,0:T(8,128)(2,1)S(1)} %get-tuple-element.36.refs_1_), channel_id=1, source_target_pairs={{0,1},{1,0},{2,3},{3,2},{4,5},{5,4},{6,7},{7,6},{8,9},{9,8},{10,11... | collective-permute-start | bytes 1572872 | tf_op jit(solution)/shard_map/ppermute | solution.py:332
  65.8 6.7 %cube.1 = (f32[256,2048]{1,0:T(8,128)S(1)}, bf16[2,8,2,128,128]{4,3,2,1,0:T(8,128)(2,1)}, bf16[1024,2048]{1,0:T(8,128)(2,1)S(1)}) custom-call(f32[16,128]{1,0:T(8,128)S(1)} %get-tuple-element.26.kept, bf16[256,1024]{1,0:T(8,128)(2,1)S(1)} %get-tuple-element.32.refs_0_, bf16[256,1024]{1,0:T(8,128)(2,1)S(1)} %get-tuple-element.36.refs_1_, ...), custom_call_target="tpu_custom_call" | custom-call | tf_op jit(solution)/shard_map/cube/pallas_call | solution.py:450
  72.5 4.3 %collective-permute-done.33.refs_2_ = bf16[256,1024]{1,0:T(8,128)(2,1)S(1)} collective-permute-done((bf16[256,1024]{1,0:T(8,128)(2,1)S(1)}, bf16[256,1024]{1,0:T(8,128)(2,1)S(1)}, u32[]{:S(2)}, u32[]{:S(2)}) %collective-permute-start.33) | collective-permute-done | bytes 524320 | tf_op jit(solution)/shard_map/ppermute | solution.py:332
  76.8 2.4 %final.1 = bf16[2,8,2,128,128]{4,3,2,1,0:T(8,128)(2,1)} custom-call(f32[16,128]{1,0:T(8,128)S(1)} %get-tuple-element.26.kept, f32[256,2048]{1,0:T(8,128)S(1)} %get-tuple-element.44.acc, bf16[1024,2048]{1,0:T(8,128)(2,1)S(1)} %get-tuple-element.45.later, bf16[256,1024]{1,0:T(8,128)(2,1)S(1)} %get-tuple-element.32.refs_0_, ...), custom_call_target="tpu_custom_call" | custom-call | tf_op jit(solution)/shard_map/final/pallas_call | solution.py:464
  (20 shorter events, 0.0 us)
Async XLA Ops:
  0.6 1.0 %copy-start = (bf16[2,8,1,128,128]{4,3,2,1,0:T(8,128)(2,1)S(1)}, bf16[2,8,1,128,128]{4,3,2,1,0:T(8,128)(2,1)}, u32[]{:S(2)}) copy-start(bf16[2,8,1,128,128]{4,3,2,1,0:T(8,128)(2,1)} %param.3) | copy-start | bytes 1572868
  1.7 0.7 copy-start.2
  3.2 8.8 %collective-permute-start.7 = (bf16[1040,128]{1,0:T(8,128)(2,1)S(1)}, bf16[1040,128]{1,0:T(8,128)(2,1)S(1)}, u32[]{:S(2)}, u32[]{:S(2)}) collective-permute-start(bf16[1040,128]{1,0:T(8,128)(2,1)S(1)} %get-tuple-element.24.refs_0_.refs_1_), channel_id=1, source_target_pairs={{8,0},{6,2},{16,8},{2,10},{24,16},{10,18},{28,24},{18,26},{20,28},... | collective-permute-start | bytes 798728 | tf_op jit(solution)/shard_map/ppermute | solution.py:434
  6.2 9.2 %collective-permute-start.5 = (bf16[1040,128]{1,0:T(8,128)(2,1)S(1)}, bf16[1040,128]{1,0:T(8,128)(2,1)S(1)}, u32[]{:S(2)}, u32[]{:S(2)}) collective-permute-start(bf16[1040,128]{1,0:T(8,128)(2,1)S(1)} %get-tuple-element.24.refs_0_.refs_1_), channel_id=1, source_target_pairs={{0,2},{2,0},{4,6},{6,4},{8,10},{10,8},{12,14},{14,12},{16,18},{18,... | collective-permute-start | bytes 798728 | tf_op jit(solution)/shard_map/ppermute | solution.py:354
  6.2 9.2 %collective-permute-start.2 = (bf16[1040,128]{1,0:T(8,128)(2,1)S(1)}, bf16[1040,128]{1,0:T(8,128)(2,1)S(1)}, u32[]{:S(2)}, u32[]{:S(2)}) collective-permute-start(bf16[1040,128]{1,0:T(8,128)(2,1)S(1)} %get-tuple-element.24.refs_0_.refs_1_), channel_id=1, source_target_pairs={{0,8},{2,6},{8,16},{10,2},{16,24},{18,10},{24,28},{26,18},{28,20},... | collective-permute-start | bytes 798728 | tf_op jit(solution)/shard_map/ppermute | solution.py:434
  7.4 9.6 %collective-permute-start = (bf16[1040,128]{1,0:T(8,128)(2,1)S(1)}, bf16[1040,128]{1,0:T(8,128)(2,1)S(1)}, u32[]{:S(2)}, u32[]{:S(2)}) collective-permute-start(bf16[1040,128]{1,0:T(8,128)(2,1)S(1)} %get-tuple-element.24.refs_0_.refs_1_), channel_id=1, source_target_pairs={{0,1},{1,0},{2,3},{3,2},{4,5},{5,4},{6,7},{7,6},{8,9},{9,8},{10,11... | collective-permute-start | bytes 798728 | tf_op jit(solution)/shard_map/ppermute | solution.py:332
  8.9 9.3 %collective-permute-start.12 = (bf16[1040,128]{1,0:T(8,128)(2,1)S(1)}, bf16[1040,128]{1,0:T(8,128)(2,1)S(1)}, u32[]{:S(2)}, u32[]{:S(2)}) collective-permute-start(bf16[1040,128]{1,0:T(8,128)(2,1)S(1)} %get-tuple-element.25.refs_1_), channel_id=1, source_target_pairs={{8,0},{6,2},{16,8},{2,10},{24,16},{10,18},{28,24},{18,26},{20,28},... | collective-permute-start | bytes 798728 | tf_op jit(solution)/shard_map/ppermute | solution.py:434
  11.9 9.1 %collective-permute-start.10 = (bf16[1040,128]{1,0:T(8,128)(2,1)S(1)}, bf16[1040,128]{1,0:T(8,128)(2,1)S(1)}, u32[]{:S(2)}, u32[]{:S(2)}) collective-permute-start(bf16[1040,128]{1,0:T(8,128)(2,1)S(1)} %get-tuple-element.25.refs_1_), channel_id=1, source_target_pairs={{0,8},{2,6},{8,16},{10,2},{16,24},{18,10},{24,28},{26,18},{28,20},... | collective-permute-start | bytes 798728 | tf_op jit(solution)/shard_map/ppermute | solution.py:434
  15.3 5.7 %collective-permute-start.9 = (bf16[1040,128]{1,0:T(8,128)(2,1)S(1)}, bf16[1040,128]{1,0:T(8,128)(2,1)S(1)}, u32[]{:S(2)}, u32[]{:S(2)}) collective-permute-start(bf16[1040,128]{1,0:T(8,128)(2,1)S(1)} %get-tuple-element.25.refs_1_), channel_id=1, source_target_pairs={{0,2},{2,0},{4,6},{6,4},{8,10},{10,8},{12,14},{14,12},{16,18},{18,... | collective-permute-start | bytes 798728 | tf_op jit(solution)/shard_map/ppermute | solution.py:354
  15.4 8.8 %collective-permute-start.1 = (bf16[1040,128]{1,0:T(8,128)(2,1)S(1)}, bf16[1040,128]{1,0:T(8,128)(2,1)S(1)}, u32[]{:S(2)}, u32[]{:S(2)}) collective-permute-start(bf16[1040,128]{1,0:T(8,128)(2,1)S(1)} %get-tuple-element.25.refs_1_), channel_id=1, source_target_pairs={{0,1},{1,0},{2,3},{3,2},{4,5},{5,4},{6,7},{7,6},{8,9},{9,8},{10,11... | collective-permute-start | bytes 798728 | tf_op jit(solution)/shard_map/ppermute | solution.py:332
  16.9 8.8 %collective-permute-start.17 = (bf16[1040,128]{1,0:T(8,128)(2,1)S(1)}, bf16[1040,128]{1,0:T(8,128)(2,1)S(1)}, u32[]{:S(2)}, u32[]{:S(2)}) collective-permute-start(bf16[1040,128]{1,0:T(8,128)(2,1)S(1)} %collective-permute-done.7.refs_5_), channel_id=1, source_target_pairs={{8,0},{6,2},{16,8},{2,10},{24,16},{10,18},{28,24},{18,26},{20,28},... | collective-permute-start | bytes 798728 | tf_op jit(solution)/shard_map/ppermute | solution.py:434
  18.2 7.6 %collective-permute-start.3 = (bf16[1040,128]{1,0:T(8,128)(2,1)S(1)}, bf16[1040,128]{1,0:T(8,128)(2,1)S(1)}, u32[]{:S(2)}, u32[]{:S(2)}) collective-permute-start(bf16[1040,128]{1,0:T(8,128)(2,1)S(1)} %collective-permute-done.2.refs_3_), channel_id=1, source_target_pairs={{0,8},{2,6},{8,16},{10,2},{16,24},{18,10},{24,28},{26,18},{28,20},... | collective-permute-start | bytes 798728 | tf_op jit(solution)/shard_map/ppermute | solution.py:434
  21.0 6.4 %collective-permute-start.8 = (bf16[1040,128]{1,0:T(8,128)(2,1)S(1)}, bf16[1040,128]{1,0:T(8,128)(2,1)S(1)}, u32[]{:S(2)}, u32[]{:S(2)}) collective-permute-start(bf16[1040,128]{1,0:T(8,128)(2,1)S(1)} %collective-permute-done.7.refs_5_), channel_id=1, source_target_pairs={{0,2},{2,0},{4,6},{6,4},{8,10},{10,8},{12,14},{14,12},{16,18},{18,... | collective-permute-start | bytes 798728 | tf_op jit(solution)/shard_map/ppermute | solution.py:354
  21.1 6.8 %collective-permute-start.13 = (bf16[1040,128]{1,0:T(8,128)(2,1)S(1)}, bf16[1040,128]{1,0:T(8,128)(2,1)S(1)}, u32[]{:S(2)}, u32[]{:S(2)}) collective-permute-start(bf16[1040,128]{1,0:T(8,128)(2,1)S(1)} %collective-permute-done.12.refs_5_), channel_id=1, source_target_pairs={{0,2},{2,0},{4,6},{6,4},{8,10},{10,8},{12,14},{14,12},{16,18},{18,... | collective-permute-start | bytes 798728 | tf_op jit(solution)/shard_map/ppermute | solution.py:354
  24.2 5.3 %collective-permute-start.11 = (bf16[1040,128]{1,0:T(8,128)(2,1)S(1)}, bf16[1040,128]{1,0:T(8,128)(2,1)S(1)}, u32[]{:S(2)}, u32[]{:S(2)}) collective-permute-start(bf16[1040,128]{1,0:T(8,128)(2,1)S(1)} %collective-permute-done.10.refs_3_), channel_id=1, source_target_pairs={{0,2},{2,0},{4,6},{6,4},{8,10},{10,8},{12,14},{14,12},{16,18},{18,... | collective-permute-start | bytes 798728 | tf_op jit(solution)/shard_map/ppermute | solution.py:354
  25.8 6.4 %collective-permute-start.6 = (bf16[1040,128]{1,0:T(8,128)(2,1)S(1)}, bf16[1040,128]{1,0:T(8,128)(2,1)S(1)}, u32[]{:S(2)}, u32[]{:S(2)}) collective-permute-start(bf16[1040,128]{1,0:T(8,128)(2,1)S(1)} %collective-permute-done.2.refs_3_), channel_id=1, source_target_pairs={{0,2},{2,0},{4,6},{6,4},{8,10},{10,8},{12,14},{14,12},{16,18},{18,... | collective-permute-start | bytes 798728 | tf_op jit(solution)/shard_map/ppermute | solution.py:354
  25.8 8.9 %collective-permute-start.4 = (bf16[1040,128]{1,0:T(8,128)(2,1)S(1)}, bf16[1040,128]{1,0:T(8,128)(2,1)S(1)}, u32[]{:S(2)}, u32[]{:S(2)}) collective-permute-start(bf16[1040,128]{1,0:T(8,128)(2,1)S(1)} %collective-permute-done.3.refs_1_), channel_id=1, source_target_pairs={{0,8},{2,6},{8,16},{10,2},{16,24},{18,10},{24,28},{26,18},{28,20},... | collective-permute-start | bytes 798728 | tf_op jit(solution)/shard_map/ppermute | solution.py:434
  27.5 9.3 %collective-permute-start.22 = (bf16[1040,128]{1,0:T(8,128)(2,1)S(1)}, bf16[1040,128]{1,0:T(8,128)(2,1)S(1)}, u32[]{:S(2)}, u32[]{:S(2)}) collective-permute-start(bf16[1040,128]{1,0:T(8,128)(2,1)S(1)} %collective-permute-done.12.refs_5_), channel_id=1, source_target_pairs={{8,0},{6,2},{16,8},{2,10},{24,16},{10,18},{28,24},{18,26},{20,28},... | collective-permute-start | bytes 798728 | tf_op jit(solution)/shard_map/ppermute | solution.py:434
  27.8 12.6 %collective-permute-start.26 = (bf16[1040,128]{1,0:T(8,128)(2,1)S(1)}, bf16[1040,128]{1,0:T(8,128)(2,1)S(1)}, u32[]{:S(2)}, u32[]{:S(2)}) collective-permute-start(bf16[1040,128]{1,0:T(8,128)(2,1)S(1)} %collective-permute-done.10.refs_3_), channel_id=1, source_target_pairs={{0,8},{2,6},{8,16},{10,2},{16,24},{18,10},{24,28},{26,18},{28,20},... | collective-permute-start | bytes 798728 | tf_op jit(solution)/shard_map/ppermute | solution.py:434
  29.5 13.0 %collective-permute-start.20 = (bf16[1040,128]{1,0:T(8,128)(2,1)S(1)}, bf16[1040,128]{1,0:T(8,128)(2,1)S(1)}, u32[]{:S(2)}, u32[]{:S(2)}) collective-permute-start(bf16[1040,128]{1,0:T(8,128)(2,1)S(1)} %collective-permute-done.17.refs_3_), channel_id=1, source_target_pairs={{8,0},{6,2},{16,8},{2,10},{24,16},{10,18},{28,24},{18,26},{20,28},... | collective-permute-start | bytes 798728 | tf_op jit(solution)/shard_map/ppermute | solution.py:434
  29.9 0.7 copy-start.1
  32.2 10.3 %collective-permute-start.18 = (bf16[1040,128]{1,0:T(8,128)(2,1)S(1)}, bf16[1040,128]{1,0:T(8,128)(2,1)S(1)}, u32[]{:S(2)}, u32[]{:S(2)}) collective-permute-start(bf16[1040,128]{1,0:T(8,128)(2,1)S(1)} %collective-permute-done.17.refs_3_), channel_id=1, source_target_pairs={{0,2},{2,0},{4,6},{6,4},{8,10},{10,8},{12,14},{14,12},{16,18},{18,... | collective-permute-start | bytes 798728 | tf_op jit(solution)/shard_map/ppermute | solution.py:354
  34.7 11.4 %collective-permute-start.14 = (bf16[1040,128]{1,0:T(8,128)(2,1)S(1)}, bf16[1040,128]{1,0:T(8,128)(2,1)S(1)}, u32[]{:S(2)}, u32[]{:S(2)}) collective-permute-start(bf16[1040,128]{1,0:T(8,128)(2,1)S(1)} %collective-permute-done.4.refs_5_), channel_id=1, source_target_pairs={{0,8},{2,6},{8,16},{10,2},{16,24},{18,10},{24,28},{26,18},{28,20},... | collective-permute-start | bytes 798728 | tf_op jit(solution)/shard_map/ppermute | solution.py:434
  36.8 9.4 %collective-permute-start.16 = (bf16[1040,128]{1,0:T(8,128)(2,1)S(1)}, bf16[1040,128]{1,0:T(8,128)(2,1)S(1)}, u32[]{:S(2)}, u32[]{:S(2)}) collective-permute-start(bf16[1040,128]{1,0:T(8,128)(2,1)S(1)} %collective-permute-done.3.refs_1_), channel_id=1, source_target_pairs={{0,2},{2,0},{4,6},{6,4},{8,10},{10,8},{12,14},{14,12},{16,18},{18,... | collective-permute-start | bytes 798728 | tf_op jit(solution)/shard_map/ppermute | solution.py:354
  40.4 6.4 %collective-permute-start.23 = (bf16[1040,128]{1,0:T(8,128)(2,1)S(1)}, bf16[1040,128]{1,0:T(8,128)(2,1)S(1)}, u32[]{:S(2)}, u32[]{:S(2)}) collective-permute-start(bf16[1040,128]{1,0:T(8,128)(2,1)S(1)} %collective-permute-done.22.refs_3_), channel_id=1, source_target_pairs={{8,0},{6,2},{16,8},{2,10},{24,16},{10,18},{28,24},{18,26},{20,28},... | collective-permute-start | bytes 798728 | tf_op jit(solution)/shard_map/ppermute | solution.py:434
  42.5 6.0 %collective-permute-start.21 = (bf16[1040,128]{1,0:T(8,128)(2,1)S(1)}, bf16[1040,128]{1,0:T(8,128)(2,1)S(1)}, u32[]{:S(2)}, u32[]{:S(2)}) collective-permute-start(bf16[1040,128]{1,0:T(8,128)(2,1)S(1)} %collective-permute-done.20.refs_7_), channel_id=1, source_target_pairs={{0,2},{2,0},{4,6},{6,4},{8,10},{10,8},{12,14},{14,12},{16,18},{18,... | collective-permute-start | bytes 798728 | tf_op jit(solution)/shard_map/ppermute | solution.py:354
  42.5 6.4 %collective-permute-start.19 = (bf16[1040,128]{1,0:T(8,128)(2,1)S(1)}, bf16[1040,128]{1,0:T(8,128)(2,1)S(1)}, u32[]{:S(2)}, u32[]{:S(2)}) collective-permute-start(bf16[1040,128]{1,0:T(8,128)(2,1)S(1)} %collective-permute-done.4.refs_5_), channel_id=1, source_target_pairs={{0,2},{2,0},{4,6},{6,4},{8,10},{10,8},{12,14},{14,12},{16,18},{18,... | collective-permute-start | bytes 798728 | tf_op jit(solution)/shard_map/ppermute | solution.py:354
  46.2 4.1 %collective-permute-start.15 = (bf16[1040,128]{1,0:T(8,128)(2,1)S(1)}, bf16[1040,128]{1,0:T(8,128)(2,1)S(1)}, u32[]{:S(2)}, u32[]{:S(2)}) collective-permute-start(bf16[1040,128]{1,0:T(8,128)(2,1)S(1)} %collective-permute-done.14.refs_1_), channel_id=1, source_target_pairs={{0,2},{2,0},{4,6},{6,4},{8,10},{10,8},{12,14},{14,12},{16,18},{18,... | collective-permute-start | bytes 798728 | tf_op jit(solution)/shard_map/ppermute | solution.py:354
  46.2 5.9 %collective-permute-start.28 = (bf16[1040,128]{1,0:T(8,128)(2,1)S(1)}, bf16[1040,128]{1,0:T(8,128)(2,1)S(1)}, u32[]{:S(2)}, u32[]{:S(2)}) collective-permute-start(bf16[1040,128]{1,0:T(8,128)(2,1)S(1)} %collective-permute-done.22.refs_3_), channel_id=1, source_target_pairs={{0,2},{2,0},{4,6},{6,4},{8,10},{10,8},{12,14},{14,12},{16,18},{18,... | collective-permute-start | bytes 798728 | tf_op jit(solution)/shard_map/ppermute | solution.py:354
  46.9 8.7 %collective-permute-start.29 = (bf16[1040,128]{1,0:T(8,128)(2,1)S(1)}, bf16[1040,128]{1,0:T(8,128)(2,1)S(1)}, u32[]{:S(2)}, u32[]{:S(2)}) collective-permute-start(bf16[1040,128]{1,0:T(8,128)(2,1)S(1)} %collective-permute-done.26.refs_1_), channel_id=1, source_target_pairs={{0,8},{2,6},{8,16},{10,2},{16,24},{18,10},{24,28},{26,18},{28,20},... | collective-permute-start | bytes 798728 | tf_op jit(solution)/shard_map/ppermute | solution.py:434
  48.5 7.1 %collective-permute-start.24 = (bf16[1040,128]{1,0:T(8,128)(2,1)S(1)}, bf16[1040,128]{1,0:T(8,128)(2,1)S(1)}, u32[]{:S(2)}, u32[]{:S(2)}) collective-permute-start(bf16[1040,128]{1,0:T(8,128)(2,1)S(1)} %collective-permute-done.23.refs_7_), channel_id=1, source_target_pairs={{8,0},{6,2},{16,8},{2,10},{24,16},{10,18},{28,24},{18,26},{20,28},... | collective-permute-start | bytes 798728 | tf_op jit(solution)/shard_map/ppermute | solution.py:434
  50.8 13.2 %collective-permute-start.32 = (bf16[256,1024]{1,0:T(8,128)(2,1)S(1)}, bf16[256,1024]{1,0:T(8,128)(2,1)S(1)}, u32[]{:S(2)}, u32[]{:S(2)}) collective-permute-start(bf16[256,1024]{1,0:T(8,128)(2,1)S(1)} %get-tuple-element.32.refs_0_), channel_id=1, source_target_pairs={{0,1},{1,0},{2,3},{3,2},{4,5},{5,4},{6,7},{7,6},{8,9},{9,8},{10,11... | collective-permute-start | bytes 1572872 | tf_op jit(solution)/shard_map/ppermute | solution.py:332
  52.0 4.1 %collective-permute-start.27 = (bf16[1040,128]{1,0:T(8,128)(2,1)S(1)}, bf16[1040,128]{1,0:T(8,128)(2,1)S(1)}, u32[]{:S(2)}, u32[]{:S(2)}) collective-permute-start(bf16[1040,128]{1,0:T(8,128)(2,1)S(1)} %collective-permute-done.26.refs_1_), channel_id=1, source_target_pairs={{0,2},{2,0},{4,6},{6,4},{8,10},{10,8},{12,14},{14,12},{16,18},{18,... | collective-permute-start | bytes 798728 | tf_op jit(solution)/shard_map/ppermute | solution.py:354
  52.0 4.1 %collective-permute-start.31 = (bf16[1040,128]{1,0:T(8,128)(2,1)S(1)}, bf16[1040,128]{1,0:T(8,128)(2,1)S(1)}, u32[]{:S(2)}, u32[]{:S(2)}) collective-permute-start(bf16[1040,128]{1,0:T(8,128)(2,1)S(1)} %collective-permute-done.23.refs_7_), channel_id=1, source_target_pairs={{0,2},{2,0},{4,6},{6,4},{8,10},{10,8},{12,14},{14,12},{16,18},{18,... | collective-permute-start | bytes 798728 | tf_op jit(solution)/shard_map/ppermute | solution.py:354
  55.6 1.5 %collective-permute-start.30 = (bf16[1040,128]{1,0:T(8,128)(2,1)S(1)}, bf16[1040,128]{1,0:T(8,128)(2,1)S(1)}, u32[]{:S(2)}, u32[]{:S(2)}) collective-permute-start(bf16[1040,128]{1,0:T(8,128)(2,1)S(1)} %collective-permute-done.29.refs_5_), channel_id=1, source_target_pairs={{0,2},{2,0},{4,6},{6,4},{8,10},{10,8},{12,14},{14,12},{16,18},{18,... | collective-permute-start | bytes 798728 | tf_op jit(solution)/shard_map/ppermute | solution.py:354
  55.6 8.4 %collective-permute-start.25 = (bf16[1040,128]{1,0:T(8,128)(2,1)S(1)}, bf16[1040,128]{1,0:T(8,128)(2,1)S(1)}, u32[]{:S(2)}, u32[]{:S(2)}) collective-permute-start(bf16[1040,128]{1,0:T(8,128)(2,1)S(1)} %collective-permute-done.24.refs_1_), channel_id=1, source_target_pairs={{0,2},{2,0},{4,6},{6,4},{8,10},{10,8},{12,14},{14,12},{16,18},{18,... | collective-permute-start | bytes 798728 | tf_op jit(solution)/shard_map/ppermute | solution.py:354
  64.5 12.3 %collective-permute-start.33 = (bf16[256,1024]{1,0:T(8,128)(2,1)S(1)}, bf16[256,1024]{1,0:T(8,128)(2,1)S(1)}, u32[]{:S(2)}, u32[]{:S(2)}) collective-permute-start(bf16[256,1024]{1,0:T(8,128)(2,1)S(1)} %get-tuple-element.36.refs_1_), channel_id=1, source_target_pairs={{0,1},{1,0},{2,3},{3,2},{4,5},{5,4},{6,7},{7,6},{8,9},{9,8},{10,11... | collective-permute-start | bytes 1572872 | tf_op jit(solution)/shard_map/ppermute | solution.py:332

commit v5 on v4

--- a/solution.py
+++ b/solution.py
@@ -275,10 +275,11 @@
     chunks = len(sizes)
     own = refs[:chunks]
     received = refs[chunks : chunks + groups - 1]
-    purified = refs[-1]
+    purified, staged, sems = refs[-3:]
     dense = width * tile
     panels = sum(sizes)
     span = sizes[-1] * dense
+    copies = []
     first = 0
     for size, source in zip(sizes, own):
         columns = slice(first * dense, (first + size) * dense)
@@ -296,9 +297,17 @@
                     local * tile : (local + 1) * tile, panel * dense : (panel + 1) * dense
                 ]
                 a, b = ordered(kept, local * panels + first + panel, part, tile)
-                purified[local, first + panel, 0] = a.astype(purified.dtype)
-                purified[local, first + panel, 1] = b.astype(purified.dtype)
+                staged[local, first + panel, 0] = a.astype(staged.dtype)
+                staged[local, first + panel, 1] = b.astype(staged.dtype)
+        for local in range(width):
+            where = (local, pl.ds(first, size))
+            copies.append(
+                pltpu.make_async_copy(staged.at[where], purified.at[where], sems.at[len(copies)])
+            )
+            copies[-1].start()
         first += size
+    for copy in copies:
+        copy.wait()
 
 
 def vmem(count):
@@ -429,6 +438,8 @@
             for ahead in (True, False):
                 if hop == hops and ahead == (chunk == 1):
                     continue
+                if chunk > 0 and hop >= hops - 1:
+                    continue
                 value = after(moved[chunk][ahead][-1], *gates.get(hop, []))
                 moved[chunk][ahead].append(
                     lax.ppermute(value, "row", forward if ahead else backward)
@@ -438,11 +449,17 @@
         for part in range(1, len(groups_of)):
             for past in groups_of[part]:
                 swap(chunk, past)
-            if chunk > 0 and part == len(groups_of) - 1:
-                totals[chunk][-1] = after(totals[chunk][-1], *received[0])
             multiply(chunk, part)
         squares.append(totals[chunk][-1])
-        received.append([across(squares[-1], shift) for shift in range(1, groups)])
+        for hop, ahead in ((hops - 1, True), (hops - 1, False), (hops, False)):
+            if chunk == 0:
+                waits = gates.get(hop, []) + (squares[:1] if ahead else [])
+                value = after(moved[1][ahead][-1], *waits)
+                moved[1][ahead].append(
+                    lax.ppermute(value, "row", forward if ahead else backward)
+                )
+        ready = after(squares[-1], *received[0]) if chunk > 0 else squares[-1]
+        received.append([across(ready, shift) for shift in range(1, groups)])
     rights = [right for some in rights for right in some]
 
     already = [part[shift] for shift in range(groups - 1) for part in received[:-1]]
@@ -465,7 +482,11 @@
         functools.partial(final_kernel, sizes, groups, width, tile),
         out_shape=jax.ShapeDtypeStruct((width, panels, 2, tile, tile), bf16),
         in_specs=vmem(3 + len(squares) + groups - 1),
-        out_specs=vmem(1)[0],
+        out_specs=anywhere(1)[0],
+        scratch_shapes=[
+            pltpu.VMEM((width, panels, 2, tile, tile), bf16),
+            pltpu.SemaphoreType.DMA((width * len(sizes),)),
+        ],
         compiler_params=params(8),
         name="final",
     )(kept, acc, later, *squares, *received[-1])

time: 79.4 us -> 78.2 us (0.985)
    ppermute x4, waiting for transfers between devices: 12.3 us -> 9.45 us  [across(): return lax.ppermute(value, 'col', pairs)]
    ppermute x14, waiting for transfers between devices: 17.4 us -> 19.6 us  [shards(): lax.ppermute(value, 'row', forward if ahead else backward)]
  transfers between devices with their start and end apart: 34 -> 34, of which waited for: 14 -> 12; matrix products, arithmetic and copies ran while one was open for 0% -> 0% of each run, Pallas kernels for 16% -> 17%
where the time goes in v5:
time: 78.2 us; the launch traced here: 78 us
  waiting for transfers between devices  30.1 us (38%)
  starting transfers between devices  28.3 us (36%)
  Pallas kernels  16.2 us (21%)
  local copies, waits for them, and re-layouts  2.39 us (3%)
  between operations  0.93 us (1%)
    ppermute x14, starting transfers between devices, shards(): lax.ppermute(value, 'row', forward if ahead else backward)  20.3 us
    ppermute x14, waiting for transfers between devices, shards(): lax.ppermute(value, 'row', forward if ahead else backward)  19.6 us
    ppermute x4, waiting for transfers between devices, across(): return lax.ppermute(value, 'col', pairs)  9.45 us
    pallas_call x1, Pallas kernels, shards(): pl.pallas_call(functools.partial(cube_kernel, sizes, rows, groups, width,...  6.69 us
    ppermute x4, starting transfers between devices, across(): return lax.ppermute(value, 'col', pairs)  6.05 us
    pallas_call x6, Pallas kernels, square_of(): pl.pallas_call(functools.partial(square_kernel, size, width, tile, start,...  5.87 us
    unnamed x6, local copies, waits for them, and re-layouts  2.39 us
    pallas_call x1, Pallas kernels, shards(): pl.pallas_call(functools.partial(final_kernel, sizes, groups, width, tile...  2.25 us
  transfers between devices with their start and end apart: 34, of which 12 were waited for; matrix products, arithmetic and copies ran while one was open for 0% of the time, Pallas kernels for 17%

profile of v5, /device:TPU:0, one launch (start us, length us, event | category | flops | bytes accessed | tf_op | source)
XLA Modules:
  0.0 78.0 jit_solution(14986374994121779370)
XLA Ops:
  0.6 1.0 %copy-done = bf16[2,8,1,128,128]{4,3,2,1,0:T(8,128)(2,1)S(1)} copy-done((bf16[2,8,1,128,128]{4,3,2,1,0:T(8,128)(2,1)S(1)}, bf16[2,8,1,128,128]{4,3,2,1,0:T(8,128)(2,1)}, u32[]{:S(2)}) %copy-start) | copy-done | bytes 524312
  1.7 0.7 copy-done.2
  2.4 0.8 %pack.1 = (bf16[1040,128]{1,0:T(8,128)(2,1)S(1)}, bf16[1040,128]{1,0:T(8,128)(2,1)S(1)}) custom-call(s32[2,8]{1,0:T(2,128)S(1)} %bitcast.7, bf16[2,1024,128]{2,1,0:T(8,128)(2,1)S(1)} %bitcast.5), custom_call_target="tpu_custom_call" | custom-call | tf_op jit(solution)/shard_map/pack/pallas_call | solution.py:346
  3.2 3.0 %collective-permute-start.7 = (bf16[1040,128]{1,0:T(8,128)(2,1)S(1)}, bf16[1040,128]{1,0:T(8,128)(2,1)S(1)}, u32[]{:S(2)}, u32[]{:S(2)}) collective-permute-start(bf16[1040,128]{1,0:T(8,128)(2,1)S(1)} %get-tuple-element.25.refs_0_.refs_1_), channel_id=1, source_target_pairs={{8,0},{6,2},{16,8},{2,10},{24,16},{10,18},{28,24},{18,26},{20,28},... | collective-permute-start | bytes 798728 | tf_op jit(solution)/shard_map/ppermute | solution.py:445
  6.2 0.0 collective-permute-start.5
  6.2 1.2 %collective-permute-start.2 = (bf16[1040,128]{1,0:T(8,128)(2,1)S(1)}, bf16[1040,128]{1,0:T(8,128)(2,1)S(1)}, u32[]{:S(2)}, u32[]{:S(2)}) collective-permute-start(bf16[1040,128]{1,0:T(8,128)(2,1)S(1)} %get-tuple-element.25.refs_0_.refs_1_), channel_id=1, source_target_pairs={{0,8},{2,6},{8,16},{10,2},{16,24},{18,10},{24,28},{26,18},{28,20},... | collective-permute-start | bytes 798728 | tf_op jit(solution)/shard_map/ppermute | solution.py:445
  7.4 1.5 %collective-permute-start = (bf16[1040,128]{1,0:T(8,128)(2,1)S(1)}, bf16[1040,128]{1,0:T(8,128)(2,1)S(1)}, u32[]{:S(2)}, u32[]{:S(2)}) collective-permute-start(bf16[1040,128]{1,0:T(8,128)(2,1)S(1)} %get-tuple-element.25.refs_0_.refs_1_), channel_id=1, source_target_pairs={{0,1},{1,0},{2,3},{3,2},{4,5},{5,4},{6,7},{7,6},{8,9},{9,8},{10,11... | collective-permute-start | bytes 798728 | tf_op jit(solution)/shard_map/ppermute | solution.py:341
  8.9 0.8 %collective-permute-start.12 = (bf16[1040,128]{1,0:T(8,128)(2,1)S(1)}, bf16[1040,128]{1,0:T(8,128)(2,1)S(1)}, u32[]{:S(2)}, u32[]{:S(2)}) collective-permute-start(bf16[1040,128]{1,0:T(8,128)(2,1)S(1)} %get-tuple-element.26.refs_1_), channel_id=1, source_target_pairs={{8,0},{6,2},{16,8},{2,10},{24,16},{10,18},{28,24},{18,26},{20,28},... | collective-permute-start | bytes 798728 | tf_op jit(solution)/shard_map/ppermute | solution.py:445
  9.7 2.2 %collective-permute-done.7.refs_5_ = bf16[1040,128]{1,0:T(8,128)(2,1)S(1)} collective-permute-done((bf16[1040,128]{1,0:T(8,128)(2,1)S(1)}, bf16[1040,128]{1,0:T(8,128)(2,1)S(1)}, u32[]{:S(2)}, u32[]{:S(2)}) %collective-permute-start.7) | collective-permute-done | bytes 266272 | tf_op jit(solution)/shard_map/ppermute | solution.py:445
  11.9 3.4 %collective-permute-start.10 = (bf16[1040,128]{1,0:T(8,128)(2,1)S(1)}, bf16[1040,128]{1,0:T(8,128)(2,1)S(1)}, u32[]{:S(2)}, u32[]{:S(2)}) collective-permute-start(bf16[1040,128]{1,0:T(8,128)(2,1)S(1)} %get-tuple-element.26.refs_1_), channel_id=1, source_target_pairs={{0,8},{2,6},{8,16},{10,2},{16,24},{18,10},{24,28},{26,18},{28,20},... | collective-permute-start | bytes 798728 | tf_op jit(solution)/shard_map/ppermute | solution.py:445
  15.3 0.0 collective-permute-done.5.refs_2_
  15.4 1.6 %collective-permute-start.1 = (bf16[1040,128]{1,0:T(8,128)(2,1)S(1)}, bf16[1040,128]{1,0:T(8,128)(2,1)S(1)}, u32[]{:S(2)}, u32[]{:S(2)}) collective-permute-start(bf16[1040,128]{1,0:T(8,128)(2,1)S(1)} %get-tuple-element.26.refs_1_), channel_id=1, source_target_pairs={{0,1},{1,0},{2,3},{3,2},{4,5},{5,4},{6,7},{7,6},{8,9},{9,8},{10,11... | collective-permute-start | bytes 798728 | tf_op jit(solution)/shard_map/ppermute | solution.py:341
  16.9 0.0 collective-permute-done.refs_2_
  16.9 1.6 %collective-permute-start.3 = (bf16[1040,128]{1,0:T(8,128)(2,1)S(1)}, bf16[1040,128]{1,0:T(8,128)(2,1)S(1)}, u32[]{:S(2)}, u32[]{:S(2)}) collective-permute-start(bf16[1040,128]{1,0:T(8,128)(2,1)S(1)} %collective-permute-done.2.refs_3_), channel_id=1, source_target_pairs={{0,8},{2,6},{8,16},{10,2},{16,24},{18,10},{24,28},{26,18},{28,20},... | collective-permute-start | bytes 798728 | tf_op jit(solution)/shard_map/ppermute | solution.py:445
  18.5 0.0 collective-permute-done.12.refs_5_
  18.5 0.8 collective-permute-done.10.refs_3_
  19.3 0.0 collective-permute-start.11
  19.3 0.0 collective-permute-done.9.refs_2_
  19.3 1.9 %collective-permute-start.17 = (bf16[1040,128]{1,0:T(8,128)(2,1)S(1)}, bf16[1040,128]{1,0:T(8,128)(2,1)S(1)}, u32[]{:S(2)}, u32[]{:S(2)}) collective-permute-start(bf16[1040,128]{1,0:T(8,128)(2,1)S(1)} %collective-permute-done.7.refs_5_), channel_id=1, source_target_pairs={{8,0},{6,2},{16,8},{2,10},{24,16},{10,18},{28,24},{18,26},{20,28},... | collective-permute-start | bytes 798728 | tf_op jit(solution)/shard_map/ppermute | solution.py:445
  21.2 2.9 %collective-permute-done.1.refs_3_ = bf16[1040,128]{1,0:T(8,128)(2,1)S(1)} collective-permute-done((bf16[1040,128]{1,0:T(8,128)(2,1)S(1)}, bf16[1040,128]{1,0:T(8,128)(2,1)S(1)}, u32[]{:S(2)}, u32[]{:S(2)}) %collective-permute-start.1) | collective-permute-done | bytes 266272 | tf_op jit(solution)/shard_map/ppermute | solution.py:341
  24.2 0.0 collective-permute-start.8
  24.2 0.1 collective-permute-done.3.refs_1_
  24.3 0.4 collective-permute-start.6
  24.7 0.0 collective-permute-done.13.refs_6_
  24.7 1.6 %collective-permute-start.4 = (bf16[1040,128]{1,0:T(8,128)(2,1)S(1)}, bf16[1040,128]{1,0:T(8,128)(2,1)S(1)}, u32[]{:S(2)}, u32[]{:S(2)}) collective-permute-start(bf16[1040,128]{1,0:T(8,128)(2,1)S(1)} %collective-permute-done.3.refs_1_), channel_id=1, source_target_pairs={{0,8},{2,6},{8,16},{10,2},{16,24},{18,10},{24,28},{26,18},{28,20},... | collective-permute-start | bytes 798728 | tf_op jit(solution)/shard_map/ppermute | solution.py:445
  26.3 0.4 collective-permute-start.22
  26.7 0.7 copy-done.1
  27.4 0.6 left.1
  28.0 1.1 %square.7 = (f32[256,1024]{1,0:T(8,128)S(1)}, bf16[1536,1024]{1,0:T(8,128)(2,1)S(1)}) custom-call(bf16[256,4096]{1,0:T(8,128)(2,1)S(1)} %get-tuple-element.28.refs_0_, bf16[1040,128]{1,0:T(8,128)(2,1)S(1)} %get-tuple-element.26.refs_1_, bf16[1040,128]{1,0:T(8,128)(2,1)S(1)} %collective-permute-done.9.refs_2_, ...), custom_call_target="tpu_custom_call" | custom-call | tf_op jit(solution)/shard_map/square/pallas_call | solution.py:381
  29.1 0.0 collective-permute-done.17.refs_3_
  29.1 0.9 %collective-permute-start.20 = (bf16[1040,128]{1,0:T(8,128)(2,1)S(1)}, bf16[1040,128]{1,0:T(8,128)(2,1)S(1)}, u32[]{:S(2)}, u32[]{:S(2)}) collective-permute-start(bf16[1040,128]{1,0:T(8,128)(2,1)S(1)} %collective-permute-done.17.refs_3_), channel_id=1, source_target_pairs={{8,0},{6,2},{16,8},{2,10},{24,16},{10,18},{28,24},{18,26},{20,28},... | collective-permute-start | bytes 798728 | tf_op jit(solution)/shard_map/ppermute | solution.py:445
  30.0 1.1 %square.6 = (f32[256,1024]{1,0:T(8,128)S(1)}, bf16[1536,1024]{1,0:T(8,128)(2,1)S(1)}) custom-call(bf16[256,4096]{1,0:T(8,128)(2,1)S(1)} %get-tuple-element.28.refs_0_, bf16[1040,128]{1,0:T(8,128)(2,1)S(1)} %get-tuple-element.25.refs_0_.refs_1_, bf16[1040,128]{1,0:T(8,128)(2,1)S(1)} %collective-permute-done.5.refs_2_, ...), custom_call_target="tpu_custom_call" | custom-call | tf_op jit(solution)/shard_map/square/pallas_call | solution.py:381
  31.0 2.9 %collective-permute-done.4.refs_5_ = bf16[1040,128]{1,0:T(8,128)(2,1)S(1)} collective-permute-done((bf16[1040,128]{1,0:T(8,128)(2,1)S(1)}, bf16[1040,128]{1,0:T(8,128)(2,1)S(1)}, u32[]{:S(2)}, u32[]{:S(2)}) %collective-permute-start.4) | collective-permute-done | bytes 266272 | tf_op jit(solution)/shard_map/ppermute | solution.py:445
  33.9 1.5 %collective-permute-start.14 = (bf16[1040,128]{1,0:T(8,128)(2,1)S(1)}, bf16[1040,128]{1,0:T(8,128)(2,1)S(1)}, u32[]{:S(2)}, u32[]{:S(2)}) collective-permute-start(bf16[1040,128]{1,0:T(8,128)(2,1)S(1)} %collective-permute-done.4.refs_5_), channel_id=1, source_target_pairs={{0,8},{2,6},{8,16},{10,2},{16,24},{18,10},{24,28},{26,18},{28,20},... | collective-permute-start | bytes 798728 | tf_op jit(solution)/shard_map/ppermute | solution.py:445
  35.5 0.5 collective-permute-start.23
  36.0 1.6 %collective-permute-done.20.refs_7_ = bf16[1040,128]{1,0:T(8,128)(2,1)S(1)} collective-permute-done((bf16[1040,128]{1,0:T(8,128)(2,1)S(1)}, bf16[1040,128]{1,0:T(8,128)(2,1)S(1)}, u32[]{:S(2)}, u32[]{:S(2)}) %collective-permute-start.20) | collective-permute-done | bytes 266272 | tf_op jit(solution)/shard_map/ppermute | solution.py:445
  37.6 0.0 collective-permute-start.21
  37.6 0.0 collective-permute-done.18.refs_4_
  37.6 0.5 collective-permute-start.19
  38.1 4.1 %collective-permute-done.14.refs_1_ = bf16[1040,128]{1,0:T(8,128)(2,1)S(1)} collective-permute-done((bf16[1040,128]{1,0:T(8,128)(2,1)S(1)}, bf16[1040,128]{1,0:T(8,128)(2,1)S(1)}, u32[]{:S(2)}, u32[]{:S(2)}) %collective-permute-start.14) | collective-permute-done | bytes 266272 | tf_op jit(solution)/shard_map/ppermute | solution.py:445
  42.2 1.4 %collective-permute-start.26 = (bf16[1040,128]{1,0:T(8,128)(2,1)S(1)}, bf16[1040,128]{1,0:T(8,128)(2,1)S(1)}, u32[]{:S(2)}, u32[]{:S(2)}) collective-permute-start(bf16[1040,128]{1,0:T(8,128)(2,1)S(1)} %collective-permute-done.10.refs_3_), channel_id=1, source_target_pairs={{0,8},{2,6},{8,16},{10,2},{16,24},{18,10},{24,28},{26,18},{28,20},... | collective-permute-start | bytes 798728 | tf_op jit(solution)/shard_map/ppermute | solution.py:445
  43.6 0.0 collective-permute-done.16.refs_2_
  43.6 0.0 collective-permute-start.28
  43.6 0.0 collective-permute-done.19.refs_6_
  43.6 1.4 %square.8 = (f32[256,1024]{1,0:T(8,128)S(1)}, bf16[2048,1024]{1,0:T(8,128)(2,1)S(1)}) custom-call(bf16[256,4096]{1,0:T(8,128)(2,1)S(1)} %get-tuple-element.28.refs_0_, bf16[1040,128]{1,0:T(8,128)(2,1)S(1)} %collective-permute-done.3.refs_1_, bf16[1040,128]{1,0:T(8,128)(2,1)S(1)} %collective-permute-done.16.refs_2_, ...), custom_call_target="tpu_custom_call" | custom-call | tf_op jit(solution)/shard_map/square/pallas_call | solution.py:381
  45.0 0.0 collective-permute-done.15.refs_2_
  45.0 0.5 square.9
  45.5 3.1 %collective-permute-done.26.refs_1_ = bf16[1040,128]{1,0:T(8,128)(2,1)S(1)} collective-permute-done((bf16[1040,128]{1,0:T(8,128)(2,1)S(1)}, bf16[1040,128]{1,0:T(8,128)(2,1)S(1)}, u32[]{:S(2)}, u32[]{:S(2)}) %collective-permute-start.26) | collective-permute-done | bytes 266272 | tf_op jit(solution)/shard_map/ppermute | solution.py:445
  48.6 1.4 %collective-permute-start.29 = (bf16[1040,128]{1,0:T(8,128)(2,1)S(1)}, bf16[1040,128]{1,0:T(8,128)(2,1)S(1)}, u32[]{:S(2)}, u32[]{:S(2)}) collective-permute-start(bf16[1040,128]{1,0:T(8,128)(2,1)S(1)} %collective-permute-done.26.refs_1_), channel_id=1, source_target_pairs={{0,8},{2,6},{8,16},{10,2},{16,24},{18,10},{24,28},{26,18},{28,20},... | collective-permute-start | bytes 798728 | tf_op jit(solution)/shard_map/ppermute | solution.py:459
  50.0 0.6 collective-permute-start.24
  50.6 1.5 %collective-permute-start.32 = (bf16[256,1024]{1,0:T(8,128)(2,1)S(1)}, bf16[256,1024]{1,0:T(8,128)(2,1)S(1)}, u32[]{:S(2)}, u32[]{:S(2)}) collective-permute-start(bf16[256,1024]{1,0:T(8,128)(2,1)S(1)} %get-tuple-element.33.refs_0_), channel_id=1, source_target_pairs={{0,1},{1,0},{2,3},{3,2},{4,5},{5,4},{6,7},{7,6},{8,9},{9,8},{10,11... | collective-permute-start | bytes 1572872 | tf_op jit(solution)/shard_map/ppermute | solution.py:341
  52.1 0.0 collective-permute-start.27
  52.1 0.0 collective-permute-done.28.refs_4_
  52.1 0.5 collective-permute-start.31
  52.6 4.8 %collective-permute-done.29.refs_5_ = bf16[1040,128]{1,0:T(8,128)(2,1)S(1)} collective-permute-done((bf16[1040,128]{1,0:T(8,128)(2,1)S(1)}, bf16[1040,128]{1,0:T(8,128)(2,1)S(1)}, u32[]{:S(2)}, u32[]{:S(2)}) %collective-permute-start.29) | collective-permute-done | bytes 266272 | tf_op jit(solution)/shard_map/ppermute | solution.py:459
  57.4 0.5 collective-permute-start.25
  57.9 1.0 %collective-permute-done.30.refs_6_ = bf16[1040,128]{1,0:T(8,128)(2,1)S(1)} collective-permute-done((bf16[1040,128]{1,0:T(8,128)(2,1)S(1)}, bf16[1040,128]{1,0:T(8,128)(2,1)S(1)}, u32[]{:S(2)}, u32[]{:S(2)}) %collective-permute-start.30) | collective-permute-done | bytes 266272 | tf_op jit(solution)/shard_map/ppermute | solution.py:363
  59.0 1.4 %square.10 = (f32[256,1024]{1,0:T(8,128)S(1)}, bf16[2048,1024]{1,0:T(8,128)(2,1)S(1)}) custom-call(bf16[256,4096]{1,0:T(8,128)(2,1)S(1)} %get-tuple-element.28.refs_0_, bf16[1040,128]{1,0:T(8,128)(2,1)S(1)} %collective-permute-done.26.refs_1_, bf16[1040,128]{1,0:T(8,128)(2,1)S(1)} %collective-permute-done.27.refs_2_, ...), custom_call_target="tpu_custom_call" | custom-call | tf_op jit(solution)/shard_map/square/pallas_call | solution.py:381
  60.3 0.5 square.11
  60.8 2.7 %collective-permute-done.32.refs_2_ = bf16[256,1024]{1,0:T(8,128)(2,1)S(1)} collective-permute-done((bf16[256,1024]{1,0:T(8,128)(2,1)S(1)}, bf16[256,1024]{1,0:T(8,128)(2,1)S(1)}, u32[]{:S(2)}, u32[]{:S(2)}) %collective-permute-start.32) | collective-permute-done | bytes 524320 | tf_op jit(solution)/shard_map/ppermute | solution.py:341
  63.5 1.5 %collective-permute-start.33 = (bf16[256,1024]{1,0:T(8,128)(2,1)S(1)}, bf16[256,1024]{1,0:T(8,128)(2,1)S(1)}, u32[]{:S(2)}, u32[]{:S(2)}) collective-permute-start(bf16[256,1024]{1,0:T(8,128)(2,1)S(1)} %get-tuple-element.47.refs_1_), channel_id=1, source_target_pairs={{0,1},{1,0},{2,3},{3,2},{4,5},{5,4},{6,7},{7,6},{8,9},{9,8},{10,11... | collective-permute-start | bytes 1572872 | tf_op jit(solution)/shard_map/ppermute | solution.py:341
  65.0 6.7 %cube.1 = (f32[256,2048]{1,0:T(8,128)S(1)}, bf16[2,8,2,128,128]{4,3,2,1,0:T(8,128)(2,1)}, bf16[1024,2048]{1,0:T(8,128)(2,1)S(1)}) custom-call(f32[16,128]{1,0:T(8,128)S(1)} %get-tuple-element.27.kept, bf16[256,1024]{1,0:T(8,128)(2,1)S(1)} %get-tuple-element.33.refs_0_, bf16[256,1024]{1,0:T(8,128)(2,1)S(1)} %get-tuple-element.47.refs_1_, ...), custom_call_target="tpu_custom_call" | custom-call | tf_op jit(solution)/shard_map/cube/pallas_call | solution.py:467
  71.7 3.8 %collective-permute-done.33.refs_2_ = bf16[256,1024]{1,0:T(8,128)(2,1)S(1)} collective-permute-done((bf16[256,1024]{1,0:T(8,128)(2,1)S(1)}, bf16[256,1024]{1,0:T(8,128)(2,1)S(1)}, u32[]{:S(2)}, u32[]{:S(2)}) %collective-permute-start.33) | collective-permute-done | bytes 524320 | tf_op jit(solution)/shard_map/ppermute | solution.py:341
  75.5 2.3 %final.1 = bf16[2,8,2,128,128]{4,3,2,1,0:T(8,128)(2,1)} custom-call(f32[16,128]{1,0:T(8,128)S(1)} %get-tuple-element.27.kept, f32[256,2048]{1,0:T(8,128)S(1)} %get-tuple-element.45.acc, bf16[1024,2048]{1,0:T(8,128)(2,1)S(1)} %get-tuple-element.46.later, bf16[256,1024]{1,0:T(8,128)(2,1)S(1)} %get-tuple-element.33.refs_0_, ...), custom_call_target="tpu_custom_call" | custom-call | tf_op jit(solution)/shard_map/final/pallas_call | solution.py:481
  (20 shorter events, 0.0 us)
Async XLA Ops:
  0.6 1.0 %copy-start = (bf16[2,8,1,128,128]{4,3,2,1,0:T(8,128)(2,1)S(1)}, bf16[2,8,1,128,128]{4,3,2,1,0:T(8,128)(2,1)}, u32[]{:S(2)}) copy-start(bf16[2,8,1,128,128]{4,3,2,1,0:T(8,128)(2,1)} %param.3) | copy-start | bytes 1572868
  1.7 0.7 copy-start.2
  3.2 8.8 %collective-permute-start.7 = (bf16[1040,128]{1,0:T(8,128)(2,1)S(1)}, bf16[1040,128]{1,0:T(8,128)(2,1)S(1)}, u32[]{:S(2)}, u32[]{:S(2)}) collective-permute-start(bf16[1040,128]{1,0:T(8,128)(2,1)S(1)} %get-tuple-element.25.refs_0_.refs_1_), channel_id=1, source_target_pairs={{8,0},{6,2},{16,8},{2,10},{24,16},{10,18},{28,24},{18,26},{20,28},... | collective-permute-start | bytes 798728 | tf_op jit(solution)/shard_map/ppermute | solution.py:445
  6.2 9.2 %collective-permute-start.5 = (bf16[1040,128]{1,0:T(8,128)(2,1)S(1)}, bf16[1040,128]{1,0:T(8,128)(2,1)S(1)}, u32[]{:S(2)}, u32[]{:S(2)}) collective-permute-start(bf16[1040,128]{1,0:T(8,128)(2,1)S(1)} %get-tuple-element.25.refs_0_.refs_1_), channel_id=1, source_target_pairs={{0,2},{2,0},{4,6},{6,4},{8,10},{10,8},{12,14},{14,12},{16,18},{18,... | collective-permute-start | bytes 798728 | tf_op jit(solution)/shard_map/ppermute | solution.py:363
  6.2 9.2 %collective-permute-start.2 = (bf16[1040,128]{1,0:T(8,128)(2,1)S(1)}, bf16[1040,128]{1,0:T(8,128)(2,1)S(1)}, u32[]{:S(2)}, u32[]{:S(2)}) collective-permute-start(bf16[1040,128]{1,0:T(8,128)(2,1)S(1)} %get-tuple-element.25.refs_0_.refs_1_), channel_id=1, source_target_pairs={{0,8},{2,6},{8,16},{10,2},{16,24},{18,10},{24,28},{26,18},{28,20},... | collective-permute-start | bytes 798728 | tf_op jit(solution)/shard_map/ppermute | solution.py:445
  7.4 9.6 %collective-permute-start = (bf16[1040,128]{1,0:T(8,128)(2,1)S(1)}, bf16[1040,128]{1,0:T(8,128)(2,1)S(1)}, u32[]{:S(2)}, u32[]{:S(2)}) collective-permute-start(bf16[1040,128]{1,0:T(8,128)(2,1)S(1)} %get-tuple-element.25.refs_0_.refs_1_), channel_id=1, source_target_pairs={{0,1},{1,0},{2,3},{3,2},{4,5},{5,4},{6,7},{7,6},{8,9},{9,8},{10,11... | collective-permute-start | bytes 798728 | tf_op jit(solution)/shard_map/ppermute | solution.py:341
  8.9 9.6 %collective-permute-start.12 = (bf16[1040,128]{1,0:T(8,128)(2,1)S(1)}, bf16[1040,128]{1,0:T(8,128)(2,1)S(1)}, u32[]{:S(2)}, u32[]{:S(2)}) collective-permute-start(bf16[1040,128]{1,0:T(8,128)(2,1)S(1)} %get-tuple-element.26.refs_1_), channel_id=1, source_target_pairs={{8,0},{6,2},{16,8},{2,10},{24,16},{10,18},{28,24},{18,26},{20,28},... | collective-permute-start | bytes 798728 | tf_op jit(solution)/shard_map/ppermute | solution.py:445
  11.9 7.3 %collective-permute-start.10 = (bf16[1040,128]{1,0:T(8,128)(2,1)S(1)}, bf16[1040,128]{1,0:T(8,128)(2,1)S(1)}, u32[]{:S(2)}, u32[]{:S(2)}) collective-permute-start(bf16[1040,128]{1,0:T(8,128)(2,1)S(1)} %get-tuple-element.26.refs_1_), channel_id=1, source_target_pairs={{0,8},{2,6},{8,16},{10,2},{16,24},{18,10},{24,28},{26,18},{28,20},... | collective-permute-start | bytes 798728 | tf_op jit(solution)/shard_map/ppermute | solution.py:445
  15.3 4.0 %collective-permute-start.9 = (bf16[1040,128]{1,0:T(8,128)(2,1)S(1)}, bf16[1040,128]{1,0:T(8,128)(2,1)S(1)}, u32[]{:S(2)}, u32[]{:S(2)}) collective-permute-start(bf16[1040,128]{1,0:T(8,128)(2,1)S(1)} %get-tuple-element.26.refs_1_), channel_id=1, source_target_pairs={{0,2},{2,0},{4,6},{6,4},{8,10},{10,8},{12,14},{14,12},{16,18},{18,... | collective-permute-start | bytes 798728 | tf_op jit(solution)/shard_map/ppermute | solution.py:363
  15.4 8.8 %collective-permute-start.1 = (bf16[1040,128]{1,0:T(8,128)(2,1)S(1)}, bf16[1040,128]{1,0:T(8,128)(2,1)S(1)}, u32[]{:S(2)}, u32[]{:S(2)}) collective-permute-start(bf16[1040,128]{1,0:T(8,128)(2,1)S(1)} %get-tuple-element.26.refs_1_), channel_id=1, source_target_pairs={{0,1},{1,0},{2,3},{3,2},{4,5},{5,4},{6,7},{7,6},{8,9},{9,8},{10,11... | collective-permute-start | bytes 798728 | tf_op jit(solution)/shard_map/ppermute | solution.py:341
  16.9 7.3 %collective-permute-start.3 = (bf16[1040,128]{1,0:T(8,128)(2,1)S(1)}, bf16[1040,128]{1,0:T(8,128)(2,1)S(1)}, u32[]{:S(2)}, u32[]{:S(2)}) collective-permute-start(bf16[1040,128]{1,0:T(8,128)(2,1)S(1)} %collective-permute-done.2.refs_3_), channel_id=1, source_target_pairs={{0,8},{2,6},{8,16},{10,2},{16,24},{18,10},{24,28},{26,18},{28,20},... | collective-permute-start | bytes 798728 | tf_op jit(solution)/shard_map/ppermute | solution.py:445
  18.5 6.2 %collective-permute-start.13 = (bf16[1040,128]{1,0:T(8,128)(2,1)S(1)}, bf16[1040,128]{1,0:T(8,128)(2,1)S(1)}, u32[]{:S(2)}, u32[]{:S(2)}) collective-permute-start(bf16[1040,128]{1,0:T(8,128)(2,1)S(1)} %collective-permute-done.12.refs_5_), channel_id=1, source_target_pairs={{0,2},{2,0},{4,6},{6,4},{8,10},{10,8},{12,14},{14,12},{16,18},{18,... | collective-permute-start | bytes 798728 | tf_op jit(solution)/shard_map/ppermute | solution.py:363
  19.3 7.0 %collective-permute-start.11 = (bf16[1040,128]{1,0:T(8,128)(2,1)S(1)}, bf16[1040,128]{1,0:T(8,128)(2,1)S(1)}, u32[]{:S(2)}, u32[]{:S(2)}) collective-permute-start(bf16[1040,128]{1,0:T(8,128)(2,1)S(1)} %collective-permute-done.10.refs_3_), channel_id=1, source_target_pairs={{0,2},{2,0},{4,6},{6,4},{8,10},{10,8},{12,14},{14,12},{16,18},{18,... | collective-permute-start | bytes 798728 | tf_op jit(solution)/shard_map/ppermute | solution.py:363
  19.3 9.8 %collective-permute-start.17 = (bf16[1040,128]{1,0:T(8,128)(2,1)S(1)}, bf16[1040,128]{1,0:T(8,128)(2,1)S(1)}, u32[]{:S(2)}, u32[]{:S(2)}) collective-permute-start(bf16[1040,128]{1,0:T(8,128)(2,1)S(1)} %collective-permute-done.7.refs_5_), channel_id=1, source_target_pairs={{8,0},{6,2},{16,8},{2,10},{24,16},{10,18},{28,24},{18,26},{20,28},... | collective-permute-start | bytes 798728 | tf_op jit(solution)/shard_map/ppermute | solution.py:445
  24.2 5.8 %collective-permute-start.8 = (bf16[1040,128]{1,0:T(8,128)(2,1)S(1)}, bf16[1040,128]{1,0:T(8,128)(2,1)S(1)}, u32[]{:S(2)}, u32[]{:S(2)}) collective-permute-start(bf16[1040,128]{1,0:T(8,128)(2,1)S(1)} %collective-permute-done.7.refs_5_), channel_id=1, source_target_pairs={{0,2},{2,0},{4,6},{6,4},{8,10},{10,8},{12,14},{14,12},{16,18},{18,... | collective-permute-start | bytes 798728 | tf_op jit(solution)/shard_map/ppermute | solution.py:363
  24.3 5.7 %collective-permute-start.6 = (bf16[1040,128]{1,0:T(8,128)(2,1)S(1)}, bf16[1040,128]{1,0:T(8,128)(2,1)S(1)}, u32[]{:S(2)}, u32[]{:S(2)}) collective-permute-start(bf16[1040,128]{1,0:T(8,128)(2,1)S(1)} %collective-permute-done.2.refs_3_), channel_id=1, source_target_pairs={{0,2},{2,0},{4,6},{6,4},{8,10},{10,8},{12,14},{14,12},{16,18},{18,... | collective-permute-start | bytes 798728 | tf_op jit(solution)/shard_map/ppermute | solution.py:363
  24.7 9.3 %collective-permute-start.4 = (bf16[1040,128]{1,0:T(8,128)(2,1)S(1)}, bf16[1040,128]{1,0:T(8,128)(2,1)S(1)}, u32[]{:S(2)}, u32[]{:S(2)}) collective-permute-start(bf16[1040,128]{1,0:T(8,128)(2,1)S(1)} %collective-permute-done.3.refs_1_), channel_id=1, source_target_pairs={{0,8},{2,6},{8,16},{10,2},{16,24},{18,10},{24,28},{26,18},{28,20},... | collective-permute-start | bytes 798728 | tf_op jit(solution)/shard_map/ppermute | solution.py:445
  26.3 9.2 %collective-permute-start.22 = (bf16[1040,128]{1,0:T(8,128)(2,1)S(1)}, bf16[1040,128]{1,0:T(8,128)(2,1)S(1)}, u32[]{:S(2)}, u32[]{:S(2)}) collective-permute-start(bf16[1040,128]{1,0:T(8,128)(2,1)S(1)} %collective-permute-done.12.refs_5_), channel_id=1, source_target_pairs={{8,0},{6,2},{16,8},{2,10},{24,16},{10,18},{28,24},{18,26},{20,28},... | collective-permute-start | bytes 798728 | tf_op jit(solution)/shard_map/ppermute | solution.py:445
  26.7 0.7 copy-start.1
  29.1 8.5 %collective-permute-start.20 = (bf16[1040,128]{1,0:T(8,128)(2,1)S(1)}, bf16[1040,128]{1,0:T(8,128)(2,1)S(1)}, u32[]{:S(2)}, u32[]{:S(2)}) collective-permute-start(bf16[1040,128]{1,0:T(8,128)(2,1)S(1)} %collective-permute-done.17.refs_3_), channel_id=1, source_target_pairs={{8,0},{6,2},{16,8},{2,10},{24,16},{10,18},{28,24},{18,26},{20,28},... | collective-permute-start | bytes 798728 | tf_op jit(solution)/shard_map/ppermute | solution.py:445
  30.0 7.6 %collective-permute-start.18 = (bf16[1040,128]{1,0:T(8,128)(2,1)S(1)}, bf16[1040,128]{1,0:T(8,128)(2,1)S(1)}, u32[]{:S(2)}, u32[]{:S(2)}) collective-permute-start(bf16[1040,128]{1,0:T(8,128)(2,1)S(1)} %collective-permute-done.17.refs_3_), channel_id=1, source_target_pairs={{0,2},{2,0},{4,6},{6,4},{8,10},{10,8},{12,14},{14,12},{16,18},{18,... | collective-permute-start | bytes 798728 | tf_op jit(solution)/shard_map/ppermute | solution.py:363
  33.9 8.2 %collective-permute-start.14 = (bf16[1040,128]{1,0:T(8,128)(2,1)S(1)}, bf16[1040,128]{1,0:T(8,128)(2,1)S(1)}, u32[]{:S(2)}, u32[]{:S(2)}) collective-permute-start(bf16[1040,128]{1,0:T(8,128)(2,1)S(1)} %collective-permute-done.4.refs_5_), channel_id=1, source_target_pairs={{0,8},{2,6},{8,16},{10,2},{16,24},{18,10},{24,28},{26,18},{28,20},... | collective-permute-start | bytes 798728 | tf_op jit(solution)/shard_map/ppermute | solution.py:445
  35.5 6.7 %collective-permute-start.23 = (bf16[1040,128]{1,0:T(8,128)(2,1)S(1)}, bf16[1040,128]{1,0:T(8,128)(2,1)S(1)}, u32[]{:S(2)}, u32[]{:S(2)}) collective-permute-start(bf16[1040,128]{1,0:T(8,128)(2,1)S(1)} %collective-permute-done.22.refs_3_), channel_id=1, source_target_pairs={{8,0},{6,2},{16,8},{2,10},{24,16},{10,18},{28,24},{18,26},{20,28},... | collective-permute-start | bytes 798728 | tf_op jit(solution)/shard_map/ppermute | solution.py:459
  36.0 7.6 %collective-permute-start.16 = (bf16[1040,128]{1,0:T(8,128)(2,1)S(1)}, bf16[1040,128]{1,0:T(8,128)(2,1)S(1)}, u32[]{:S(2)}, u32[]{:S(2)}) collective-permute-start(bf16[1040,128]{1,0:T(8,128)(2,1)S(1)} %collective-permute-done.3.refs_1_), channel_id=1, source_target_pairs={{0,2},{2,0},{4,6},{6,4},{8,10},{10,8},{12,14},{14,12},{16,18},{18,... | collective-permute-start | bytes 798728 | tf_op jit(solution)/shard_map/ppermute | solution.py:363
  37.6 6.0 %collective-permute-start.21 = (bf16[1040,128]{1,0:T(8,128)(2,1)S(1)}, bf16[1040,128]{1,0:T(8,128)(2,1)S(1)}, u32[]{:S(2)}, u32[]{:S(2)}) collective-permute-start(bf16[1040,128]{1,0:T(8,128)(2,1)S(1)} %collective-permute-done.20.refs_7_), channel_id=1, source_target_pairs={{0,2},{2,0},{4,6},{6,4},{8,10},{10,8},{12,14},{14,12},{16,18},{18,... | collective-permute-start | bytes 798728 | tf_op jit(solution)/shard_map/ppermute | solution.py:363
  37.6 6.0 %collective-permute-start.19 = (bf16[1040,128]{1,0:T(8,128)(2,1)S(1)}, bf16[1040,128]{1,0:T(8,128)(2,1)S(1)}, u32[]{:S(2)}, u32[]{:S(2)}) collective-permute-start(bf16[1040,128]{1,0:T(8,128)(2,1)S(1)} %collective-permute-done.4.refs_5_), channel_id=1, source_target_pairs={{0,2},{2,0},{4,6},{6,4},{8,10},{10,8},{12,14},{14,12},{16,18},{18,... | collective-permute-start | bytes 798728 | tf_op jit(solution)/shard_map/ppermute | solution.py:363
  42.2 2.8 %collective-permute-start.15 = (bf16[1040,128]{1,0:T(8,128)(2,1)S(1)}, bf16[1040,128]{1,0:T(8,128)(2,1)S(1)}, u32[]{:S(2)}, u32[]{:S(2)}) collective-permute-start(bf16[1040,128]{1,0:T(8,128)(2,1)S(1)} %collective-permute-done.14.refs_1_), channel_id=1, source_target_pairs={{0,2},{2,0},{4,6},{6,4},{8,10},{10,8},{12,14},{14,12},{16,18},{18,... | collective-permute-start | bytes 798728 | tf_op jit(solution)/shard_map/ppermute | solution.py:363
  42.2 6.4 %collective-permute-start.26 = (bf16[1040,128]{1,0:T(8,128)(2,1)S(1)}, bf16[1040,128]{1,0:T(8,128)(2,1)S(1)}, u32[]{:S(2)}, u32[]{:S(2)}) collective-permute-start(bf16[1040,128]{1,0:T(8,128)(2,1)S(1)} %collective-permute-done.10.refs_3_), channel_id=1, source_target_pairs={{0,8},{2,6},{8,16},{10,2},{16,24},{18,10},{24,28},{26,18},{28,20},... | collective-permute-start | bytes 798728 | tf_op jit(solution)/shard_map/ppermute | solution.py:445
  43.6 8.5 %collective-permute-start.28 = (bf16[1040,128]{1,0:T(8,128)(2,1)S(1)}, bf16[1040,128]{1,0:T(8,128)(2,1)S(1)}, u32[]{:S(2)}, u32[]{:S(2)}) collective-permute-start(bf16[1040,128]{1,0:T(8,128)(2,1)S(1)} %collective-permute-done.22.refs_3_), channel_id=1, source_target_pairs={{0,2},{2,0},{4,6},{6,4},{8,10},{10,8},{12,14},{14,12},{16,18},{18,... | collective-permute-start | bytes 798728 | tf_op jit(solution)/shard_map/ppermute | solution.py:363
  48.6 8.8 %collective-permute-start.29 = (bf16[1040,128]{1,0:T(8,128)(2,1)S(1)}, bf16[1040,128]{1,0:T(8,128)(2,1)S(1)}, u32[]{:S(2)}, u32[]{:S(2)}) collective-permute-start(bf16[1040,128]{1,0:T(8,128)(2,1)S(1)} %collective-permute-done.26.refs_1_), channel_id=1, source_target_pairs={{0,8},{2,6},{8,16},{10,2},{16,24},{18,10},{24,28},{26,18},{28,20},... | collective-permute-start | bytes 798728 | tf_op jit(solution)/shard_map/ppermute | solution.py:459
  50.0 7.4 %collective-permute-start.24 = (bf16[1040,128]{1,0:T(8,128)(2,1)S(1)}, bf16[1040,128]{1,0:T(8,128)(2,1)S(1)}, u32[]{:S(2)}, u32[]{:S(2)}) collective-permute-start(bf16[1040,128]{1,0:T(8,128)(2,1)S(1)} %collective-permute-done.23.refs_7_), channel_id=1, source_target_pairs={{8,0},{6,2},{16,8},{2,10},{24,16},{10,18},{28,24},{18,26},{20,28},... | collective-permute-start | bytes 798728 | tf_op jit(solution)/shard_map/ppermute | solution.py:459
  50.6 12.9 %collective-permute-start.32 = (bf16[256,1024]{1,0:T(8,128)(2,1)S(1)}, bf16[256,1024]{1,0:T(8,128)(2,1)S(1)}, u32[]{:S(2)}, u32[]{:S(2)}) collective-permute-start(bf16[256,1024]{1,0:T(8,128)(2,1)S(1)} %get-tuple-element.33.refs_0_), channel_id=1, source_target_pairs={{0,1},{1,0},{2,3},{3,2},{4,5},{5,4},{6,7},{7,6},{8,9},{9,8},{10,11... | collective-permute-start | bytes 1572872 | tf_op jit(solution)/shard_map/ppermute | solution.py:341
  52.1 5.8 %collective-permute-start.27 = (bf16[1040,128]{1,0:T(8,128)(2,1)S(1)}, bf16[1040,128]{1,0:T(8,128)(2,1)S(1)}, u32[]{:S(2)}, u32[]{:S(2)}) collective-permute-start(bf16[1040,128]{1,0:T(8,128)(2,1)S(1)} %collective-permute-done.26.refs_1_), channel_id=1, source_target_pairs={{0,2},{2,0},{4,6},{6,4},{8,10},{10,8},{12,14},{14,12},{16,18},{18,... | collective-permute-start | bytes 798728 | tf_op jit(solution)/shard_map/ppermute | solution.py:363
  52.1 5.8 %collective-permute-start.31 = (bf16[1040,128]{1,0:T(8,128)(2,1)S(1)}, bf16[1040,128]{1,0:T(8,128)(2,1)S(1)}, u32[]{:S(2)}, u32[]{:S(2)}) collective-permute-start(bf16[1040,128]{1,0:T(8,128)(2,1)S(1)} %collective-permute-done.23.refs_7_), channel_id=1, source_target_pairs={{0,2},{2,0},{4,6},{6,4},{8,10},{10,8},{12,14},{14,12},{16,18},{18,... | collective-permute-start | bytes 798728 | tf_op jit(solution)/shard_map/ppermute | solution.py:363
  57.4 1.5 %collective-permute-start.30 = (bf16[1040,128]{1,0:T(8,128)(2,1)S(1)}, bf16[1040,128]{1,0:T(8,128)(2,1)S(1)}, u32[]{:S(2)}, u32[]{:S(2)}) collective-permute-start(bf16[1040,128]{1,0:T(8,128)(2,1)S(1)} %collective-permute-done.29.refs_5_), channel_id=1, source_target_pairs={{0,2},{2,0},{4,6},{6,4},{8,10},{10,8},{12,14},{14,12},{16,18},{18,... | collective-permute-start | bytes 798728 | tf_op jit(solution)/shard_map/ppermute | solution.py:363
  57.4 2.9 %collective-permute-start.25 = (bf16[1040,128]{1,0:T(8,128)(2,1)S(1)}, bf16[1040,128]{1,0:T(8,128)(2,1)S(1)}, u32[]{:S(2)}, u32[]{:S(2)}) collective-permute-start(bf16[1040,128]{1,0:T(8,128)(2,1)S(1)} %collective-permute-done.24.refs_1_), channel_id=1, source_target_pairs={{0,2},{2,0},{4,6},{6,4},{8,10},{10,8},{12,14},{14,12},{16,18},{18,... | collective-permute-start | bytes 798728 | tf_op jit(solution)/shard_map/ppermute | solution.py:363
  63.5 12.0 %collective-permute-start.33 = (bf16[256,1024]{1,0:T(8,128)(2,1)S(1)}, bf16[256,1024]{1,0:T(8,128)(2,1)S(1)}, u32[]{:S(2)}, u32[]{:S(2)}) collective-permute-start(bf16[256,1024]{1,0:T(8,128)(2,1)S(1)} %get-tuple-element.47.refs_1_), channel_id=1, source_target_pairs={{0,1},{1,0},{2,3},{3,2},{4,5},{5,4},{6,7},{7,6},{8,9},{9,8},{10,11... | collective-permute-start | bytes 1572872 | tf_op jit(solution)/shard_map/ppermute | solution.py:341

commit v6 on v5

--- a/solution.py
+++ b/solution.py
@@ -225,7 +225,9 @@
                 preferred_element_type=jnp.float32,
             )
             total = product if total is None else total + product
-        acc[:, column : column + size * dense] = total
+        acc[:, column : column + size * dense] = (
+            3.0 * own[chunk][...].astype(jnp.float32) - 2.0 * total
+        )
         column += size * dense
 
     last = sizes[-1]
@@ -271,26 +273,25 @@
     return jnp.where(swap, right, left), jnp.where(swap, left, right)
 
 
-def final_kernel(sizes, groups, width, tile, kept, acc, later, *refs):
-    chunks = len(sizes)
-    own = refs[:chunks]
-    received = refs[chunks : chunks + groups - 1]
+def final_kernel(sizes, groups, width, tile, kept, base, later, *refs):
+    received = refs[: groups - 1]
     purified, staged, sems = refs[-3:]
     dense = width * tile
     panels = sum(sizes)
     span = sizes[-1] * dense
     copies = []
-    first = 0
-    for size, source in zip(sizes, own):
+    for first in range(0, panels, 2):
+        size = min(2, panels - first)
         columns = slice(first * dense, (first + size) * dense)
-        total = acc[:, columns]
+        total = None
         for shift in range(groups - 1):
-            total += jnp.dot(
+            product = jnp.dot(
                 received[shift][...],
                 later[shift * span : (shift + 1) * span, columns],
                 preferred_element_type=jnp.float32,
             )
-        value = 3.0 * source[...].astype(jnp.float32) - 2.0 * total
+            total = product if total is None else total + product
+        value = base[:, columns] - 2.0 * total
         for panel in range(size):
             for local in range(width):
                 part = value[
@@ -305,7 +306,6 @@
                 pltpu.make_async_copy(staged.at[where], purified.at[where], sems.at[len(copies)])
             )
             copies[-1].start()
-        first += size
     for copy in copies:
         copy.wait()
 
@@ -481,15 +481,15 @@
     purified = pl.pallas_call(
         functools.partial(final_kernel, sizes, groups, width, tile),
         out_shape=jax.ShapeDtypeStruct((width, panels, 2, tile, tile), bf16),
-        in_specs=vmem(3 + len(squares) + groups - 1),
+        in_specs=vmem(3 + groups - 1),
         out_specs=anywhere(1)[0],
         scratch_shapes=[
             pltpu.VMEM((width, panels, 2, tile, tile), bf16),
-            pltpu.SemaphoreType.DMA((width * len(sizes),)),
+            pltpu.SemaphoreType.DMA((width * -(-panels // 2),)),
         ],
         compiler_params=params(8),
         name="final",
-    )(kept, acc, later, *squares, *received[-1])
+    )(kept, acc, later, *received[-1])
     return (square_out, purified)
 
 

time: 78.2 us -> 78 us (level)
  no operation moved by 1% of the time
where the time goes in v6:
time: 78 us; the launch traced here: 77.8 us
  waiting for transfers between devices  30.1 us (39%)
  starting transfers between devices  28.3 us (36%)
  Pallas kernels  16 us (21%)
  local copies, waits for them, and re-layouts  2.39 us (3%)
  between operations  0.93 us (1%)
    ppermute x14, starting transfers between devices, shards(): lax.ppermute(value, 'row', forward if ahead else backward)  20.3 us
    ppermute x14, waiting for transfers between devices, shards(): lax.ppermute(value, 'row', forward if ahead else backward)  19.6 us
    ppermute x4, waiting for transfers between devices, across(): return lax.ppermute(value, 'col', pairs)  9.43 us
    pallas_call x1, Pallas kernels, shards(): pl.pallas_call(functools.partial(cube_kernel, sizes, rows, groups, width,...  6.71 us
    ppermute x4, starting transfers between devices, across(): return lax.ppermute(value, 'col', pairs)  6.05 us
    pallas_call x6, Pallas kernels, square_of(): pl.pallas_call(functools.partial(square_kernel, size, width, tile, start,...  5.85 us
    unnamed x6, local copies, waits for them, and re-layouts  2.39 us
    pallas_call x1, Pallas kernels, shards(): pl.pallas_call(functools.partial(final_kernel, sizes, groups, width, tile...  2.06 us
  transfers between devices with their start and end apart: 34, of which 12 were waited for; matrix products, arithmetic and copies ran while one was open for 0% of the time, Pallas kernels for 17%

profile of v6, /device:TPU:0, one launch (start us, length us, event | category | flops | bytes accessed | tf_op | source)
XLA Modules:
  0.0 77.8 jit_solution(427375854913043122)
XLA Ops:
  0.6 1.0 %copy-done = bf16[2,8,1,128,128]{4,3,2,1,0:T(8,128)(2,1)S(1)} copy-done((bf16[2,8,1,128,128]{4,3,2,1,0:T(8,128)(2,1)S(1)}, bf16[2,8,1,128,128]{4,3,2,1,0:T(8,128)(2,1)}, u32[]{:S(2)}) %copy-start) | copy-done | bytes 524312
  1.7 0.7 copy-done.2
  2.4 0.8 %pack.1 = (bf16[1040,128]{1,0:T(8,128)(2,1)S(1)}, bf16[1040,128]{1,0:T(8,128)(2,1)S(1)}) custom-call(s32[2,8]{1,0:T(2,128)S(1)} %bitcast.7, bf16[2,1024,128]{2,1,0:T(8,128)(2,1)S(1)} %bitcast.5), custom_call_target="tpu_custom_call" | custom-call | tf_op jit(solution)/shard_map/pack/pallas_call | solution.py:346
  3.2 3.0 %collective-permute-start.7 = (bf16[1040,128]{1,0:T(8,128)(2,1)S(1)}, bf16[1040,128]{1,0:T(8,128)(2,1)S(1)}, u32[]{:S(2)}, u32[]{:S(2)}) collective-permute-start(bf16[1040,128]{1,0:T(8,128)(2,1)S(1)} %get-tuple-element.25.refs_0_.refs_1_), channel_id=1, source_target_pairs={{8,0},{6,2},{16,8},{2,10},{24,16},{10,18},{28,24},{18,26},{20,28},... | collective-permute-start | bytes 798728 | tf_op jit(solution)/shard_map/ppermute | solution.py:445
  6.2 1.2 %collective-permute-start.2 = (bf16[1040,128]{1,0:T(8,128)(2,1)S(1)}, bf16[1040,128]{1,0:T(8,128)(2,1)S(1)}, u32[]{:S(2)}, u32[]{:S(2)}) collective-permute-start(bf16[1040,128]{1,0:T(8,128)(2,1)S(1)} %get-tuple-element.25.refs_0_.refs_1_), channel_id=1, source_target_pairs={{0,8},{2,6},{8,16},{10,2},{16,24},{18,10},{24,28},{26,18},{28,20},... | collective-permute-start | bytes 798728 | tf_op jit(solution)/shard_map/ppermute | solution.py:445
  7.4 1.5 %collective-permute-start = (bf16[1040,128]{1,0:T(8,128)(2,1)S(1)}, bf16[1040,128]{1,0:T(8,128)(2,1)S(1)}, u32[]{:S(2)}, u32[]{:S(2)}) collective-permute-start(bf16[1040,128]{1,0:T(8,128)(2,1)S(1)} %get-tuple-element.25.refs_0_.refs_1_), channel_id=1, source_target_pairs={{0,1},{1,0},{2,3},{3,2},{4,5},{5,4},{6,7},{7,6},{8,9},{9,8},{10,11... | collective-permute-start | bytes 798728 | tf_op jit(solution)/shard_map/ppermute | solution.py:341
  8.9 0.8 %collective-permute-start.12 = (bf16[1040,128]{1,0:T(8,128)(2,1)S(1)}, bf16[1040,128]{1,0:T(8,128)(2,1)S(1)}, u32[]{:S(2)}, u32[]{:S(2)}) collective-permute-start(bf16[1040,128]{1,0:T(8,128)(2,1)S(1)} %get-tuple-element.26.refs_1_), channel_id=1, source_target_pairs={{8,0},{6,2},{16,8},{2,10},{24,16},{10,18},{28,24},{18,26},{20,28},... | collective-permute-start | bytes 798728 | tf_op jit(solution)/shard_map/ppermute | solution.py:445
  9.7 2.2 %collective-permute-done.7.refs_5_ = bf16[1040,128]{1,0:T(8,128)(2,1)S(1)} collective-permute-done((bf16[1040,128]{1,0:T(8,128)(2,1)S(1)}, bf16[1040,128]{1,0:T(8,128)(2,1)S(1)}, u32[]{:S(2)}, u32[]{:S(2)}) %collective-permute-start.7) | collective-permute-done | bytes 266272 | tf_op jit(solution)/shard_map/ppermute | solution.py:445
  11.9 3.4 %collective-permute-start.10 = (bf16[1040,128]{1,0:T(8,128)(2,1)S(1)}, bf16[1040,128]{1,0:T(8,128)(2,1)S(1)}, u32[]{:S(2)}, u32[]{:S(2)}) collective-permute-start(bf16[1040,128]{1,0:T(8,128)(2,1)S(1)} %get-tuple-element.26.refs_1_), channel_id=1, source_target_pairs={{0,8},{2,6},{8,16},{10,2},{16,24},{18,10},{24,28},{26,18},{28,20},... | collective-permute-start | bytes 798728 | tf_op jit(solution)/shard_map/ppermute | solution.py:445
  15.3 0.0 collective-permute-done.2.refs_3_
  15.4 1.6 %collective-permute-start.1 = (bf16[1040,128]{1,0:T(8,128)(2,1)S(1)}, bf16[1040,128]{1,0:T(8,128)(2,1)S(1)}, u32[]{:S(2)}, u32[]{:S(2)}) collective-permute-start(bf16[1040,128]{1,0:T(8,128)(2,1)S(1)} %get-tuple-element.26.refs_1_), channel_id=1, source_target_pairs={{0,1},{1,0},{2,3},{3,2},{4,5},{5,4},{6,7},{7,6},{8,9},{9,8},{10,11... | collective-permute-start | bytes 798728 | tf_op jit(solution)/shard_map/ppermute | solution.py:341
  16.9 0.0 collective-permute-done.refs_2_
  16.9 1.6 %collective-permute-start.3 = (bf16[1040,128]{1,0:T(8,128)(2,1)S(1)}, bf16[1040,128]{1,0:T(8,128)(2,1)S(1)}, u32[]{:S(2)}, u32[]{:S(2)}) collective-permute-start(bf16[1040,128]{1,0:T(8,128)(2,1)S(1)} %collective-permute-done.2.refs_3_), channel_id=1, source_target_pairs={{0,8},{2,6},{8,16},{10,2},{16,24},{18,10},{24,28},{26,18},{28,20},... | collective-permute-start | bytes 798728 | tf_op jit(solution)/shard_map/ppermute | solution.py:445
  18.5 0.8 collective-permute-done.10.refs_3_
  19.3 0.0 collective-permute-start.11
  19.3 0.0 collective-permute-done.9.refs_2_
  19.3 1.9 %collective-permute-start.17 = (bf16[1040,128]{1,0:T(8,128)(2,1)S(1)}, bf16[1040,128]{1,0:T(8,128)(2,1)S(1)}, u32[]{:S(2)}, u32[]{:S(2)}) collective-permute-start(bf16[1040,128]{1,0:T(8,128)(2,1)S(1)} %collective-permute-done.7.refs_5_), channel_id=1, source_target_pairs={{8,0},{6,2},{16,8},{2,10},{24,16},{10,18},{28,24},{18,26},{20,28},... | collective-permute-start | bytes 798728 | tf_op jit(solution)/shard_map/ppermute | solution.py:445
  21.2 2.9 %collective-permute-done.1.refs_3_ = bf16[1040,128]{1,0:T(8,128)(2,1)S(1)} collective-permute-done((bf16[1040,128]{1,0:T(8,128)(2,1)S(1)}, bf16[1040,128]{1,0:T(8,128)(2,1)S(1)}, u32[]{:S(2)}, u32[]{:S(2)}) %collective-permute-start.1) | collective-permute-done | bytes 266272 | tf_op jit(solution)/shard_map/ppermute | solution.py:341
  24.2 0.0 collective-permute-start.8
  24.2 0.1 collective-permute-done.3.refs_1_
  24.3 0.4 collective-permute-start.6
  24.7 1.6 %collective-permute-start.4 = (bf16[1040,128]{1,0:T(8,128)(2,1)S(1)}, bf16[1040,128]{1,0:T(8,128)(2,1)S(1)}, u32[]{:S(2)}, u32[]{:S(2)}) collective-permute-start(bf16[1040,128]{1,0:T(8,128)(2,1)S(1)} %collective-permute-done.3.refs_1_), channel_id=1, source_target_pairs={{0,8},{2,6},{8,16},{10,2},{16,24},{18,10},{24,28},{26,18},{28,20},... | collective-permute-start | bytes 798728 | tf_op jit(solution)/shard_map/ppermute | solution.py:445
  26.3 0.4 collective-permute-start.22
  26.7 0.7 copy-done.1
  27.4 0.6 left.1
  28.0 1.1 %square.7 = (f32[256,1024]{1,0:T(8,128)S(1)}, bf16[1536,1024]{1,0:T(8,128)(2,1)S(1)}) custom-call(bf16[256,4096]{1,0:T(8,128)(2,1)S(1)} %get-tuple-element.28.refs_0_, bf16[1040,128]{1,0:T(8,128)(2,1)S(1)} %get-tuple-element.26.refs_1_, bf16[1040,128]{1,0:T(8,128)(2,1)S(1)} %collective-permute-done.9.refs_2_, ...), custom_call_target="tpu_custom_call" | custom-call | tf_op jit(solution)/shard_map/square/pallas_call | solution.py:381
  29.1 0.0 collective-permute-done.17.refs_3_
  29.1 0.9 %collective-permute-start.20 = (bf16[1040,128]{1,0:T(8,128)(2,1)S(1)}, bf16[1040,128]{1,0:T(8,128)(2,1)S(1)}, u32[]{:S(2)}, u32[]{:S(2)}) collective-permute-start(bf16[1040,128]{1,0:T(8,128)(2,1)S(1)} %collective-permute-done.17.refs_3_), channel_id=1, source_target_pairs={{8,0},{6,2},{16,8},{2,10},{24,16},{10,18},{28,24},{18,26},{20,28},... | collective-permute-start | bytes 798728 | tf_op jit(solution)/shard_map/ppermute | solution.py:445
  30.0 0.0 collective-permute-done.8.refs_6_
  30.0 0.0 collective-permute-start.18
  30.0 0.0 collective-permute-done.6.refs_4_
  30.0 1.1 %square.6 = (f32[256,1024]{1,0:T(8,128)S(1)}, bf16[1536,1024]{1,0:T(8,128)(2,1)S(1)}) custom-call(bf16[256,4096]{1,0:T(8,128)(2,1)S(1)} %get-tuple-element.28.refs_0_, bf16[1040,128]{1,0:T(8,128)(2,1)S(1)} %get-tuple-element.25.refs_0_.refs_1_, bf16[1040,128]{1,0:T(8,128)(2,1)S(1)} %collective-permute-done.5.refs_2_, ...), custom_call_target="tpu_custom_call" | custom-call | tf_op jit(solution)/shard_map/square/pallas_call | solution.py:381
  31.0 2.9 %collective-permute-done.4.refs_5_ = bf16[1040,128]{1,0:T(8,128)(2,1)S(1)} collective-permute-done((bf16[1040,128]{1,0:T(8,128)(2,1)S(1)}, bf16[1040,128]{1,0:T(8,128)(2,1)S(1)}, u32[]{:S(2)}, u32[]{:S(2)}) %collective-permute-start.4) | collective-permute-done | bytes 266272 | tf_op jit(solution)/shard_map/ppermute | solution.py:445
  33.9 1.5 %collective-permute-start.14 = (bf16[1040,128]{1,0:T(8,128)(2,1)S(1)}, bf16[1040,128]{1,0:T(8,128)(2,1)S(1)}, u32[]{:S(2)}, u32[]{:S(2)}) collective-permute-start(bf16[1040,128]{1,0:T(8,128)(2,1)S(1)} %collective-permute-done.4.refs_5_), channel_id=1, source_target_pairs={{0,8},{2,6},{8,16},{10,2},{16,24},{18,10},{24,28},{26,18},{28,20},... | collective-permute-start | bytes 798728 | tf_op jit(solution)/shard_map/ppermute | solution.py:445
  35.5 0.0 collective-permute-done.22.refs_3_
  35.5 0.5 collective-permute-start.23
  36.0 0.0 collective-permute-start.16
  36.0 1.6 %collective-permute-done.20.refs_7_ = bf16[1040,128]{1,0:T(8,128)(2,1)S(1)} collective-permute-done((bf16[1040,128]{1,0:T(8,128)(2,1)S(1)}, bf16[1040,128]{1,0:T(8,128)(2,1)S(1)}, u32[]{:S(2)}, u32[]{:S(2)}) %collective-permute-start.20) | collective-permute-done | bytes 266272 | tf_op jit(solution)/shard_map/ppermute | solution.py:445
  37.6 0.0 collective-permute-start.21
  37.6 0.0 collective-permute-done.18.refs_4_
  37.6 0.5 collective-permute-start.19
  38.1 4.1 %collective-permute-done.14.refs_1_ = bf16[1040,128]{1,0:T(8,128)(2,1)S(1)} collective-permute-done((bf16[1040,128]{1,0:T(8,128)(2,1)S(1)}, bf16[1040,128]{1,0:T(8,128)(2,1)S(1)}, u32[]{:S(2)}, u32[]{:S(2)}) %collective-permute-start.14) | collective-permute-done | bytes 266272 | tf_op jit(solution)/shard_map/ppermute | solution.py:445
  42.2 0.0 collective-permute-done.23.refs_7_
  42.2 1.4 %collective-permute-start.26 = (bf16[1040,128]{1,0:T(8,128)(2,1)S(1)}, bf16[1040,128]{1,0:T(8,128)(2,1)S(1)}, u32[]{:S(2)}, u32[]{:S(2)}) collective-permute-start(bf16[1040,128]{1,0:T(8,128)(2,1)S(1)} %collective-permute-done.10.refs_3_), channel_id=1, source_target_pairs={{0,8},{2,6},{8,16},{10,2},{16,24},{18,10},{24,28},{26,18},{28,20},... | collective-permute-start | bytes 798728 | tf_op jit(solution)/shard_map/ppermute | solution.py:445
  43.6 0.0 collective-permute-done.19.refs_6_
  43.6 1.4 %square.8 = (f32[256,1024]{1,0:T(8,128)S(1)}, bf16[2048,1024]{1,0:T(8,128)(2,1)S(1)}) custom-call(bf16[256,4096]{1,0:T(8,128)(2,1)S(1)} %get-tuple-element.28.refs_0_, bf16[1040,128]{1,0:T(8,128)(2,1)S(1)} %collective-permute-done.3.refs_1_, bf16[1040,128]{1,0:T(8,128)(2,1)S(1)} %collective-permute-done.16.refs_2_, ...), custom_call_target="tpu_custom_call" | custom-call | tf_op jit(solution)/shard_map/square/pallas_call | solution.py:381
  45.0 0.0 collective-permute-done.15.refs_2_
  45.0 0.5 square.9
  45.5 3.1 %collective-permute-done.26.refs_1_ = bf16[1040,128]{1,0:T(8,128)(2,1)S(1)} collective-permute-done((bf16[1040,128]{1,0:T(8,128)(2,1)S(1)}, bf16[1040,128]{1,0:T(8,128)(2,1)S(1)}, u32[]{:S(2)}, u32[]{:S(2)}) %collective-permute-start.26) | collective-permute-done | bytes 266272 | tf_op jit(solution)/shard_map/ppermute | solution.py:445
  48.6 1.4 %collective-permute-start.29 = (bf16[1040,128]{1,0:T(8,128)(2,1)S(1)}, bf16[1040,128]{1,0:T(8,128)(2,1)S(1)}, u32[]{:S(2)}, u32[]{:S(2)}) collective-permute-start(bf16[1040,128]{1,0:T(8,128)(2,1)S(1)} %collective-permute-done.26.refs_1_), channel_id=1, source_target_pairs={{0,8},{2,6},{8,16},{10,2},{16,24},{18,10},{24,28},{26,18},{28,20},... | collective-permute-start | bytes 798728 | tf_op jit(solution)/shard_map/ppermute | solution.py:459
  50.0 0.6 collective-permute-start.24
  50.6 1.5 %collective-permute-start.32 = (bf16[256,1024]{1,0:T(8,128)(2,1)S(1)}, bf16[256,1024]{1,0:T(8,128)(2,1)S(1)}, u32[]{:S(2)}, u32[]{:S(2)}) collective-permute-start(bf16[256,1024]{1,0:T(8,128)(2,1)S(1)} %get-tuple-element.33.refs_0_), channel_id=1, source_target_pairs={{0,1},{1,0},{2,3},{3,2},{4,5},{5,4},{6,7},{7,6},{8,9},{9,8},{10,11... | collective-permute-start | bytes 1572872 | tf_op jit(solution)/shard_map/ppermute | solution.py:341
  52.1 0.0 collective-permute-start.27
  52.1 0.5 collective-permute-start.31
  52.6 4.8 %collective-permute-done.29.refs_5_ = bf16[1040,128]{1,0:T(8,128)(2,1)S(1)} collective-permute-done((bf16[1040,128]{1,0:T(8,128)(2,1)S(1)}, bf16[1040,128]{1,0:T(8,128)(2,1)S(1)}, u32[]{:S(2)}, u32[]{:S(2)}) %collective-permute-start.29) | collective-permute-done | bytes 266272 | tf_op jit(solution)/shard_map/ppermute | solution.py:459
  57.4 0.5 collective-permute-start.25
  57.9 1.0 %collective-permute-done.30.refs_6_ = bf16[1040,128]{1,0:T(8,128)(2,1)S(1)} collective-permute-done((bf16[1040,128]{1,0:T(8,128)(2,1)S(1)}, bf16[1040,128]{1,0:T(8,128)(2,1)S(1)}, u32[]{:S(2)}, u32[]{:S(2)}) %collective-permute-start.30) | collective-permute-done | bytes 266272 | tf_op jit(solution)/shard_map/ppermute | solution.py:363
  59.0 1.4 %square.10 = (f32[256,1024]{1,0:T(8,128)S(1)}, bf16[2048,1024]{1,0:T(8,128)(2,1)S(1)}) custom-call(bf16[256,4096]{1,0:T(8,128)(2,1)S(1)} %get-tuple-element.28.refs_0_, bf16[1040,128]{1,0:T(8,128)(2,1)S(1)} %collective-permute-done.26.refs_1_, bf16[1040,128]{1,0:T(8,128)(2,1)S(1)} %collective-permute-done.27.refs_2_, ...), custom_call_target="tpu_custom_call" | custom-call | tf_op jit(solution)/shard_map/square/pallas_call | solution.py:381
  60.3 0.5 square.11
  60.8 2.7 %collective-permute-done.32.refs_2_ = bf16[256,1024]{1,0:T(8,128)(2,1)S(1)} collective-permute-done((bf16[256,1024]{1,0:T(8,128)(2,1)S(1)}, bf16[256,1024]{1,0:T(8,128)(2,1)S(1)}, u32[]{:S(2)}, u32[]{:S(2)}) %collective-permute-start.32) | collective-permute-done | bytes 524320 | tf_op jit(solution)/shard_map/ppermute | solution.py:341
  63.5 1.5 %collective-permute-start.33 = (bf16[256,1024]{1,0:T(8,128)(2,1)S(1)}, bf16[256,1024]{1,0:T(8,128)(2,1)S(1)}, u32[]{:S(2)}, u32[]{:S(2)}) collective-permute-start(bf16[256,1024]{1,0:T(8,128)(2,1)S(1)} %get-tuple-element.47.refs_1_), channel_id=1, source_target_pairs={{0,1},{1,0},{2,3},{3,2},{4,5},{5,4},{6,7},{7,6},{8,9},{9,8},{10,11... | collective-permute-start | bytes 1572872 | tf_op jit(solution)/shard_map/ppermute | solution.py:341
  65.0 6.7 %cube.1 = (f32[256,2048]{1,0:T(8,128)S(1)}, bf16[2,8,2,128,128]{4,3,2,1,0:T(8,128)(2,1)}, bf16[1024,2048]{1,0:T(8,128)(2,1)S(1)}) custom-call(f32[16,128]{1,0:T(8,128)S(1)} %get-tuple-element.27.kept, bf16[256,1024]{1,0:T(8,128)(2,1)S(1)} %get-tuple-element.33.refs_0_, bf16[256,1024]{1,0:T(8,128)(2,1)S(1)} %get-tuple-element.47.refs_1_, ...), custom_call_target="tpu_custom_call" | custom-call | tf_op jit(solution)/shard_map/cube/pallas_call | solution.py:467
  71.7 3.8 %collective-permute-done.33.refs_0_ = bf16[256,1024]{1,0:T(8,128)(2,1)S(1)} collective-permute-done((bf16[256,1024]{1,0:T(8,128)(2,1)S(1)}, bf16[256,1024]{1,0:T(8,128)(2,1)S(1)}, u32[]{:S(2)}, u32[]{:S(2)}) %collective-permute-start.33) | collective-permute-done | bytes 524320 | tf_op jit(solution)/shard_map/ppermute | solution.py:341
  75.5 2.1 %final.1 = bf16[2,8,2,128,128]{4,3,2,1,0:T(8,128)(2,1)} custom-call(f32[16,128]{1,0:T(8,128)S(1)} %get-tuple-element.27.kept, f32[256,2048]{1,0:T(8,128)S(1)} %get-tuple-element.45.base, bf16[1024,2048]{1,0:T(8,128)(2,1)S(1)} %get-tuple-element.46.later, bf16[256,1024]{1,0:T(8,128)(2,1)S(1)} %collective-permute-done.33.refs_0_), custom_call_target="tpu_custom_call" | custom-call | tf_op jit(solution)/shard_map/final/pallas_call | solution.py:481
  (20 shorter events, 0.0 us)
Async XLA Ops:
  0.6 1.0 %copy-start = (bf16[2,8,1,128,128]{4,3,2,1,0:T(8,128)(2,1)S(1)}, bf16[2,8,1,128,128]{4,3,2,1,0:T(8,128)(2,1)}, u32[]{:S(2)}) copy-start(bf16[2,8,1,128,128]{4,3,2,1,0:T(8,128)(2,1)} %param.3) | copy-start | bytes 1572868
  1.7 0.7 copy-start.2
  3.2 8.8 %collective-permute-start.7 = (bf16[1040,128]{1,0:T(8,128)(2,1)S(1)}, bf16[1040,128]{1,0:T(8,128)(2,1)S(1)}, u32[]{:S(2)}, u32[]{:S(2)}) collective-permute-start(bf16[1040,128]{1,0:T(8,128)(2,1)S(1)} %get-tuple-element.25.refs_0_.refs_1_), channel_id=1, source_target_pairs={{8,0},{6,2},{16,8},{2,10},{24,16},{10,18},{28,24},{18,26},{20,28},... | collective-permute-start | bytes 798728 | tf_op jit(solution)/shard_map/ppermute | solution.py:445
  6.2 9.2 %collective-permute-start.5 = (bf16[1040,128]{1,0:T(8,128)(2,1)S(1)}, bf16[1040,128]{1,0:T(8,128)(2,1)S(1)}, u32[]{:S(2)}, u32[]{:S(2)}) collective-permute-start(bf16[1040,128]{1,0:T(8,128)(2,1)S(1)} %get-tuple-element.25.refs_0_.refs_1_), channel_id=1, source_target_pairs={{0,2},{2,0},{4,6},{6,4},{8,10},{10,8},{12,14},{14,12},{16,18},{18,... | collective-permute-start | bytes 798728 | tf_op jit(solution)/shard_map/ppermute | solution.py:363
  6.2 9.2 %collective-permute-start.2 = (bf16[1040,128]{1,0:T(8,128)(2,1)S(1)}, bf16[1040,128]{1,0:T(8,128)(2,1)S(1)}, u32[]{:S(2)}, u32[]{:S(2)}) collective-permute-start(bf16[1040,128]{1,0:T(8,128)(2,1)S(1)} %get-tuple-element.25.refs_0_.refs_1_), channel_id=1, source_target_pairs={{0,8},{2,6},{8,16},{10,2},{16,24},{18,10},{24,28},{26,18},{28,20},... | collective-permute-start | bytes 798728 | tf_op jit(solution)/shard_map/ppermute | solution.py:445
  7.4 9.6 %collective-permute-start = (bf16[1040,128]{1,0:T(8,128)(2,1)S(1)}, bf16[1040,128]{1,0:T(8,128)(2,1)S(1)}, u32[]{:S(2)}, u32[]{:S(2)}) collective-permute-start(bf16[1040,128]{1,0:T(8,128)(2,1)S(1)} %get-tuple-element.25.refs_0_.refs_1_), channel_id=1, source_target_pairs={{0,1},{1,0},{2,3},{3,2},{4,5},{5,4},{6,7},{7,6},{8,9},{9,8},{10,11... | collective-permute-start | bytes 798728 | tf_op jit(solution)/shard_map/ppermute | solution.py:341
  8.9 9.6 %collective-permute-start.12 = (bf16[1040,128]{1,0:T(8,128)(2,1)S(1)}, bf16[1040,128]{1,0:T(8,128)(2,1)S(1)}, u32[]{:S(2)}, u32[]{:S(2)}) collective-permute-start(bf16[1040,128]{1,0:T(8,128)(2,1)S(1)} %get-tuple-element.26.refs_1_), channel_id=1, source_target_pairs={{8,0},{6,2},{16,8},{2,10},{24,16},{10,18},{28,24},{18,26},{20,28},... | collective-permute-start | bytes 798728 | tf_op jit(solution)/shard_map/ppermute | solution.py:445
  11.9 7.3 %collective-permute-start.10 = (bf16[1040,128]{1,0:T(8,128)(2,1)S(1)}, bf16[1040,128]{1,0:T(8,128)(2,1)S(1)}, u32[]{:S(2)}, u32[]{:S(2)}) collective-permute-start(bf16[1040,128]{1,0:T(8,128)(2,1)S(1)} %get-tuple-element.26.refs_1_), channel_id=1, source_target_pairs={{0,8},{2,6},{8,16},{10,2},{16,24},{18,10},{24,28},{26,18},{28,20},... | collective-permute-start | bytes 798728 | tf_op jit(solution)/shard_map/ppermute | solution.py:445
  15.3 4.0 %collective-permute-start.9 = (bf16[1040,128]{1,0:T(8,128)(2,1)S(1)}, bf16[1040,128]{1,0:T(8,128)(2,1)S(1)}, u32[]{:S(2)}, u32[]{:S(2)}) collective-permute-start(bf16[1040,128]{1,0:T(8,128)(2,1)S(1)} %get-tuple-element.26.refs_1_), channel_id=1, source_target_pairs={{0,2},{2,0},{4,6},{6,4},{8,10},{10,8},{12,14},{14,12},{16,18},{18,... | collective-permute-start | bytes 798728 | tf_op jit(solution)/shard_map/ppermute | solution.py:363
  15.4 8.8 %collective-permute-start.1 = (bf16[1040,128]{1,0:T(8,128)(2,1)S(1)}, bf16[1040,128]{1,0:T(8,128)(2,1)S(1)}, u32[]{:S(2)}, u32[]{:S(2)}) collective-permute-start(bf16[1040,128]{1,0:T(8,128)(2,1)S(1)} %get-tuple-element.26.refs_1_), channel_id=1, source_target_pairs={{0,1},{1,0},{2,3},{3,2},{4,5},{5,4},{6,7},{7,6},{8,9},{9,8},{10,11... | collective-permute-start | bytes 798728 | tf_op jit(solution)/shard_map/ppermute | solution.py:341
  16.9 7.3 %collective-permute-start.3 = (bf16[1040,128]{1,0:T(8,128)(2,1)S(1)}, bf16[1040,128]{1,0:T(8,128)(2,1)S(1)}, u32[]{:S(2)}, u32[]{:S(2)}) collective-permute-start(bf16[1040,128]{1,0:T(8,128)(2,1)S(1)} %collective-permute-done.2.refs_3_), channel_id=1, source_target_pairs={{0,8},{2,6},{8,16},{10,2},{16,24},{18,10},{24,28},{26,18},{28,20},... | collective-permute-start | bytes 798728 | tf_op jit(solution)/shard_map/ppermute | solution.py:445
  18.5 6.2 %collective-permute-start.13 = (bf16[1040,128]{1,0:T(8,128)(2,1)S(1)}, bf16[1040,128]{1,0:T(8,128)(2,1)S(1)}, u32[]{:S(2)}, u32[]{:S(2)}) collective-permute-start(bf16[1040,128]{1,0:T(8,128)(2,1)S(1)} %collective-permute-done.12.refs_5_), channel_id=1, source_target_pairs={{0,2},{2,0},{4,6},{6,4},{8,10},{10,8},{12,14},{14,12},{16,18},{18,... | collective-permute-start | bytes 798728 | tf_op jit(solution)/shard_map/ppermute | solution.py:363
  19.3 7.0 %collective-permute-start.11 = (bf16[1040,128]{1,0:T(8,128)(2,1)S(1)}, bf16[1040,128]{1,0:T(8,128)(2,1)S(1)}, u32[]{:S(2)}, u32[]{:S(2)}) collective-permute-start(bf16[1040,128]{1,0:T(8,128)(2,1)S(1)} %collective-permute-done.10.refs_3_), channel_id=1, source_target_pairs={{0,2},{2,0},{4,6},{6,4},{8,10},{10,8},{12,14},{14,12},{16,18},{18,... | collective-permute-start | bytes 798728 | tf_op jit(solution)/shard_map/ppermute | solution.py:363
  19.3 9.8 %collective-permute-start.17 = (bf16[1040,128]{1,0:T(8,128)(2,1)S(1)}, bf16[1040,128]{1,0:T(8,128)(2,1)S(1)}, u32[]{:S(2)}, u32[]{:S(2)}) collective-permute-start(bf16[1040,128]{1,0:T(8,128)(2,1)S(1)} %collective-permute-done.7.refs_5_), channel_id=1, source_target_pairs={{8,0},{6,2},{16,8},{2,10},{24,16},{10,18},{28,24},{18,26},{20,28},... | collective-permute-start | bytes 798728 | tf_op jit(solution)/shard_map/ppermute | solution.py:445
  24.2 5.8 %collective-permute-start.8 = (bf16[1040,128]{1,0:T(8,128)(2,1)S(1)}, bf16[1040,128]{1,0:T(8,128)(2,1)S(1)}, u32[]{:S(2)}, u32[]{:S(2)}) collective-permute-start(bf16[1040,128]{1,0:T(8,128)(2,1)S(1)} %collective-permute-done.7.refs_5_), channel_id=1, source_target_pairs={{0,2},{2,0},{4,6},{6,4},{8,10},{10,8},{12,14},{14,12},{16,18},{18,... | collective-permute-start | bytes 798728 | tf_op jit(solution)/shard_map/ppermute | solution.py:363
  24.3 5.7 %collective-permute-start.6 = (bf16[1040,128]{1,0:T(8,128)(2,1)S(1)}, bf16[1040,128]{1,0:T(8,128)(2,1)S(1)}, u32[]{:S(2)}, u32[]{:S(2)}) collective-permute-start(bf16[1040,128]{1,0:T(8,128)(2,1)S(1)} %collective-permute-done.2.refs_3_), channel_id=1, source_target_pairs={{0,2},{2,0},{4,6},{6,4},{8,10},{10,8},{12,14},{14,12},{16,18},{18,... | collective-permute-start | bytes 798728 | tf_op jit(solution)/shard_map/ppermute | solution.py:363
  24.7 9.3 %collective-permute-start.4 = (bf16[1040,128]{1,0:T(8,128)(2,1)S(1)}, bf16[1040,128]{1,0:T(8,128)(2,1)S(1)}, u32[]{:S(2)}, u32[]{:S(2)}) collective-permute-start(bf16[1040,128]{1,0:T(8,128)(2,1)S(1)} %collective-permute-done.3.refs_1_), channel_id=1, source_target_pairs={{0,8},{2,6},{8,16},{10,2},{16,24},{18,10},{24,28},{26,18},{28,20},... | collective-permute-start | bytes 798728 | tf_op jit(solution)/shard_map/ppermute | solution.py:445
  26.3 9.2 %collective-permute-start.22 = (bf16[1040,128]{1,0:T(8,128)(2,1)S(1)}, bf16[1040,128]{1,0:T(8,128)(2,1)S(1)}, u32[]{:S(2)}, u32[]{:S(2)}) collective-permute-start(bf16[1040,128]{1,0:T(8,128)(2,1)S(1)} %collective-permute-done.12.refs_5_), channel_id=1, source_target_pairs={{8,0},{6,2},{16,8},{2,10},{24,16},{10,18},{28,24},{18,26},{20,28},... | collective-permute-start | bytes 798728 | tf_op jit(solution)/shard_map/ppermute | solution.py:445
  26.7 0.7 copy-start.1
  29.1 8.5 %collective-permute-start.20 = (bf16[1040,128]{1,0:T(8,128)(2,1)S(1)}, bf16[1040,128]{1,0:T(8,128)(2,1)S(1)}, u32[]{:S(2)}, u32[]{:S(2)}) collective-permute-start(bf16[1040,128]{1,0:T(8,128)(2,1)S(1)} %collective-permute-done.17.refs_3_), channel_id=1, source_target_pairs={{8,0},{6,2},{16,8},{2,10},{24,16},{10,18},{28,24},{18,26},{20,28},... | collective-permute-start | bytes 798728 | tf_op jit(solution)/shard_map/ppermute | solution.py:445
  30.0 7.7 %collective-permute-start.18 = (bf16[1040,128]{1,0:T(8,128)(2,1)S(1)}, bf16[1040,128]{1,0:T(8,128)(2,1)S(1)}, u32[]{:S(2)}, u32[]{:S(2)}) collective-permute-start(bf16[1040,128]{1,0:T(8,128)(2,1)S(1)} %collective-permute-done.17.refs_3_), channel_id=1, source_target_pairs={{0,2},{2,0},{4,6},{6,4},{8,10},{10,8},{12,14},{14,12},{16,18},{18,... | collective-permute-start | bytes 798728 | tf_op jit(solution)/shard_map/ppermute | solution.py:363
  33.9 8.2 %collective-permute-start.14 = (bf16[1040,128]{1,0:T(8,128)(2,1)S(1)}, bf16[1040,128]{1,0:T(8,128)(2,1)S(1)}, u32[]{:S(2)}, u32[]{:S(2)}) collective-permute-start(bf16[1040,128]{1,0:T(8,128)(2,1)S(1)} %collective-permute-done.4.refs_5_), channel_id=1, source_target_pairs={{0,8},{2,6},{8,16},{10,2},{16,24},{18,10},{24,28},{26,18},{28,20},... | collective-permute-start | bytes 798728 | tf_op jit(solution)/shard_map/ppermute | solution.py:445
  35.5 6.7 %collective-permute-start.23 = (bf16[1040,128]{1,0:T(8,128)(2,1)S(1)}, bf16[1040,128]{1,0:T(8,128)(2,1)S(1)}, u32[]{:S(2)}, u32[]{:S(2)}) collective-permute-start(bf16[1040,128]{1,0:T(8,128)(2,1)S(1)} %collective-permute-done.22.refs_3_), channel_id=1, source_target_pairs={{8,0},{6,2},{16,8},{2,10},{24,16},{10,18},{28,24},{18,26},{20,28},... | collective-permute-start | bytes 798728 | tf_op jit(solution)/shard_map/ppermute | solution.py:459
  36.0 7.6 %collective-permute-start.16 = (bf16[1040,128]{1,0:T(8,128)(2,1)S(1)}, bf16[1040,128]{1,0:T(8,128)(2,1)S(1)}, u32[]{:S(2)}, u32[]{:S(2)}) collective-permute-start(bf16[1040,128]{1,0:T(8,128)(2,1)S(1)} %collective-permute-done.3.refs_1_), channel_id=1, source_target_pairs={{0,2},{2,0},{4,6},{6,4},{8,10},{10,8},{12,14},{14,12},{16,18},{18,... | collective-permute-start | bytes 798728 | tf_op jit(solution)/shard_map/ppermute | solution.py:363
  37.6 6.0 %collective-permute-start.21 = (bf16[1040,128]{1,0:T(8,128)(2,1)S(1)}, bf16[1040,128]{1,0:T(8,128)(2,1)S(1)}, u32[]{:S(2)}, u32[]{:S(2)}) collective-permute-start(bf16[1040,128]{1,0:T(8,128)(2,1)S(1)} %collective-permute-done.20.refs_7_), channel_id=1, source_target_pairs={{0,2},{2,0},{4,6},{6,4},{8,10},{10,8},{12,14},{14,12},{16,18},{18,... | collective-permute-start | bytes 798728 | tf_op jit(solution)/shard_map/ppermute | solution.py:363
  37.6 6.0 %collective-permute-start.19 = (bf16[1040,128]{1,0:T(8,128)(2,1)S(1)}, bf16[1040,128]{1,0:T(8,128)(2,1)S(1)}, u32[]{:S(2)}, u32[]{:S(2)}) collective-permute-start(bf16[1040,128]{1,0:T(8,128)(2,1)S(1)} %collective-permute-done.4.refs_5_), channel_id=1, source_target_pairs={{0,2},{2,0},{4,6},{6,4},{8,10},{10,8},{12,14},{14,12},{16,18},{18,... | collective-permute-start | bytes 798728 | tf_op jit(solution)/shard_map/ppermute | solution.py:363
  42.2 2.8 %collective-permute-start.15 = (bf16[1040,128]{1,0:T(8,128)(2,1)S(1)}, bf16[1040,128]{1,0:T(8,128)(2,1)S(1)}, u32[]{:S(2)}, u32[]{:S(2)}) collective-permute-start(bf16[1040,128]{1,0:T(8,128)(2,1)S(1)} %collective-permute-done.14.refs_1_), channel_id=1, source_target_pairs={{0,2},{2,0},{4,6},{6,4},{8,10},{10,8},{12,14},{14,12},{16,18},{18,... | collective-permute-start | bytes 798728 | tf_op jit(solution)/shard_map/ppermute | solution.py:363
  42.2 6.4 %collective-permute-start.26 = (bf16[1040,128]{1,0:T(8,128)(2,1)S(1)}, bf16[1040,128]{1,0:T(8,128)(2,1)S(1)}, u32[]{:S(2)}, u32[]{:S(2)}) collective-permute-start(bf16[1040,128]{1,0:T(8,128)(2,1)S(1)} %collective-permute-done.10.refs_3_), channel_id=1, source_target_pairs={{0,8},{2,6},{8,16},{10,2},{16,24},{18,10},{24,28},{26,18},{28,20},... | collective-permute-start | bytes 798728 | tf_op jit(solution)/shard_map/ppermute | solution.py:445
  43.6 8.5 %collective-permute-start.28 = (bf16[1040,128]{1,0:T(8,128)(2,1)S(1)}, bf16[1040,128]{1,0:T(8,128)(2,1)S(1)}, u32[]{:S(2)}, u32[]{:S(2)}) collective-permute-start(bf16[1040,128]{1,0:T(8,128)(2,1)S(1)} %collective-permute-done.22.refs_3_), channel_id=1, source_target_pairs={{0,2},{2,0},{4,6},{6,4},{8,10},{10,8},{12,14},{14,12},{16,18},{18,... | collective-permute-start | bytes 798728 | tf_op jit(solution)/shard_map/ppermute | solution.py:363
  48.6 8.8 %collective-permute-start.29 = (bf16[1040,128]{1,0:T(8,128)(2,1)S(1)}, bf16[1040,128]{1,0:T(8,128)(2,1)S(1)}, u32[]{:S(2)}, u32[]{:S(2)}) collective-permute-start(bf16[1040,128]{1,0:T(8,128)(2,1)S(1)} %collective-permute-done.26.refs_1_), channel_id=1, source_target_pairs={{0,8},{2,6},{8,16},{10,2},{16,24},{18,10},{24,28},{26,18},{28,20},... | collective-permute-start | bytes 798728 | tf_op jit(solution)/shard_map/ppermute | solution.py:459
  50.0 7.4 %collective-permute-start.24 = (bf16[1040,128]{1,0:T(8,128)(2,1)S(1)}, bf16[1040,128]{1,0:T(8,128)(2,1)S(1)}, u32[]{:S(2)}, u32[]{:S(2)}) collective-permute-start(bf16[1040,128]{1,0:T(8,128)(2,1)S(1)} %collective-permute-done.23.refs_7_), channel_id=1, source_target_pairs={{8,0},{6,2},{16,8},{2,10},{24,16},{10,18},{28,24},{18,26},{20,28},... | collective-permute-start | bytes 798728 | tf_op jit(solution)/shard_map/ppermute | solution.py:459
  50.6 12.9 %collective-permute-start.32 = (bf16[256,1024]{1,0:T(8,128)(2,1)S(1)}, bf16[256,1024]{1,0:T(8,128)(2,1)S(1)}, u32[]{:S(2)}, u32[]{:S(2)}) collective-permute-start(bf16[256,1024]{1,0:T(8,128)(2,1)S(1)} %get-tuple-element.33.refs_0_), channel_id=1, source_target_pairs={{0,1},{1,0},{2,3},{3,2},{4,5},{5,4},{6,7},{7,6},{8,9},{9,8},{10,11... | collective-permute-start | bytes 1572872 | tf_op jit(solution)/shard_map/ppermute | solution.py:341
  52.1 5.8 %collective-permute-start.27 = (bf16[1040,128]{1,0:T(8,128)(2,1)S(1)}, bf16[1040,128]{1,0:T(8,128)(2,1)S(1)}, u32[]{:S(2)}, u32[]{:S(2)}) collective-permute-start(bf16[1040,128]{1,0:T(8,128)(2,1)S(1)} %collective-permute-done.26.refs_1_), channel_id=1, source_target_pairs={{0,2},{2,0},{4,6},{6,4},{8,10},{10,8},{12,14},{14,12},{16,18},{18,... | collective-permute-start | bytes 798728 | tf_op jit(solution)/shard_map/ppermute | solution.py:363
  52.1 5.8 %collective-permute-start.31 = (bf16[1040,128]{1,0:T(8,128)(2,1)S(1)}, bf16[1040,128]{1,0:T(8,128)(2,1)S(1)}, u32[]{:S(2)}, u32[]{:S(2)}) collective-permute-start(bf16[1040,128]{1,0:T(8,128)(2,1)S(1)} %collective-permute-done.23.refs_7_), channel_id=1, source_target_pairs={{0,2},{2,0},{4,6},{6,4},{8,10},{10,8},{12,14},{14,12},{16,18},{18,... | collective-permute-start | bytes 798728 | tf_op jit(solution)/shard_map/ppermute | solution.py:363
  57.4 1.5 %collective-permute-start.30 = (bf16[1040,128]{1,0:T(8,128)(2,1)S(1)}, bf16[1040,128]{1,0:T(8,128)(2,1)S(1)}, u32[]{:S(2)}, u32[]{:S(2)}) collective-permute-start(bf16[1040,128]{1,0:T(8,128)(2,1)S(1)} %collective-permute-done.29.refs_5_), channel_id=1, source_target_pairs={{0,2},{2,0},{4,6},{6,4},{8,10},{10,8},{12,14},{14,12},{16,18},{18,... | collective-permute-start | bytes 798728 | tf_op jit(solution)/shard_map/ppermute | solution.py:363
  57.4 2.9 %collective-permute-start.25 = (bf16[1040,128]{1,0:T(8,128)(2,1)S(1)}, bf16[1040,128]{1,0:T(8,128)(2,1)S(1)}, u32[]{:S(2)}, u32[]{:S(2)}) collective-permute-start(bf16[1040,128]{1,0:T(8,128)(2,1)S(1)} %collective-permute-done.24.refs_1_), channel_id=1, source_target_pairs={{0,2},{2,0},{4,6},{6,4},{8,10},{10,8},{12,14},{14,12},{16,18},{18,... | collective-permute-start | bytes 798728 | tf_op jit(solution)/shard_map/ppermute | solution.py:363
  63.5 12.0 %collective-permute-start.33 = (bf16[256,1024]{1,0:T(8,128)(2,1)S(1)}, bf16[256,1024]{1,0:T(8,128)(2,1)S(1)}, u32[]{:S(2)}, u32[]{:S(2)}) collective-permute-start(bf16[256,1024]{1,0:T(8,128)(2,1)S(1)} %get-tuple-element.47.refs_1_), channel_id=1, source_target_pairs={{0,1},{1,0},{2,3},{3,2},{4,5},{5,4},{6,7},{7,6},{8,9},{9,8},{10,11... | collective-permute-start | bytes 1572872 | tf_op jit(solution)/shard_map/ppermute | solution.py:341
